TPU v7x, 512 devices: a whole 4x8x8 slice. The times are simulated.
512 devices in a mesh: cp: 8 (over y_hi, core), blk: 8 (over x, y_lo), head: 8 (over z).
Axes of the slice: x: 4, y: 8 (y_hi: 4, y_lo: 2; y = y_hi * 2 + y_lo), z: 8, core: 2. Of those that a mesh axis runs over, the one named last changes fastest.
Arguments:
- queries: bfloat16 [8192, 8, 1024], P(('cp', 'blk'), 'head'), may hold values from -4 to 4
- new_kv: bfloat16 [8192, 8, 2, 128], P(('cp', 'blk'), 'head'), may hold values from -105 to 105
- cached_key_value: bfloat16 [4096, 8, 2, 128], P(('cp', 'blk'), 'head'), may hold values from -4 to 4
- new_doc: int32 [8192], replicated, may hold values from 0 to 15, never falling along the last dimension, each value on 1 to 1024 neighbouring positions
- cache_doc: int32 [4096], replicated, may hold values from 0 to 15, never falling along the last dimension, each value on 1 to 512 neighbouring positions
- cache_len: int32 [64], replicated, may hold values from 16 to 64, as said below
Outputs:
- attended: bfloat16 [8192, 8, 1024], P(('cp', 'blk', 'head'))
Inputs may be any that keep to these rules, and one draw needn't show every extreme that they name: `new_doc`: request numbers never fall along the new positions, and each of the 16 requests has at least one new position. `cache_doc`: request numbers never fall along the cached positions, and each of the 16 requests has at least one cached position. `cache_len`: shard s holds cached positions s * 64 to (s + 1) * 64 - 1, the valid ones first; some shard is full.
All inputs are finite; a program needn't handle non-finite values.
Results may differ from a plain program's by a relative error of at most 0.0065.
Values may be sent and summed in bfloat16 or wider, within the bound.
No kernel may reach another device: no remote copies, remote signals or barrier semaphores. Data moves between devices by JAX's collectives and lax.ppermute only.
A program may use at most 64 MiB of HBM per device.

v0:
```python
import functools
import math

import jax
import jax.numpy as jnp
from jax import lax
from jax.experimental import pallas as pl
from jax.experimental.pallas import tpu as pltpu
from jax.sharding import PartitionSpec as P

negative = -1e30
documents = 16
longest = 1024
head = 128
pieces = 4
smem = pl.BlockSpec(memory_space=pltpu.SMEM)
vmem = pl.BlockSpec(memory_space=pltpu.VMEM)
limits = pltpu.CompilerParams(vmem_limit_bytes=44 * 1024 * 1024)


def split_pairs(raw, wide, rows):
    wide[: 2 * rows, :] = raw.astype(jnp.float32)
    keys = wide[pl.ds(0, rows, 2), :]
    values = wide[pl.ds(1, rows, 2), :]
    return jnp.concatenate([keys, values], axis=1).astype(jnp.bfloat16)


def prepare_kernel(
    new_ref,
    before_ref,
    new_doc_ref,
    cache_doc_ref,
    pair_ref,
    starts_ref,
    pick_ref,
    wide,
    *,
    turns,
    period,
):
    tok = pair_ref.shape[0] // 2
    pair_ref[:tok] = split_pairs(before_ref[...], wide, tok)
    pair_ref[tok:] = split_pairs(new_ref[...], wide, tok)
    new_doc = new_doc_ref[...]
    cache_doc = cache_doc_ref[...]
    first_doc = new_doc[:, :1]
    last_doc = new_doc[:, -1:]
    low = jnp.zeros(first_doc.shape, jnp.float32)
    high = jnp.full(first_doc.shape, float(cache_doc.size), jnp.float32)
    starts_ref[0] = 0
    starts_ref[documents + 1] = 0
    for doc in range(1, documents):
        before = jnp.sum((new_doc < doc).astype(jnp.float32))
        starts_ref[doc] = before.astype(jnp.int32)
        before = jnp.sum((cache_doc < doc).astype(jnp.float32))
        starts_ref[documents + 1 + doc] = before.astype(jnp.int32)
        low = jnp.where(first_doc == doc, before, low)
        high = jnp.where(last_doc == doc - 1, before, high)
    starts_ref[documents] = new_doc.size
    starts_ref[2 * documents + 1] = cache_doc.size
    widest = jnp.max(high - low).astype(jnp.int32)
    pick = jnp.int32(0)
    for turn in turns[:-1]:
        pick += (widest > turn * period).astype(jnp.int32)
    pick_ref[0] = pick


def pack_cache_kernel(
    place_ref, starts_ref, raw_ref, out_ref, shards_ref, wide, *, turns, tok
):
    groups, shard_rows, _ = shards_ref.shape
    for group in range(groups):
        wide[group] = raw_ref[group].astype(jnp.float32)
        shards_ref[group, :, :head] = wide[group, pl.ds(0, shard_rows, 2), :]
        shards_ref[group, :, head:] = wide[group, pl.ds(1, shard_rows, 2), :]
    count = out_ref.shape[0]
    period = count * shard_rows
    cp_index = place_ref[0]
    blk_index = place_ref[1]
    row = lax.broadcasted_iota(jnp.int32, (shard_rows, 1), 0)
    for target in range(count):
        first = (cp_index * count + target) * tok
        low = jnp.int32(0)
        for doc in range(1, documents):
            low = jnp.where(first >= starts_ref[doc], starts_ref[documents + 1 + doc], low)
        reached = low - blk_index * shard_rows
        group = (reached - (shard_rows - 1) + period - 1) // period
        cut = reached - group * period
        for at, turn in enumerate(turns):
            here = jnp.minimum(group + turn, groups - 1)
            after = jnp.minimum(group + turn + 1, groups - 1)
            chosen = jnp.where(row >= cut, shards_ref[here], shards_ref[after])
            out_ref[target, at * shard_rows : (at + 1) * shard_rows] = chosen.astype(
                jnp.bfloat16
            )


def attention_kernel(
    place_ref,
    starts_ref,
    cache_len_ref,
    queries_ref,
    pair_ref,
    second_ref,
    fourth_ref,
    sixth_ref,
    arrived_ref,
    out_ref,
    window,
    new_scores,
    cache_scores,
    lane_max,
    lane_sum,
    total,
    *,
    shard_rows,
    rounds,
):
    tok, width = queries_ref.shape
    heads = width // head
    count = arrived_ref.shape[0]
    shards = cache_len_ref.shape[0]
    period = count * shard_rows
    span = pieces * shard_rows
    exponent_scale = math.log2(math.e) * head**-0.5
    block = place_ref[0] * count + place_ref[1]
    first = block * tok

    row_place = first + lax.broadcasted_iota(jnp.int32, (tok, 1), 0)
    row_start = jnp.zeros((tok, 1), jnp.int32)
    row_low = jnp.zeros((tok, 1), jnp.int32)
    row_high = jnp.full((tok, 1), starts_ref[documents + 2], jnp.int32)
    new_low = jnp.int32(0)
    cache_low = jnp.int32(0)
    cache_high = starts_ref[documents + 2]
    for doc in range(1, documents):
        start = starts_ref[doc]
        low = starts_ref[documents + 1 + doc]
        high = starts_ref[documents + 2 + doc]
        reached = row_place >= start
        row_start = jnp.where(reached, start, row_start)
        row_low = jnp.where(reached, low, row_low)
        row_high = jnp.where(reached, high, row_high)
        new_low = jnp.where(first >= start, start, new_low)
        cache_low = jnp.where(first >= start, low, cache_low)
        cache_high = jnp.where(first + tok - 1 >= start, high, cache_high)

    lane_max[...] = jnp.full(lane_max.shape, negative, jnp.float32)
    lane_sum[...] = jnp.zeros(lane_sum.shape, jnp.float32)
    total[...] = jnp.zeros(total.shape, jnp.float32)

    def score(keys, allowed, scores_ref, at):
        for h in range(heads):
            scores = lax.dot_general(
                queries_ref[:, h * head : (h + 1) * head],
                keys,
                (((1,), (1,)), ((), ())),
                preferred_element_type=jnp.float32,
            )
            scores = jnp.where(allowed, scores, negative)
            scores_ref[at, h] = scores
            best = scores[:, :head]
            for part in range(1, scores.shape[1] // head):
                best = jnp.maximum(best, scores[:, part * head : (part + 1) * head])
            lane_max[h] = jnp.maximum(lane_max[h], best)

    def weigh(values, scores_ref, at):
        for h in range(heads):
            scores = scores_ref[at, h]
            best = lane_max[h]
            added = lane_sum[h]
            parts = []
            for part in range(scores.shape[1] // head):
                piece = scores[:, part * head : (part + 1) * head]
                weight = jnp.exp2((piece - best) * exponent_scale)
                added = added + weight
                parts.append(weight.astype(jnp.bfloat16))
            lane_sum[h] = added
            rounded = parts[0] if len(parts) == 1 else jnp.concatenate(parts, axis=1)
            total[h] += jnp.dot(rounded, values, preferred_element_type=jnp.float32)

    first_block = new_low // tok
    farthest = block - count
    filled_rows = 0
    for part in (sixth_ref, fourth_ref, second_ref, pair_ref):
        window[filled_rows : filled_rows + part.shape[0]] = part[...]
        filled_rows += part.shape[0]

    @pl.loop(first_block, block + 1)
    def _(number):
        slot = number - farthest
        offset = pl.multiple_of(slot * tok, tok)
        keys = window[pl.ds(offset, tok), :head]
        key_place = number * tok + lax.broadcasted_iota(jnp.int32, (1, tok), 1)
        allowed = (key_place >= row_start) & (key_place <= row_place)
        score(keys, allowed, new_scores, slot)

    def cache_tile(number):
        turn = number // (count // pieces)
        source = number % (count // pieces) * pieces
        base = cache_low + turn * period
        begin = base + jnp.bitwise_and(source * shard_rows - base, period - 1)
        holds = jnp.bitwise_and(base - source * shard_rows, period - 1) < span
        return turn, source, base, (begin < cache_high) | (holds & (base < cache_high))

    def cache_part(turn, source, first_lane):
        offset = pl.multiple_of(turn * shard_rows, shard_rows)
        return jnp.concatenate(
            [
                arrived_ref[source + part, pl.ds(offset, shard_rows), first_lane : first_lane + head]
                for part in range(pieces)
            ],
            axis=0,
        )

    tiles = rounds * count // pieces

    @pl.loop(0, tiles)
    def _(number):
        turn, source, base, needed = cache_tile(number)

        @pl.when(needed)
        def _():
            lane = lax.broadcasted_iota(jnp.int32, (1, span), 1)
            place = base + jnp.bitwise_and(source * shard_rows + lane - base, period - 1)
            shard = place // shard_rows
            filled = jnp.zeros((1, span), jnp.int32)
            for part in range(pieces):
                edge = (source + part) * shard_rows
                for at in (0, shard_rows - 1):
                    where = base + jnp.bitwise_and(edge + at - base, period - 1)
                    where = where // shard_rows
                    length = cache_len_ref[jnp.minimum(where, shards - 1)]
                    filled = jnp.where(shard == where, length, filled)
            usable = jnp.bitwise_and(place, shard_rows - 1) < filled
            allowed = (place >= row_low) & (place < row_high) & usable
            score(cache_part(turn, source, 0), allowed, cache_scores, number)

    for h in range(heads):
        best = jnp.max(lane_max[h], axis=1, keepdims=True)
        lane_max[h] = jnp.broadcast_to(best, (tok, head))

    @pl.loop(first_block, block + 1)
    def _(number):
        slot = number - farthest
        offset = pl.multiple_of(slot * tok, tok)
        weigh(window[pl.ds(offset, tok), head:], new_scores, slot)

    @pl.loop(0, tiles)
    def _(number):
        turn, source, base, needed = cache_tile(number)

        @pl.when(needed)
        def _():
            weigh(cache_part(turn, source, head), cache_scores, number)

    for h in range(heads):
        row_total = jnp.sum(lane_sum[h], axis=1, keepdims=True)
        out_ref[:, h * head : (h + 1) * head] = (total[h] / row_total).astype(jnp.bfloat16)


def local(queries, new_kv, cached_key_value, new_doc, cache_doc, cache_len):
    tok = queries.shape[0]
    width = queries.shape[-1]
    heads = width // head
    shard_rows = cached_key_value.shape[0]
    blk_count = lax.axis_size("blk")
    cp_count = lax.axis_size("cp")
    head_count = lax.axis_size("head")
    assert tok * blk_count >= longest
    place = jnp.stack([lax.axis_index("cp"), lax.axis_index("blk")]).astype(jnp.int32)
    period = blk_count * shard_rows
    turns = [2, 3, cp_count]
    block_count = cp_count * blk_count

    def ahead(value, steps):
        pairs = [(block, (block + steps) % block_count) for block in range(block_count)]
        return lax.ppermute(value, ("cp", "blk"), pairs)

    new_raw = new_kv.reshape(2 * tok, head)
    cache_raw = cached_key_value.reshape(2 * shard_rows, head)
    raw_before = ahead(new_raw, 1)
    spread = jnp.broadcast_to(cache_raw[None], (cp_count,) + cache_raw.shape)
    spread, raw_before = lax.optimization_barrier((spread, raw_before))
    shards = lax.all_to_all(spread, "cp", split_axis=0, concat_axis=0)
    operands = (new_raw, raw_before, new_doc.reshape(-1, tok), cache_doc.reshape(-1, 128))
    pair, starts, pick = pl.pallas_call(
        functools.partial(prepare_kernel, turns=turns, period=period),
        grid=(1,),
        out_shape=[
            jax.ShapeDtypeStruct((2 * tok, 2 * head), jnp.bfloat16),
            jax.ShapeDtypeStruct((2 * documents + 2,), jnp.int32),
            jax.ShapeDtypeStruct((1,), jnp.int32),
        ],
        in_specs=[pl.BlockSpec(operand.shape, lambda i: (0, 0)) for operand in operands],
        out_specs=[vmem, smem, smem],
        scratch_shapes=[pltpu.VMEM((2 * tok, head), jnp.float32)],
        compiler_params=pltpu.CompilerParams(vmem_limit_bytes=56 * 1024 * 1024),
    )(*operands)
    second = ahead(pair, 2)
    fourth = ahead(pair, 4)
    sixth = ahead(jnp.concatenate([second[tok:], pair], axis=0), 6)

    def cached_rows(turns, shards, starts):
        rows = len(turns) * shard_rows
        packed = pl.pallas_call(
            functools.partial(pack_cache_kernel, turns=turns, tok=tok),
            out_shape=jax.ShapeDtypeStruct((blk_count, rows, 2 * head), jnp.bfloat16),
            in_specs=[smem, smem, vmem],
            out_specs=vmem,
            scratch_shapes=[
                pltpu.VMEM((cp_count, shard_rows, 2 * head), jnp.float32),
                pltpu.VMEM((cp_count, 2 * shard_rows, head), jnp.float32),
            ],
            compiler_params=limits,
        )(place, starts, shards)
        return lax.all_to_all(packed, "blk", split_axis=0, concat_axis=0)

    arrived = cached_rows(range(turns[0]), shards, starts)

    def attend(rounds):
        def run(shards, pair, second, fourth, sixth, arrived, starts, cache_len, queries):
            if rounds > turns[0]:
                more = cached_rows(range(turns[0], rounds), shards, starts)
                arrived = jnp.concatenate([arrived, more], axis=1)
            span = pieces * shard_rows
            tiles = rounds * blk_count // pieces
            return pl.pallas_call(
                functools.partial(attention_kernel, shard_rows=shard_rows, rounds=rounds),
                out_shape=jax.ShapeDtypeStruct((tok, width), jnp.bfloat16),
                in_specs=[smem] * 3 + [vmem] * 6,
                out_specs=vmem,
                scratch_shapes=[
                    pltpu.VMEM(((blk_count + 1) * tok, 2 * head), jnp.bfloat16),
                    pltpu.VMEM((blk_count + 1, heads, tok, tok), jnp.float32),
                    pltpu.VMEM((tiles, heads, tok, span), jnp.float32),
                    pltpu.VMEM((heads, tok, head), jnp.float32),
                    pltpu.VMEM((heads, tok, head), jnp.float32),
                    pltpu.VMEM((heads, tok, head), jnp.float32),
                ],
                compiler_params=limits,
            )(place, starts, cache_len, queries, pair, second, fourth, sixth, arrived)

        return run

    attended = lax.switch(
        pick[0],
        [attend(turn) for turn in turns],
        shards,
        pair,
        second,
        fourth,
        sixth,
        arrived,
        starts,
        cache_len,
        queries[:, 0],
    )
    share = tok // head_count
    moved = lax.all_to_all(
        attended.reshape(head_count, share, width), "head", split_axis=0, concat_axis=0
    )
    return jnp.transpose(moved, (1, 0, 2))


def solution(mesh):
    placed = (
        P(("cp", "blk"), "head", None),
        P(("cp", "blk"), "head", None, None),
        P(("cp", "blk"), "head", None, None),
        P(),
        P(),
        P(),
    )
    return jax.shard_map(
        local,
        mesh=mesh,
        in_specs=placed,
        out_specs=P(("cp", "blk", "head"), None, None),
        check_vma=False,
    )
```

profile of v0, /device:TPU:3, one launch (start us, length us, event | category | flops | bytes accessed | tf_op | source)
XLA Modules:
  0.0 88.6 jit_solution(16533604031184730331)
XLA Ops:
  0.0 0.0 copy-start.2
  0.0 3.3 %collective-permute-start = (bf16[256,128]{1,0:T(8,128)(2,1)}, bf16[256,128]{1,0:T(8,128)(2,1)S(1)}, u32[]{:S(2)}, u32[]{:S(2)}) collective-permute-start(bf16[256,128]{1,0:T(8,128)(2,1)} %bitcast.15), channel_id=1, source_target_pairs={{0,8},{8,16},{16,24},{24,32},{32,40},{40,48},{48,56},{56,64},{64,7... | collective-permute-start | bytes 196616 | tf_op jit(solution)/shard_map/ppermute | solution.py:278
  3.3 2.9 %collective-permute-done.before_ref = bf16[256,128]{1,0:T(8,128)(2,1)S(1)} collective-permute-done((bf16[256,128]{1,0:T(8,128)(2,1)}, bf16[256,128]{1,0:T(8,128)(2,1)S(1)}, u32[]{:S(2)}, u32[]{:S(2)}) %collective-permute-start) | collective-permute-done | bytes 65568 | tf_op jit(solution)/shard_map/ppermute | solution.py:278
  6.2 1.5 %broadcast_in_dim.8 = bf16[8,128,128]{2,1,0:T(8,128)(2,1)} broadcast(bf16[128,128]{1,0:T(8,128)(2,1)} %bitcast.17), dimensions={1,2} | broadcast | bytes 294912 | tf_op jit(solution)/shard_map/broadcast_in_dim | solution.py:283
  7.7 8.9 %all-to-all-start.2 = ((bf16[8,128,128]{2,1,0:T(8,128)(2,1)}), bf16[8,128,128]{2,1,0:T(8,128)(2,1)S(1)}, u32[]{:S(2)}, u32[]{:S(2)}) async-start(bf16[8,128,128]{2,1,0:T(8,128)(2,1)} %broadcast_in_dim.8), calls=%async_computation.2 | async-start | bytes 524288 | tf_op jit(solution)/shard_map/all_to_all | solution.py:285
  16.7 0.1 pad_add_fusion.place_ref
  16.7 0.0 copy-done.1
  16.7 1.8 %shard_map.64 = (bf16[256,256]{1,0:T(8,128)(2,1)S(1)}, s32[34]{0:T(128)S(1)}, s32[1]{0:T(128)}) custom-call(bf16[256,128]{1,0:T(8,128)(2,1)} %bitcast.16, bf16[256,128]{1,0:T(8,128)(2,1)} %copy-done.1, s32[64,128]{1,0:T(8,128)} %bitcast.18, s32[32,128]{1,0:T(8,128)} %bitcast.19), custom_call_target="tpu_custom_call" | custom-call | tf_op jit(solution)/shard_map/pallas_call | solution.py:287
  18.6 8.8 %all-to-all-done.2.raw_ref = bf16[8,128,128]{2,1,0:T(8,128)(2,1)S(1)} async-done(((bf16[8,128,128]{2,1,0:T(8,128)(2,1)}), bf16[8,128,128]{2,1,0:T(8,128)(2,1)S(1)}, u32[]{:S(2)}, u32[]{:S(2)}) %all-to-all-start.2) | async-done | bytes 262176 | tf_op jit(solution)/shard_map/all_to_all | solution.py:285
  27.4 1.6 %shard_map.65 = bf16[8,128,256]{2,1,0:T(8,128)(2,1)} custom-call(s32[2]{0:T(128)S(1)} %pad_add_fusion.place_ref, s32[34]{0:T(128)S(1)} %get-tuple-element.103.starts_ref, bf16[8,128,128]{2,1,0:T(8,128)(2,1)S(1)} %all-to-all-done.2.raw_ref), custom_call_target="tpu_custom_call" | custom-call | tf_op jit(solution)/shard_map/pallas_call | solution.py:306
  29.0 6.1 %all-to-all-start.3 = ((bf16[8,128,256]{2,1,0:T(8,128)(2,1)}), bf16[8,128,256]{2,1,0:T(8,128)(2,1)S(1)}, u32[]{:S(2)}, u32[]{:S(2)}) async-start(bf16[8,128,256]{2,1,0:T(8,128)(2,1)} %shard_map.65), calls=%async_computation.3 | async-start | bytes 1048576 | tf_op jit(solution)/shard_map/all_to_all | solution.py:317
  35.1 3.1 %collective-permute-start.1 = (bf16[256,256]{1,0:T(8,128)(2,1)S(1)}, bf16[256,256]{1,0:T(8,128)(2,1)S(1)}, u32[]{:S(2)}, u32[]{:S(2)}) collective-permute-start(bf16[256,256]{1,0:T(8,128)(2,1)S(1)} %get-tuple-element.104), channel_id=1, source_target_pairs={{0,16},{8,24},{16,32},{24,40},{32,48},{40,56},{48,64},{56,72},{64,... | collective-permute-start | bytes 393224 | tf_op jit(solution)/shard_map/ppermute | solution.py:278
  38.2 6.3 %collective-permute-done.1 = bf16[256,256]{1,0:T(8,128)(2,1)S(1)} collective-permute-done((bf16[256,256]{1,0:T(8,128)(2,1)S(1)}, bf16[256,256]{1,0:T(8,128)(2,1)S(1)}, u32[]{:S(2)}, u32[]{:S(2)}) %collective-permute-start.1) | collective-permute-done | bytes 131104 | tf_op jit(solution)/shard_map/ppermute | solution.py:278
  44.5 7.2 %collective-permute-start.3 = (bf16[384,256]{1,0:T(8,128)(2,1)S(1)}, bf16[384,256]{1,0:T(8,128)(2,1)S(1)}, u32[]{:S(2)}, u32[]{:S(2)}) collective-permute-start(bf16[384,256]{1,0:T(8,128)(2,1)S(1)} %pad_maximum_fusion.2), channel_id=1, source_target_pairs={{0,48},{8,56},{16,64},{24,72},{32,80},{40,88},{48,96},{56,104},{64... | collective-permute-start | bytes 589832 | tf_op jit(solution)/shard_map/ppermute | solution.py:278
  51.7 1.9 %collective-permute-start.2 = (bf16[256,256]{1,0:T(8,128)(2,1)S(1)}, bf16[256,256]{1,0:T(8,128)(2,1)S(1)}, u32[]{:S(2)}, u32[]{:S(2)}) collective-permute-start(bf16[256,256]{1,0:T(8,128)(2,1)S(1)} %get-tuple-element.104), channel_id=1, source_target_pairs={{0,32},{8,40},{16,48},{24,56},{32,64},{40,72},{48,80},{56,88},{64,... | collective-permute-start | bytes 393224 | tf_op jit(solution)/shard_map/ppermute | solution.py:278
  54.2 5.7 %collective-permute-done.2 = bf16[256,256]{1,0:T(8,128)(2,1)S(1)} collective-permute-done((bf16[256,256]{1,0:T(8,128)(2,1)S(1)}, bf16[256,256]{1,0:T(8,128)(2,1)S(1)}, u32[]{:S(2)}, u32[]{:S(2)}) %collective-permute-start.2) | collective-permute-done | bytes 131104 | tf_op jit(solution)/shard_map/ppermute | solution.py:278
  60.0 0.0 collective-permute-done.3
  60.0 0.0 all-to-all-done.3
  60.0 0.0 copy-done.2
  60.0 0.0 copy-done
  60.0 4.2 %conditional.1 = (bf16[128,1024]{1,0:T(8,128)(2,1)S(1)}) conditional(s32[]{:T(128)} %bitcast.4, (s32[2]{0:T(128)S(1)}, s32[34]{0:T(128)S(1)}, s32[64]{0:T(128)S(1)}, bf16[128,1024]{1,0:T(8,128)(2,1)S(1)}, bf16[256,256]{1,0:T(8,128)(2,1)S(1)}, /*index=5*/bf16[256,256]{1,0:T(8,128)(2,1)S(1)}, bf16[256,256]{1,0:T(8,128)(2,1)S(1)}, ...), branch_computations={%region_0.0_spmd, %region_1.0_spmd, %region_2.0_spmd} | conditional | flops 4194304 | bytes 7340040 | solution.py:346
  60.0 4.2 %branch_0_fun.1 = bf16[128,1024]{1,0:T(8,128)(2,1)S(1)} custom-call(s32[2]{0:T(128)S(1)} %get-tuple-element.66.place_ref, s32[34]{0:T(128)S(1)} %get-tuple-element.68.starts_ref, s32[64]{0:T(128)S(1)} %get-tuple-element.69.cache_len_ref, bf16[128,1024]{1,0:T(8,128)(2,1)S(1)} %get-tuple-element.70.queries_ref, ...), custom_call_target="tpu_custom_call" | custom-call | tf_op jit(solution)/shard_map/cond/branch_0_fun/pallas_call | solution.py:328
  64.2 23.5 %all_to_all.25 = bf16[8,16,1024]{2,1,0:T(8,128)(2,1)S(1)} all-to-all(bf16[8,16,1024]{2,1,0:T(8,128)(2,1)S(1)} %bitcast.14), channel_id=1, replica_groups=mesh['cp'=8,'blk'=8,'head'=8] {'head'}, dimensions={0} | all-to-all | bytes 524288 | tf_op jit(solution)/shard_map/all_to_all | solution.py:360
  87.8 0.9 copy.7
  (4 shorter events, 0.0 us)
Async XLA Ops:
  0.0 60.0 %copy-start.2 = (s32[64]{0:T(128)S(1)}, s32[64]{0:T(128)}, u32[]{:S(2)}) copy-start(s32[64]{0:T(128)} %param.14) | copy-start | bytes 772
  0.0 60.0 %copy-start = (bf16[128,1,1024]{2,0,1:T(8,128)(2,1)S(1)}, bf16[128,1,1024]{2,0,1:T(8,128)(2,1)}, u32[]{:S(2)}) copy-start(bf16[128,1,1024]{2,0,1:T(8,128)(2,1)} %param.9) | copy-start | bytes 786436
  0.0 6.2 %collective-permute-start = (bf16[256,128]{1,0:T(8,128)(2,1)}, bf16[256,128]{1,0:T(8,128)(2,1)S(1)}, u32[]{:S(2)}, u32[]{:S(2)}) collective-permute-start(bf16[256,128]{1,0:T(8,128)(2,1)} %bitcast.15), channel_id=1, source_target_pairs={{0,8},{8,16},{16,24},{24,32},{32,40},{40,48},{48,56},{56,64},{64,7... | collective-permute-start | bytes 196616 | tf_op jit(solution)/shard_map/ppermute | solution.py:278
  6.2 10.5 %copy-start.1 = (bf16[256,128]{1,0:T(8,128)(2,1)}, bf16[256,128]{1,0:T(8,128)(2,1)S(1)}, u32[]{:S(2)}) copy-start(bf16[256,128]{1,0:T(8,128)(2,1)S(1)} %collective-permute-done.before_ref) | copy-start | bytes 196612
  7.7 19.6 %all-to-all-start.2 = ((bf16[8,128,128]{2,1,0:T(8,128)(2,1)}), bf16[8,128,128]{2,1,0:T(8,128)(2,1)S(1)}, u32[]{:S(2)}, u32[]{:S(2)}) async-start(bf16[8,128,128]{2,1,0:T(8,128)(2,1)} %broadcast_in_dim.8), calls=%async_computation.2 | async-start | bytes 524288 | tf_op jit(solution)/shard_map/all_to_all | solution.py:285
  29.0 31.0 %all-to-all-start.3 = ((bf16[8,128,256]{2,1,0:T(8,128)(2,1)}), bf16[8,128,256]{2,1,0:T(8,128)(2,1)S(1)}, u32[]{:S(2)}, u32[]{:S(2)}) async-start(bf16[8,128,256]{2,1,0:T(8,128)(2,1)} %shard_map.65), calls=%async_computation.3 | async-start | bytes 1048576 | tf_op jit(solution)/shard_map/all_to_all | solution.py:317
  35.1 9.4 %collective-permute-start.1 = (bf16[256,256]{1,0:T(8,128)(2,1)S(1)}, bf16[256,256]{1,0:T(8,128)(2,1)S(1)}, u32[]{:S(2)}, u32[]{:S(2)}) collective-permute-start(bf16[256,256]{1,0:T(8,128)(2,1)S(1)} %get-tuple-element.104), channel_id=1, source_target_pairs={{0,16},{8,24},{16,32},{24,40},{32,48},{40,56},{48,64},{56,72},{64,... | collective-permute-start | bytes 393224 | tf_op jit(solution)/shard_map/ppermute | solution.py:278
  44.5 15.5 %collective-permute-start.3 = (bf16[384,256]{1,0:T(8,128)(2,1)S(1)}, bf16[384,256]{1,0:T(8,128)(2,1)S(1)}, u32[]{:S(2)}, u32[]{:S(2)}) collective-permute-start(bf16[384,256]{1,0:T(8,128)(2,1)S(1)} %pad_maximum_fusion.2), channel_id=1, source_target_pairs={{0,48},{8,56},{16,64},{24,72},{32,80},{40,88},{48,96},{56,104},{64... | collective-permute-start | bytes 589832 | tf_op jit(solution)/shard_map/ppermute | solution.py:278
  51.7 8.3 %collective-permute-start.2 = (bf16[256,256]{1,0:T(8,128)(2,1)S(1)}, bf16[256,256]{1,0:T(8,128)(2,1)S(1)}, u32[]{:S(2)}, u32[]{:S(2)}) collective-permute-start(bf16[256,256]{1,0:T(8,128)(2,1)S(1)} %get-tuple-element.104), channel_id=1, source_target_pairs={{0,32},{8,40},{16,48},{24,56},{32,64},{40,72},{48,80},{56,88},{64,... | collective-permute-start | bytes 393224 | tf_op jit(solution)/shard_map/ppermute | solution.py:278
where the time goes:
time: 89.2 us; the launch traced here: 88.6 us
  starting transfers between devices  30.5 us (34%)
  waiting for transfers between devices  23.7 us (27%)
  blocking collectives  23.5 us (26%)
  Pallas kernels  7.64 us (9%)
  local copies, waits for them, and re-layouts  2.36 us (3%)
    all_to_all x1, blocking collectives, local(): lax.all_to_all(attended.reshape(head_count, share, width), 'head', split_...  23.5 us
    ppermute x4, starting transfers between devices, ahead(): return lax.ppermute(value, ('cp', 'blk'), pairs)  15.5 us
    ppermute x4, waiting for transfers between devices, ahead(): return lax.ppermute(value, ('cp', 'blk'), pairs)  14.9 us
    all_to_all x1, starting transfers between devices, local(): shards = lax.all_to_all(spread, 'cp', split_axis=0, concat_axis=0)  8.92 us
    all_to_all x1, waiting for transfers between devices, local(): shards = lax.all_to_all(spread, 'cp', split_axis=0, concat_axis=0)  8.78 us
    all_to_all x1, starting transfers between devices, cached_rows(): return lax.all_to_all(packed, 'blk', split_axis=0, concat_axis=0)  6.11 us
    pallas_call x1, Pallas kernels, run(): pl.pallas_call(functools.partial(attention_kernel, shard_rows=shard_rows,...  4.21 us
    pallas_call x1, Pallas kernels, local(): pl.pallas_call(functools.partial(prepare_kernel, turns=turns, period=peri...  1.83 us
  transfers between devices with their start and end apart: 6, of which 4 were waited for; matrix products, arithmetic and copies ran while one was open for 0% of the time, Pallas kernels for 2%

commit v1 on v0

v1 whole, which is shorter than its diff:
```python
import functools
import math

import jax
import jax.numpy as jnp
from jax import lax
from jax.experimental import pallas as pl
from jax.experimental.pallas import tpu as pltpu
from jax.sharding import PartitionSpec as P

negative = -1e30
documents = 16
longest = 1024
head = 128
pieces = 4
exponent_scale = math.log2(math.e) * head**-0.5
smem = pl.BlockSpec(memory_space=pltpu.SMEM)
vmem = pl.BlockSpec(memory_space=pltpu.VMEM)
limits = pltpu.CompilerParams(vmem_limit_bytes=44 * 1024 * 1024)
large = pltpu.CompilerParams(vmem_limit_bytes=56 * 1024 * 1024)


def split_pairs(raw, wide, rows):
    wide[: 2 * rows, :] = raw.astype(jnp.float32)
    keys = wide[pl.ds(0, rows, 2), :]
    values = wide[pl.ds(1, rows, 2), :]
    return jnp.concatenate([keys, values], axis=1).astype(jnp.bfloat16)


def spread_kernel(cache_ref, spread_ref, wide):
    shard = split_pairs(cache_ref[...], wide, spread_ref.shape[1])
    for target in range(spread_ref.shape[0]):
        spread_ref[target] = shard


def prepare_kernel(
    new_ref,
    before_ref,
    new_doc_ref,
    cache_doc_ref,
    pair_ref,
    own_ref,
    starts_ref,
    pick_ref,
    wide,
    *,
    turns,
    period,
):
    tok = pair_ref.shape[0] // 2
    pair_ref[:tok] = split_pairs(before_ref[...], wide, tok)
    own = split_pairs(new_ref[...], wide, tok)
    pair_ref[tok:] = own
    own_ref[...] = own
    new_doc = new_doc_ref[...]
    cache_doc = cache_doc_ref[...]
    first_doc = new_doc[:, :1]
    last_doc = new_doc[:, -1:]
    low = jnp.zeros(first_doc.shape, jnp.float32)
    high = jnp.full(first_doc.shape, float(cache_doc.size), jnp.float32)
    starts_ref[0] = 0
    starts_ref[documents + 1] = 0
    for doc in range(1, documents):
        before = jnp.sum((new_doc < doc).astype(jnp.float32))
        starts_ref[doc] = before.astype(jnp.int32)
        before = jnp.sum((cache_doc < doc).astype(jnp.float32))
        starts_ref[documents + 1 + doc] = before.astype(jnp.int32)
        low = jnp.where(first_doc == doc, before, low)
        high = jnp.where(last_doc == doc - 1, before, high)
    starts_ref[documents] = new_doc.size
    starts_ref[2 * documents + 1] = cache_doc.size
    widest = jnp.max(high - low).astype(jnp.int32)
    pick = jnp.int32(0)
    for turn in turns[:-1]:
        pick += (widest > turn * period).astype(jnp.int32)
    pick_ref[0] = pick


def pack_cache_kernel(place_ref, starts_ref, shards_ref, out_ref, *, turns, tok):
    groups, shard_rows, _ = shards_ref.shape
    count = out_ref.shape[0]
    period = count * shard_rows
    cp_index = place_ref[0] // count
    blk_index = place_ref[0] % count
    row = lax.broadcasted_iota(jnp.int32, (shard_rows, 1), 0)
    for target in range(count):
        first = (cp_index * count + target) * tok
        low = jnp.int32(0)
        for doc in range(1, documents):
            low = jnp.where(first >= starts_ref[doc], starts_ref[documents + 1 + doc], low)
        reached = low - blk_index * shard_rows
        group = (reached - (shard_rows - 1) + period - 1) // period
        cut = reached - group * period
        for at, turn in enumerate(turns):
            here = jnp.minimum(group + turn, groups - 1)
            after = jnp.minimum(group + turn + 1, groups - 1)
            chosen = jnp.where(
                row >= cut,
                shards_ref[here].astype(jnp.float32),
                shards_ref[after].astype(jnp.float32),
            )
            out_ref[target, at * shard_rows : (at + 1) * shard_rows] = chosen.astype(
                jnp.bfloat16
            )


def row_bounds(starts_ref, first, tok):
    row_place = first + lax.broadcasted_iota(jnp.int32, (tok, 1), 0)
    row_start = jnp.zeros((tok, 1), jnp.int32)
    row_low = jnp.zeros((tok, 1), jnp.int32)
    row_high = jnp.full((tok, 1), starts_ref[documents + 2], jnp.int32)
    for doc in range(1, documents):
        reached = row_place >= starts_ref[doc]
        row_start = jnp.where(reached, starts_ref[doc], row_start)
        row_low = jnp.where(reached, starts_ref[documents + 1 + doc], row_low)
        row_high = jnp.where(reached, starts_ref[documents + 2 + doc], row_high)
    return row_place, row_start, row_low, row_high


def block_bounds(starts_ref, first, tok):
    new_low = jnp.int32(0)
    cache_low = jnp.int32(0)
    cache_high = starts_ref[documents + 2]
    for doc in range(1, documents):
        start = starts_ref[doc]
        new_low = jnp.where(first >= start, start, new_low)
        cache_low = jnp.where(first >= start, starts_ref[documents + 1 + doc], cache_low)
        cache_high = jnp.where(
            first + tok - 1 >= start, starts_ref[documents + 2 + doc], cache_high
        )
    return new_low, cache_low, cache_high


def score(queries_ref, keys, allowed, scores_ref, at, lane_max):
    for h in range(lane_max.shape[0]):
        scores = lax.dot_general(
            queries_ref[:, h * head : (h + 1) * head],
            keys,
            (((1,), (1,)), ((), ())),
            preferred_element_type=jnp.float32,
        )
        scores = jnp.where(allowed, scores, negative)
        scores_ref[at, h] = scores
        best = scores[:, :head]
        for part in range(1, scores.shape[1] // head):
            best = jnp.maximum(best, scores[:, part * head : (part + 1) * head])
        lane_max[h] = jnp.maximum(lane_max[h], best)


def weigh(values, scores_ref, at, lane_max, lane_sum, total):
    for h in range(lane_max.shape[0]):
        scores = scores_ref[at, h]
        best = lane_max[h]
        added = lane_sum[h]
        parts = []
        for part in range(scores.shape[1] // head):
            piece = scores[:, part * head : (part + 1) * head]
            weight = jnp.exp2((piece - best) * exponent_scale)
            added = added + weight
            parts.append(weight.astype(jnp.bfloat16))
        lane_sum[h] = added
        rounded = parts[0] if len(parts) == 1 else jnp.concatenate(parts, axis=1)
        total[h] += jnp.dot(rounded, values, preferred_element_type=jnp.float32)


def settle(lane_max):
    for h in range(lane_max.shape[0]):
        best = jnp.max(lane_max[h], axis=1, keepdims=True)
        lane_max[h] = jnp.broadcast_to(best, lane_max.shape[1:])


def new_kernel(
    place_ref,
    starts_ref,
    queries_ref,
    pair_ref,
    second_ref,
    fourth_ref,
    sixth_ref,
    lane_max,
    lane_sum,
    total,
    window,
    scores_ref,
):
    tok = queries_ref.shape[0]
    count = window.shape[0] // tok
    block = place_ref[0]
    first = block * tok
    row_place, row_start, _, _ = row_bounds(starts_ref, first, tok)
    new_low, _, _ = block_bounds(starts_ref, first, tok)
    lane_max[...] = jnp.full(lane_max.shape, negative, jnp.float32)
    lane_sum[...] = jnp.zeros(lane_sum.shape, jnp.float32)
    total[...] = jnp.zeros(total.shape, jnp.float32)
    filled = 0
    for part in (sixth_ref, fourth_ref, second_ref, pair_ref):
        window[filled : filled + part.shape[0]] = part[...]
        filled += part.shape[0]
    oldest = block - count + 1
    first_block = jnp.maximum(new_low // tok, oldest)

    @pl.loop(first_block, block + 1)
    def _(number):
        slot = number - oldest
        keys = window[pl.ds(pl.multiple_of(slot * tok, tok), tok), :head]
        key_place = number * tok + lax.broadcasted_iota(jnp.int32, (1, tok), 1)
        allowed = (key_place >= row_start) & (key_place <= row_place)
        score(queries_ref, keys, allowed, scores_ref, slot, lane_max)

    settle(lane_max)

    @pl.loop(first_block, block + 1)
    def _(number):
        slot = number - oldest
        values = window[pl.ds(pl.multiple_of(slot * tok, tok), tok), head:]
        weigh(values, scores_ref, slot, lane_max, lane_sum, total)


def cache_kernel(
    place_ref,
    starts_ref,
    cache_len_ref,
    queries_ref,
    eighth_ref,
    arrived_ref,
    new_max_ref,
    new_sum_ref,
    new_total_ref,
    out_ref,
    cache_scores,
    eighth_scores,
    lane_max,
    lane_sum,
    total,
    *,
    shard_rows,
    rounds,
):
    tok = queries_ref.shape[0]
    heads = lane_max.shape[0]
    count = arrived_ref.shape[0]
    shards = cache_len_ref.shape[0]
    period = count * shard_rows
    span = pieces * shard_rows
    block = place_ref[0]
    first = block * tok
    row_place, row_start, row_low, row_high = row_bounds(starts_ref, first, tok)
    new_low, cache_low, cache_high = block_bounds(starts_ref, first, tok)
    lane_max[...] = new_max_ref[...]
    farthest = block - count
    reaches = new_low // tok <= farthest

    @pl.when(reaches)
    def _():
        key_place = farthest * tok + lax.broadcasted_iota(jnp.int32, (1, tok), 1)
        allowed = (key_place >= row_start) & (key_place <= row_place)
        score(queries_ref, eighth_ref[:, :head], allowed, eighth_scores, 0, lane_max)

    def cache_tile(number):
        turn = number // (count // pieces)
        source = number % (count // pieces) * pieces
        base = cache_low + turn * period
        begin = base + jnp.bitwise_and(source * shard_rows - base, period - 1)
        holds = jnp.bitwise_and(base - source * shard_rows, period - 1) < span
        return turn, source, base, (begin < cache_high) | (holds & (base < cache_high))

    def cache_part(turn, source, first_lane):
        offset = pl.multiple_of(turn * shard_rows, shard_rows)
        return jnp.concatenate(
            [
                arrived_ref[source + part, pl.ds(offset, shard_rows), first_lane : first_lane + head]
                for part in range(pieces)
            ],
            axis=0,
        )

    tiles = rounds * count // pieces

    @pl.loop(0, tiles)
    def _(number):
        turn, source, base, needed = cache_tile(number)

        @pl.when(needed)
        def _():
            lane = lax.broadcasted_iota(jnp.int32, (1, span), 1)
            place = base + jnp.bitwise_and(source * shard_rows + lane - base, period - 1)
            shard = place // shard_rows
            filled = jnp.zeros((1, span), jnp.int32)
            for part in range(pieces):
                edge = (source + part) * shard_rows
                for at in (0, shard_rows - 1):
                    where = base + jnp.bitwise_and(edge + at - base, period - 1)
                    where = where // shard_rows
                    length = cache_len_ref[jnp.minimum(where, shards - 1)]
                    filled = jnp.where(shard == where, length, filled)
            usable = jnp.bitwise_and(place, shard_rows - 1) < filled
            allowed = (place >= row_low) & (place < row_high) & usable
            keys = cache_part(turn, source, 0)
            score(queries_ref, keys, allowed, cache_scores, number, lane_max)

    settle(lane_max)
    for h in range(heads):
        scale = jnp.exp2((new_max_ref[h] - lane_max[h]) * exponent_scale)
        lane_sum[h] = new_sum_ref[h] * scale
        total[h] = new_total_ref[h] * scale

    @pl.when(reaches)
    def _():
        weigh(eighth_ref[:, head:], eighth_scores, 0, lane_max, lane_sum, total)

    @pl.loop(0, tiles)
    def _(number):
        turn, source, base, needed = cache_tile(number)

        @pl.when(needed)
        def _():
            values = cache_part(turn, source, head)
            weigh(values, cache_scores, number, lane_max, lane_sum, total)

    for h in range(heads):
        row_total = jnp.sum(lane_sum[h], axis=1, keepdims=True)
        out_ref[:, h * head : (h + 1) * head] = (total[h] / row_total).astype(jnp.bfloat16)


def local(queries, new_kv, cached_key_value, new_doc, cache_doc, cache_len):
    tok = queries.shape[0]
    width = queries.shape[-1]
    heads = width // head
    shard_rows = cached_key_value.shape[0]
    blk_count = lax.axis_size("blk")
    cp_count = lax.axis_size("cp")
    head_count = lax.axis_size("head")
    assert tok * blk_count >= longest
    block_count = cp_count * blk_count
    period = blk_count * shard_rows
    turns = [2, 3, cp_count]
    place = lax.axis_index(("cp", "blk")).astype(jnp.int32)[None]

    def ahead(value, steps):
        pairs = [(block, (block + steps) % block_count) for block in range(block_count)]
        return lax.ppermute(value, ("cp", "blk"), pairs)

    new_raw = new_kv.reshape(2 * tok, head)
    cache_raw = cached_key_value.reshape(2 * shard_rows, head)
    raw_before = ahead(new_raw, 1)
    spread = pl.pallas_call(
        spread_kernel,
        out_shape=jax.ShapeDtypeStruct((cp_count, shard_rows, 2 * head), jnp.bfloat16),
        in_specs=[vmem],
        out_specs=vmem,
        scratch_shapes=[pltpu.VMEM((2 * shard_rows, head), jnp.float32)],
        compiler_params=large,
    )(cache_raw)
    spread, raw_before = lax.optimization_barrier((spread, raw_before))
    shards = lax.all_to_all(spread, "cp", split_axis=0, concat_axis=0)
    operands = (new_raw, raw_before, new_doc.reshape(-1, tok), cache_doc.reshape(-1, 128))
    pair, own, starts, pick = pl.pallas_call(
        functools.partial(prepare_kernel, turns=turns, period=period),
        grid=(1,),
        out_shape=[
            jax.ShapeDtypeStruct((2 * tok, 2 * head), jnp.bfloat16),
            jax.ShapeDtypeStruct((tok, 2 * head), jnp.bfloat16),
            jax.ShapeDtypeStruct((2 * documents + 2,), jnp.int32),
            jax.ShapeDtypeStruct((1,), jnp.int32),
        ],
        in_specs=[pl.BlockSpec(operand.shape, lambda i: (0, 0)) for operand in operands],
        out_specs=[vmem, vmem, smem, smem],
        scratch_shapes=[pltpu.VMEM((2 * tok, head), jnp.float32)],
        compiler_params=limits,
    )(*operands)
    second = ahead(pair, 2)
    fourth = ahead(pair, 4)
    sixth = ahead(pair, 6)
    shards, own, second, fourth, sixth = lax.optimization_barrier(
        (shards, own, second, fourth, sixth)
    )
    eighth = ahead(own, 8)

    def cached_rows(turns, shards, starts):
        rows = len(turns) * shard_rows
        packed = pl.pallas_call(
            functools.partial(pack_cache_kernel, turns=turns, tok=tok),
            out_shape=jax.ShapeDtypeStruct((blk_count, rows, 2 * head), jnp.bfloat16),
            in_specs=[smem, smem, vmem],
            out_specs=vmem,
            compiler_params=limits,
        )(place, starts, shards)
        return lax.all_to_all(packed, "blk", split_axis=0, concat_axis=0)

    arrived = cached_rows(range(turns[0]), shards, starts)
    state = jax.ShapeDtypeStruct((heads, tok, head), jnp.float32)
    states = pl.pallas_call(
        new_kernel,
        out_shape=[state] * 3,
        in_specs=[smem] * 2 + [vmem] * 5,
        out_specs=[vmem] * 3,
        scratch_shapes=[
            pltpu.VMEM((blk_count * tok, 2 * head), jnp.bfloat16),
            pltpu.VMEM((blk_count, heads, tok, tok), jnp.float32),
        ],
        compiler_params=limits,
        cost_estimate=pl.CostEstimate(
            flops=4 * heads * tok * tok * head * blk_count,
            bytes_accessed=8 * tok * width,
            transcendentals=heads * tok * tok * blk_count,
        ),
    )(place, starts, queries[:, 0], pair, second, fourth, sixth)

    def attend(rounds):
        def run(shards, eighth, arrived, starts, cache_len, queries, states):
            if rounds > turns[0]:
                more = cached_rows(range(turns[0], rounds), shards, starts)
                arrived = jnp.concatenate([arrived, more], axis=1)
            span = pieces * shard_rows
            tiles = rounds * blk_count // pieces
            return pl.pallas_call(
                functools.partial(cache_kernel, shard_rows=shard_rows, rounds=rounds),
                out_shape=jax.ShapeDtypeStruct((tok, width), jnp.bfloat16),
                in_specs=[smem] * 3 + [vmem] * 6,
                out_specs=vmem,
                scratch_shapes=[
                    pltpu.VMEM((tiles, heads, tok, span), jnp.float32),
                    pltpu.VMEM((1, heads, tok, tok), jnp.float32),
                    pltpu.VMEM((heads, tok, head), jnp.float32),
                    pltpu.VMEM((heads, tok, head), jnp.float32),
                    pltpu.VMEM((heads, tok, head), jnp.float32),
                ],
                compiler_params=limits,
            )(place, starts, cache_len, queries, eighth, arrived, *states)

        return run

    attended = lax.switch(
        pick[0],
        [attend(turn) for turn in turns],
        shards,
        eighth,
        arrived,
        starts,
        cache_len,
        queries[:, 0],
        states,
    )
    share = tok // head_count
    moved = lax.all_to_all(
        attended.reshape(head_count, share, width), "head", split_axis=0, concat_axis=0
    )
    return jnp.transpose(moved, (1, 0, 2))


def solution(mesh):
    placed = (
        P(("cp", "blk"), "head", None),
        P(("cp", "blk"), "head", None, None),
        P(("cp", "blk"), "head", None, None),
        P(),
        P(),
        P(),
    )
    return jax.shard_map(
        local,
        mesh=mesh,
        in_specs=placed,
        out_specs=P(("cp", "blk", "head"), None, None),
        check_vma=False,
    )
```

time: 89.2 us -> 79.6 us (0.89)
  the two profiles are of different devices: /device:TPU:3 before, /device:TPU:1 now
where the time goes in v1:
time: 79.6 us; the launch traced here: 78.9 us
  starting transfers between devices  32 us (40%)
  blocking collectives  22 us (28%)
  waiting for transfers between devices  12.5 us (16%)
  Pallas kernels  8.5 us (11%)
  local copies, waits for them, and re-layouts  3.19 us (4%)
    all_to_all x1, blocking collectives, local(): lax.all_to_all(attended.reshape(head_count, share, width), 'head', split_...  22 us
    ppermute x5, starting transfers between devices, ahead(): return lax.ppermute(value, ('cp', 'blk'), pairs)  18.1 us
    ppermute x5, waiting for transfers between devices, ahead(): return lax.ppermute(value, ('cp', 'blk'), pairs)  10.5 us
    all_to_all x1, starting transfers between devices, local(): shards = lax.all_to_all(spread, 'cp', split_axis=0, concat_axis=0)  10.4 us
    all_to_all x1, starting transfers between devices, cached_rows(): return lax.all_to_all(packed, 'blk', split_axis=0, concat_axis=0)  3.49 us
    pallas_call x1, Pallas kernels, run(): pl.pallas_call(functools.partial(cache_kernel, shard_rows=shard_rows, rou...  2.5 us
    unnamed x10, local copies, waits for them, and re-layouts  2.33 us
    all_to_all x1, waiting for transfers between devices, cached_rows(): return lax.all_to_all(packed, 'blk', split_axis=0, concat_axis=0)  2.01 us
  transfers between devices with their start and end apart: 7, of which 5 were waited for; matrix products, arithmetic and copies ran while one was open for 0% of the time, Pallas kernels for 6%

profile of v1, /device:TPU:1, one launch (start us, length us, event | category | flops | bytes accessed | tf_op | source)
XLA Modules:
  0.0 78.9 jit_solution(17606086504249413609)
XLA Ops:
  0.0 4.2 %collective-permute-start = (bf16[256,128]{1,0:T(8,128)(2,1)}, bf16[256,128]{1,0:T(8,128)(2,1)S(1)}, u32[]{:S(2)}, u32[]{:S(2)}) collective-permute-start(bf16[256,128]{1,0:T(8,128)(2,1)} %bitcast.9), channel_id=1, source_target_pairs={{0,8},{8,16},{16,24},{24,32},{32,40},{40,48},{48,56},{56,64},{64,7... | collective-permute-start | bytes 196616 | tf_op jit(solution)/shard_map/ppermute | solution.py:341
  4.2 1.5 %shard_map.64 = bf16[8,64,256]{2,1,0:T(8,128)(2,1)} custom-call(bf16[128,128]{1,0:T(8,128)(2,1)} %bitcast.19), custom_call_target="tpu_custom_call" | custom-call | tf_op jit(solution)/shard_map/pallas_call | solution.py:346
  5.7 3.4 %collective-permute-done.before_ref = bf16[256,128]{1,0:T(8,128)(2,1)S(1)} collective-permute-done((bf16[256,128]{1,0:T(8,128)(2,1)}, bf16[256,128]{1,0:T(8,128)(2,1)S(1)}, u32[]{:S(2)}, u32[]{:S(2)}) %collective-permute-start) | collective-permute-done | bytes 65568 | tf_op jit(solution)/shard_map/ppermute | solution.py:341
  9.1 10.4 %all-to-all-start.2 = ((bf16[8,64,256]{2,1,0:T(8,128)(2,1)}), bf16[8,64,256]{2,1,0:T(8,128)(2,1)S(1)}, u32[]{:S(2)}, u32[]{:S(2)}) async-start(bf16[8,64,256]{2,1,0:T(8,128)(2,1)} %shard_map.64), calls=%async_computation.2 | async-start | bytes 524288 | tf_op jit(solution)/shard_map/all_to_all | solution.py:355
  19.4 0.9 %copy-done = bf16[128,1,2,128]{3,2,1,0:T(2,128)(2,1)S(1)} copy-done((bf16[128,1,2,128]{3,2,1,0:T(2,128)(2,1)S(1)}, bf16[128,1,2,128]{3,2,1,0:T(2,128)(2,1)}, u32[]{:S(2)}) %copy-start) | copy-done | bytes 65560
  20.3 0.8 copy-done.1
  21.1 0.7 copy-done.2
  21.8 0.9 %shard_map.65 = (bf16[256,256]{1,0:T(8,128)(2,1)S(1)}, bf16[128,256]{1,0:T(8,128)(2,1)S(1)}, s32[34]{0:T(128)S(1)}, s32[1]{0:T(128)}) custom-call(bf16[256,128]{1,0:T(8,128)(2,1)S(1)} %bitcast.10, bf16[256,128]{1,0:T(8,128)(2,1)S(1)} %collective-permute-done.before_ref, s32[64,128]{1,0:T(8,128)S(1)} %bitcast.11, s32[32,128]{1,0:T(8,128)S(1)} %bitcast.12), custom_call_target="tpu_custom_call" | custom-call | tf_op jit(solution)/shard_map/pallas_call | solution.py:357
  22.7 1.9 %collective-permute-start.3 = (bf16[256,256]{1,0:T(8,128)(2,1)S(1)}, bf16[256,256]{1,0:T(8,128)(2,1)S(1)}, u32[]{:S(2)}, u32[]{:S(2)}) collective-permute-start(bf16[256,256]{1,0:T(8,128)(2,1)S(1)} %get-tuple-element.115.pair_ref), channel_id=1, source_target_pairs={{0,48},{8,56},{16,64},{24,72},{32,80},{40,88},{48,96},{56,104},{64... | collective-permute-start | bytes 393224 | tf_op jit(solution)/shard_map/ppermute | solution.py:341
  24.6 3.7 %collective-permute-start.2 = (bf16[256,256]{1,0:T(8,128)(2,1)S(1)}, bf16[256,256]{1,0:T(8,128)(2,1)S(1)}, u32[]{:S(2)}, u32[]{:S(2)}) collective-permute-start(bf16[256,256]{1,0:T(8,128)(2,1)S(1)} %get-tuple-element.115.pair_ref), channel_id=1, source_target_pairs={{0,32},{8,40},{16,48},{24,56},{32,64},{40,72},{48,80},{56,88},{64,... | collective-permute-start | bytes 393224 | tf_op jit(solution)/shard_map/ppermute | solution.py:341
  28.4 3.8 %collective-permute-start.1 = (bf16[256,256]{1,0:T(8,128)(2,1)S(1)}, bf16[256,256]{1,0:T(8,128)(2,1)S(1)}, u32[]{:S(2)}, u32[]{:S(2)}) collective-permute-start(bf16[256,256]{1,0:T(8,128)(2,1)S(1)} %get-tuple-element.115.pair_ref), channel_id=1, source_target_pairs={{0,16},{8,24},{16,32},{24,40},{32,48},{40,56},{48,64},{56,72},{64,... | collective-permute-start | bytes 393224 | tf_op jit(solution)/shard_map/ppermute | solution.py:341
  32.2 0.0 collective-permute-done.3.sixth_ref
  32.2 0.2 collective-permute-done.2.fourth_ref
  32.4 6.7 %collective-permute-done.1.second_ref = bf16[256,256]{1,0:T(8,128)(2,1)S(1)} collective-permute-done((bf16[256,256]{1,0:T(8,128)(2,1)S(1)}, bf16[256,256]{1,0:T(8,128)(2,1)S(1)}, u32[]{:S(2)}, u32[]{:S(2)}) %collective-permute-start.1) | collective-permute-done | bytes 131104 | tf_op jit(solution)/shard_map/ppermute | solution.py:341
  39.1 1.6 %shard_map.66 = bf16[8,128,256]{2,1,0:T(8,128)(2,1)} custom-call(s32[1]{0:T(128)} %bitcast.5.place_ref, s32[34]{0:T(128)S(1)} %get-tuple-element.112.starts_ref, bf16[8,64,256]{2,1,0:T(8,128)(2,1)S(1)} %all-to-all-done.2.shards_ref), custom_call_target="tpu_custom_call" | custom-call | tf_op jit(solution)/shard_map/pallas_call | solution.py:381
  40.7 3.5 %all-to-all-start.3 = ((bf16[8,128,256]{2,1,0:T(8,128)(2,1)}), bf16[8,128,256]{2,1,0:T(8,128)(2,1)S(1)}, u32[]{:S(2)}, u32[]{:S(2)}) async-start(bf16[8,128,256]{2,1,0:T(8,128)(2,1)} %shard_map.66), calls=%async_computation.3 | async-start | bytes 1048576 | tf_op jit(solution)/shard_map/all_to_all | solution.py:388
  44.2 4.5 %collective-permute-start.4 = (bf16[128,256]{1,0:T(8,128)(2,1)S(1)}, bf16[128,256]{1,0:T(8,128)(2,1)S(1)}, u32[]{:S(2)}, u32[]{:S(2)}) collective-permute-start(bf16[128,256]{1,0:T(8,128)(2,1)S(1)} %get-tuple-element.116), channel_id=1, source_target_pairs={{0,64},{8,72},{16,80},{24,88},{32,96},{40,104},{48,112},{56,120},{... | collective-permute-start | bytes 196616 | tf_op jit(solution)/shard_map/ppermute | solution.py:341
  49.4 2.0 %shard_map.67 = (f32[8,128,128]{2,1,0:T(8,128)S(1)}, f32[8,128,128]{2,1,0:T(8,128)S(1)}, f32[8,128,128]{2,1,0:T(8,128)S(1)}) custom-call(s32[1]{0:T(128)} %bitcast.5.place_ref, s32[34]{0:T(128)S(1)} %get-tuple-element.112.starts_ref, bf16[128,1024]{1,0:T(8,128)(2,1)S(1)} %bitcast.13, bf16[256,256]{1,0:T(8,128)(2,1)S(1)} %get-tuple-element.115.pair_ref, ...), custom_call_target="tpu_custom_call" | custom-call | flops 536870912 | bytes 1048576 | tf_op jit(solution)/shard_map/pallas_call | solution.py:392
  51.4 0.2 collective-permute-done.4
  51.5 2.0 %all-to-all-done.3 = bf16[8,128,256]{2,1,0:T(8,128)(2,1)S(1)} async-done(((bf16[8,128,256]{2,1,0:T(8,128)(2,1)}), bf16[8,128,256]{2,1,0:T(8,128)(2,1)S(1)}, u32[]{:S(2)}, u32[]{:S(2)}) %all-to-all-start.3) | async-done | bytes 524320 | tf_op jit(solution)/shard_map/all_to_all | solution.py:388
  53.5 2.5 %conditional.1 = (bf16[128,1024]{1,0:T(8,128)(2,1)S(1)}) conditional(s32[]{:T(128)} %bitcast.4, (s32[1]{0:T(128)}, s32[34]{0:T(128)S(1)}, s32[64]{0:T(128)S(1)}, bf16[128,1024]{1,0:T(8,128)(2,1)S(1)}, bf16[128,256]{1,0:T(8,128)(2,1)S(1)}, /*index=5*/bf16[8,128,256]{2,1,0:T(8,128)(2,1)S(1)}, f32[8,128,128]{2,1,0:T(8,128)S(1)}, ...), branch_computations={%region_0.0_spmd, %region_1.0_spmd, %region_2.0_spmd} | conditional | flops 4194304 | bytes 7340040 | solution.py:433
  53.5 2.5 %branch_0_fun.1 = bf16[128,1024]{1,0:T(8,128)(2,1)S(1)} custom-call(s32[1]{0:T(128)} %get-tuple-element.66.place_ref, s32[34]{0:T(128)S(1)} %get-tuple-element.68.starts_ref, s32[64]{0:T(128)S(1)} %get-tuple-element.69.cache_len_ref, bf16[128,1024]{1,0:T(8,128)(2,1)S(1)} %get-tuple-element.70.queries_ref, bf16[128,256]{1,0:T(8,128)(2,1)S(1)} %get-tuple-element.71.eighth_ref, ...), custom_call_target="tpu_custom_call" | custom-call | tf_op jit(solution)/shard_map/cond/branch_0_fun/pallas_call | solution.py:416
  56.1 22.0 %all_to_all.25 = bf16[8,16,1024]{2,1,0:T(8,128)(2,1)S(1)} all-to-all(bf16[8,16,1024]{2,1,0:T(8,128)(2,1)S(1)} %bitcast.18), channel_id=1, replica_groups=mesh['cp'=8,'blk'=8,'head'=8] {'head'}, dimensions={0} | all-to-all | bytes 524288 | tf_op jit(solution)/shard_map/all_to_all | solution.py:445
  78.0 0.9 %copy.7 = bf16[16,8,1024]{2,1,0:T(8,128)(2,1)} copy(bf16[16,8,1024]{2,0,1:T(8,128)(2,1)S(1)} %bitcast.17) | data formatting | bytes 524288 | tf_op jit(solution)/shard_map/transpose | solution.py:448
  (8 shorter events, 0.0 us)
Async XLA Ops:
  0.0 49.4 %copy-start.3 = (bf16[128,1,1024]{2,0,1:T(8,128)(2,1)S(1)}, bf16[128,1,1024]{2,0,1:T(8,128)(2,1)}, u32[]{:S(2)}) copy-start(bf16[128,1,1024]{2,0,1:T(8,128)(2,1)} %param.9) | copy-start | bytes 786436
  0.0 9.1 %collective-permute-start = (bf16[256,128]{1,0:T(8,128)(2,1)}, bf16[256,128]{1,0:T(8,128)(2,1)S(1)}, u32[]{:S(2)}, u32[]{:S(2)}) collective-permute-start(bf16[256,128]{1,0:T(8,128)(2,1)} %bitcast.9), channel_id=1, source_target_pairs={{0,8},{8,16},{16,24},{24,32},{32,40},{40,48},{48,56},{56,64},{64,7... | collective-permute-start | bytes 196616 | tf_op jit(solution)/shard_map/ppermute | solution.py:341
  9.1 30.1 %all-to-all-start.2 = ((bf16[8,64,256]{2,1,0:T(8,128)(2,1)}), bf16[8,64,256]{2,1,0:T(8,128)(2,1)S(1)}, u32[]{:S(2)}, u32[]{:S(2)}) async-start(bf16[8,64,256]{2,1,0:T(8,128)(2,1)} %shard_map.64), calls=%async_computation.2 | async-start | bytes 524288 | tf_op jit(solution)/shard_map/all_to_all | solution.py:355
  19.4 34.1 %copy-start.4 = (s32[64]{0:T(128)S(1)}, s32[64]{0:T(128)}, u32[]{:S(2)}) copy-start(s32[64]{0:T(128)} %param.14) | copy-start | bytes 772
  19.4 0.9 %copy-start = (bf16[128,1,2,128]{3,2,1,0:T(2,128)(2,1)S(1)}, bf16[128,1,2,128]{3,2,1,0:T(2,128)(2,1)}, u32[]{:S(2)}) copy-start(bf16[128,1,2,128]{3,2,1,0:T(2,128)(2,1)} %param.10) | copy-start | bytes 196612
  20.3 0.8 copy-start.1
  21.0 0.7 copy-start.2
  22.7 9.5 %collective-permute-start.3 = (bf16[256,256]{1,0:T(8,128)(2,1)S(1)}, bf16[256,256]{1,0:T(8,128)(2,1)S(1)}, u32[]{:S(2)}, u32[]{:S(2)}) collective-permute-start(bf16[256,256]{1,0:T(8,128)(2,1)S(1)} %get-tuple-element.115.pair_ref), channel_id=1, source_target_pairs={{0,48},{8,56},{16,64},{24,72},{32,80},{40,88},{48,96},{56,104},{64... | collective-permute-start | bytes 393224 | tf_op jit(solution)/shard_map/ppermute | solution.py:341
  24.6 7.8 %collective-permute-start.2 = (bf16[256,256]{1,0:T(8,128)(2,1)S(1)}, bf16[256,256]{1,0:T(8,128)(2,1)S(1)}, u32[]{:S(2)}, u32[]{:S(2)}) collective-permute-start(bf16[256,256]{1,0:T(8,128)(2,1)S(1)} %get-tuple-element.115.pair_ref), channel_id=1, source_target_pairs={{0,32},{8,40},{16,48},{24,56},{32,64},{40,72},{48,80},{56,88},{64,... | collective-permute-start | bytes 393224 | tf_op jit(solution)/shard_map/ppermute | solution.py:341
  28.4 10.8 %collective-permute-start.1 = (bf16[256,256]{1,0:T(8,128)(2,1)S(1)}, bf16[256,256]{1,0:T(8,128)(2,1)S(1)}, u32[]{:S(2)}, u32[]{:S(2)}) collective-permute-start(bf16[256,256]{1,0:T(8,128)(2,1)S(1)} %get-tuple-element.115.pair_ref), channel_id=1, source_target_pairs={{0,16},{8,24},{16,32},{24,40},{32,48},{40,56},{48,64},{56,72},{64,... | collective-permute-start | bytes 393224 | tf_op jit(solution)/shard_map/ppermute | solution.py:341
  40.7 12.8 %all-to-all-start.3 = ((bf16[8,128,256]{2,1,0:T(8,128)(2,1)}), bf16[8,128,256]{2,1,0:T(8,128)(2,1)S(1)}, u32[]{:S(2)}, u32[]{:S(2)}) async-start(bf16[8,128,256]{2,1,0:T(8,128)(2,1)} %shard_map.66), calls=%async_computation.3 | async-start | bytes 1048576 | tf_op jit(solution)/shard_map/all_to_all | solution.py:388
  44.2 7.3 %collective-permute-start.4 = (bf16[128,256]{1,0:T(8,128)(2,1)S(1)}, bf16[128,256]{1,0:T(8,128)(2,1)S(1)}, u32[]{:S(2)}, u32[]{:S(2)}) collective-permute-start(bf16[128,256]{1,0:T(8,128)(2,1)S(1)} %get-tuple-element.116), channel_id=1, source_target_pairs={{0,64},{8,72},{16,80},{24,88},{32,96},{40,104},{48,112},{56,120},{... | collective-permute-start | bytes 196616 | tf_op jit(solution)/shard_map/ppermute | solution.py:341

commit v2 on v1

--- a/solution.py
+++ b/solution.py
@@ -13,9 +13,9 @@
 longest = 1024
 head = 128
 pieces = 4
-exponent_scale = math.log2(math.e) * head**-0.5
 smem = pl.BlockSpec(memory_space=pltpu.SMEM)
 vmem = pl.BlockSpec(memory_space=pltpu.VMEM)
+exponent_scale = math.log2(math.e) * head**-0.5
 limits = pltpu.CompilerParams(vmem_limit_bytes=44 * 1024 * 1024)
 large = pltpu.CompilerParams(vmem_limit_bytes=56 * 1024 * 1024)
 
@@ -34,24 +34,9 @@
 
 
 def prepare_kernel(
-    new_ref,
-    before_ref,
-    new_doc_ref,
-    cache_doc_ref,
-    pair_ref,
-    own_ref,
-    starts_ref,
-    pick_ref,
-    wide,
-    *,
-    turns,
-    period,
+    new_ref, new_doc_ref, cache_doc_ref, own_ref, starts_ref, pick_ref, wide, *, turns, period
 ):
-    tok = pair_ref.shape[0] // 2
-    pair_ref[:tok] = split_pairs(before_ref[...], wide, tok)
-    own = split_pairs(new_ref[...], wide, tok)
-    pair_ref[tok:] = own
-    own_ref[...] = own
+    own_ref[...] = split_pairs(new_ref[...], wide, own_ref.shape[0])
     new_doc = new_doc_ref[...]
     cache_doc = cache_doc_ref[...]
     first_doc = new_doc[:, :1]
@@ -76,12 +61,16 @@
     pick_ref[0] = pick
 
 
-def pack_cache_kernel(place_ref, starts_ref, shards_ref, out_ref, *, turns, tok):
+def pack_kernel(
+    place_ref, starts_ref, shards_ref, own_ref, raw_ref, out_ref, behind_ref, wide, *, rounds
+):
     groups, shard_rows, _ = shards_ref.shape
     count = out_ref.shape[0]
+    tok = own_ref.shape[0]
     period = count * shard_rows
-    cp_index = place_ref[0] // count
-    blk_index = place_ref[0] % count
+    cp_index = place_ref[0]
+    blk_index = place_ref[1]
+    behind_ref[...] = split_pairs(raw_ref[...], wide, tok)
     row = lax.broadcasted_iota(jnp.int32, (shard_rows, 1), 0)
     for target in range(count):
         first = (cp_index * count + target) * tok
@@ -91,7 +80,7 @@
         reached = low - blk_index * shard_rows
         group = (reached - (shard_rows - 1) + period - 1) // period
         cut = reached - group * period
-        for at, turn in enumerate(turns):
+        for turn in range(rounds):
             here = jnp.minimum(group + turn, groups - 1)
             after = jnp.minimum(group + turn + 1, groups - 1)
             chosen = jnp.where(
@@ -99,9 +88,17 @@
                 shards_ref[here].astype(jnp.float32),
                 shards_ref[after].astype(jnp.float32),
             )
-            out_ref[target, at * shard_rows : (at + 1) * shard_rows] = chosen.astype(
+            out_ref[target, turn * shard_rows : (turn + 1) * shard_rows] = chosen.astype(
                 jnp.bfloat16
             )
+
+        @pl.when(blk_index <= target)
+        def _():
+            out_ref[target, rounds * shard_rows :] = own_ref[...]
+
+        @pl.when(blk_index > target)
+        def _():
+            out_ref[target, rounds * shard_rows :] = behind_ref[...]
 
 
 def row_bounds(starts_ref, first, tok):
@@ -169,66 +166,17 @@
         lane_max[h] = jnp.broadcast_to(best, lane_max.shape[1:])
 
 
-def new_kernel(
-    place_ref,
-    starts_ref,
-    queries_ref,
-    pair_ref,
-    second_ref,
-    fourth_ref,
-    sixth_ref,
-    lane_max,
-    lane_sum,
-    total,
-    window,
-    scores_ref,
-):
-    tok = queries_ref.shape[0]
-    count = window.shape[0] // tok
-    block = place_ref[0]
-    first = block * tok
-    row_place, row_start, _, _ = row_bounds(starts_ref, first, tok)
-    new_low, _, _ = block_bounds(starts_ref, first, tok)
-    lane_max[...] = jnp.full(lane_max.shape, negative, jnp.float32)
-    lane_sum[...] = jnp.zeros(lane_sum.shape, jnp.float32)
-    total[...] = jnp.zeros(total.shape, jnp.float32)
-    filled = 0
-    for part in (sixth_ref, fourth_ref, second_ref, pair_ref):
-        window[filled : filled + part.shape[0]] = part[...]
-        filled += part.shape[0]
-    oldest = block - count + 1
-    first_block = jnp.maximum(new_low // tok, oldest)
-
-    @pl.loop(first_block, block + 1)
-    def _(number):
-        slot = number - oldest
-        keys = window[pl.ds(pl.multiple_of(slot * tok, tok), tok), :head]
-        key_place = number * tok + lax.broadcasted_iota(jnp.int32, (1, tok), 1)
-        allowed = (key_place >= row_start) & (key_place <= row_place)
-        score(queries_ref, keys, allowed, scores_ref, slot, lane_max)
-
-    settle(lane_max)
-
-    @pl.loop(first_block, block + 1)
-    def _(number):
-        slot = number - oldest
-        values = window[pl.ds(pl.multiple_of(slot * tok, tok), tok), head:]
-        weigh(values, scores_ref, slot, lane_max, lane_sum, total)
-
-
-def cache_kernel(
+def attention_kernel(
     place_ref,
     starts_ref,
     cache_len_ref,
     queries_ref,
-    eighth_ref,
     arrived_ref,
-    new_max_ref,
-    new_sum_ref,
-    new_total_ref,
+    behind_ref,
     out_ref,
+    new_scores,
+    far_scores,
     cache_scores,
-    eighth_scores,
     lane_max,
     lane_sum,
     total,
@@ -242,19 +190,42 @@
     shards = cache_len_ref.shape[0]
     period = count * shard_rows
     span = pieces * shard_rows
-    block = place_ref[0]
+    new_offset = rounds * shard_rows
+    block = place_ref[0] * count + place_ref[1]
     first = block * tok
     row_place, row_start, row_low, row_high = row_bounds(starts_ref, first, tok)
     new_low, cache_low, cache_high = block_bounds(starts_ref, first, tok)
-    lane_max[...] = new_max_ref[...]
+    lane_max[...] = jnp.full(lane_max.shape, negative, jnp.float32)
+    lane_sum[...] = jnp.zeros(lane_sum.shape, jnp.float32)
+    total[...] = jnp.zeros(total.shape, jnp.float32)
     farthest = block - count
-    reaches = new_low // tok <= farthest
+    first_block = new_low // tok
+    new_tiles = jnp.minimum((block - first_block) // 2 + 1, count // 2)
+    reaches = first_block <= farthest
+
+    def new_part(number, first_lane):
+        lanes = slice(first_lane, first_lane + head)
+        return jnp.concatenate(
+            [
+                arrived_ref[lax.rem(block - 2 * number - back + count, count), new_offset:, lanes]
+                for back in (1, 0)
+            ],
+            axis=0,
+        )
+
+    def new_allowed(place, lanes):
+        key_place = place + lax.broadcasted_iota(jnp.int32, (1, lanes), 1)
+        return (key_place >= row_start) & (key_place <= row_place)
+
+    @pl.loop(0, new_tiles)
+    def _(number):
+        allowed = new_allowed((block - 2 * number - 1) * tok, 2 * tok)
+        score(queries_ref, new_part(number, 0), allowed, new_scores, number, lane_max)
 
     @pl.when(reaches)
     def _():
-        key_place = farthest * tok + lax.broadcasted_iota(jnp.int32, (1, tok), 1)
-        allowed = (key_place >= row_start) & (key_place <= row_place)
-        score(queries_ref, eighth_ref[:, :head], allowed, eighth_scores, 0, lane_max)
+        allowed = new_allowed(farthest * tok, tok)
+        score(queries_ref, behind_ref[:, :head], allowed, far_scores, 0, lane_max)
 
     def cache_tile(number):
         turn = number // (count // pieces)
@@ -299,14 +270,14 @@
             score(queries_ref, keys, allowed, cache_scores, number, lane_max)
 
     settle(lane_max)
-    for h in range(heads):
-        scale = jnp.exp2((new_max_ref[h] - lane_max[h]) * exponent_scale)
-        lane_sum[h] = new_sum_ref[h] * scale
-        total[h] = new_total_ref[h] * scale
+
+    @pl.loop(0, new_tiles)
+    def _(number):
+        weigh(new_part(number, head), new_scores, number, lane_max, lane_sum, total)
 
     @pl.when(reaches)
     def _():
-        weigh(eighth_ref[:, head:], eighth_scores, 0, lane_max, lane_sum, total)
+        weigh(behind_ref[:, head:], far_scores, 0, lane_max, lane_sum, total)
 
     @pl.loop(0, tiles)
     def _(number):
@@ -331,18 +302,11 @@
     cp_count = lax.axis_size("cp")
     head_count = lax.axis_size("head")
     assert tok * blk_count >= longest
-    block_count = cp_count * blk_count
+    place = jnp.stack([lax.axis_index("cp"), lax.axis_index("blk")]).astype(jnp.int32)
     period = blk_count * shard_rows
     turns = [2, 3, cp_count]
-    place = lax.axis_index(("cp", "blk")).astype(jnp.int32)[None]
-
-    def ahead(value, steps):
-        pairs = [(block, (block + steps) % block_count) for block in range(block_count)]
-        return lax.ppermute(value, ("cp", "blk"), pairs)
-
     new_raw = new_kv.reshape(2 * tok, head)
     cache_raw = cached_key_value.reshape(2 * shard_rows, head)
-    raw_before = ahead(new_raw, 1)
     spread = pl.pallas_call(
         spread_kernel,
         out_shape=jax.ShapeDtypeStruct((cp_count, shard_rows, 2 * head), jnp.bfloat16),
@@ -351,95 +315,65 @@
         scratch_shapes=[pltpu.VMEM((2 * shard_rows, head), jnp.float32)],
         compiler_params=large,
     )(cache_raw)
-    spread, raw_before = lax.optimization_barrier((spread, raw_before))
     shards = lax.all_to_all(spread, "cp", split_axis=0, concat_axis=0)
-    operands = (new_raw, raw_before, new_doc.reshape(-1, tok), cache_doc.reshape(-1, 128))
-    pair, own, starts, pick = pl.pallas_call(
+    raw_behind = lax.ppermute(new_raw, "cp", [(i, (i + 1) % cp_count) for i in range(cp_count)])
+    own, starts, pick = pl.pallas_call(
         functools.partial(prepare_kernel, turns=turns, period=period),
-        grid=(1,),
         out_shape=[
-            jax.ShapeDtypeStruct((2 * tok, 2 * head), jnp.bfloat16),
             jax.ShapeDtypeStruct((tok, 2 * head), jnp.bfloat16),
             jax.ShapeDtypeStruct((2 * documents + 2,), jnp.int32),
             jax.ShapeDtypeStruct((1,), jnp.int32),
         ],
-        in_specs=[pl.BlockSpec(operand.shape, lambda i: (0, 0)) for operand in operands],
-        out_specs=[vmem, vmem, smem, smem],
+        in_specs=[vmem] * 3,
+        out_specs=[vmem, smem, smem],
         scratch_shapes=[pltpu.VMEM((2 * tok, head), jnp.float32)],
         compiler_params=limits,
-    )(*operands)
-    second = ahead(pair, 2)
-    fourth = ahead(pair, 4)
-    sixth = ahead(pair, 6)
-    shards, own, second, fourth, sixth = lax.optimization_barrier(
-        (shards, own, second, fourth, sixth)
-    )
-    eighth = ahead(own, 8)
-
-    def cached_rows(turns, shards, starts):
-        rows = len(turns) * shard_rows
-        packed = pl.pallas_call(
-            functools.partial(pack_cache_kernel, turns=turns, tok=tok),
-            out_shape=jax.ShapeDtypeStruct((blk_count, rows, 2 * head), jnp.bfloat16),
-            in_specs=[smem, smem, vmem],
-            out_specs=vmem,
-            compiler_params=limits,
-        )(place, starts, shards)
-        return lax.all_to_all(packed, "blk", split_axis=0, concat_axis=0)
-
-    arrived = cached_rows(range(turns[0]), shards, starts)
-    state = jax.ShapeDtypeStruct((heads, tok, head), jnp.float32)
-    states = pl.pallas_call(
-        new_kernel,
-        out_shape=[state] * 3,
-        in_specs=[smem] * 2 + [vmem] * 5,
-        out_specs=[vmem] * 3,
-        scratch_shapes=[
-            pltpu.VMEM((blk_count * tok, 2 * head), jnp.bfloat16),
-            pltpu.VMEM((blk_count, heads, tok, tok), jnp.float32),
-        ],
-        compiler_params=limits,
-        cost_estimate=pl.CostEstimate(
-            flops=4 * heads * tok * tok * head * blk_count,
-            bytes_accessed=8 * tok * width,
-            transcendentals=heads * tok * tok * blk_count,
-        ),
-    )(place, starts, queries[:, 0], pair, second, fourth, sixth)
-
-    def attend(rounds):
-        def run(shards, eighth, arrived, starts, cache_len, queries, states):
-            if rounds > turns[0]:
-                more = cached_rows(range(turns[0], rounds), shards, starts)
-                arrived = jnp.concatenate([arrived, more], axis=1)
+    )(new_raw, new_doc.reshape(-1, tok), cache_doc.reshape(-1, 128))
+
+    def exchange(rounds):
+        def run(shards, own, raw_behind, starts, cache_len, queries):
+            rows = rounds * shard_rows + tok
+            packed, behind = pl.pallas_call(
+                functools.partial(pack_kernel, rounds=rounds),
+                out_shape=[
+                    jax.ShapeDtypeStruct((blk_count, rows, 2 * head), jnp.bfloat16),
+                    jax.ShapeDtypeStruct((tok, 2 * head), jnp.bfloat16),
+                ],
+                in_specs=[smem, smem, vmem, vmem, vmem],
+                out_specs=[vmem, vmem],
+                scratch_shapes=[pltpu.VMEM((2 * tok, head), jnp.float32)],
+                compiler_params=limits,
+            )(place, starts, shards, own, raw_behind)
+            arrived = lax.all_to_all(packed, "blk", split_axis=0, concat_axis=0)
             span = pieces * shard_rows
             tiles = rounds * blk_count // pieces
             return pl.pallas_call(
-                functools.partial(cache_kernel, shard_rows=shard_rows, rounds=rounds),
+                functools.partial(attention_kernel, shard_rows=shard_rows, rounds=rounds),
                 out_shape=jax.ShapeDtypeStruct((tok, width), jnp.bfloat16),
-                in_specs=[smem] * 3 + [vmem] * 6,
+                in_specs=[smem, smem, smem, vmem, vmem, vmem],
                 out_specs=vmem,
                 scratch_shapes=[
+                    pltpu.VMEM((blk_count // 2, heads, tok, 2 * tok), jnp.float32),
+                    pltpu.VMEM((1, heads, tok, tok), jnp.float32),
                     pltpu.VMEM((tiles, heads, tok, span), jnp.float32),
-                    pltpu.VMEM((1, heads, tok, tok), jnp.float32),
                     pltpu.VMEM((heads, tok, head), jnp.float32),
                     pltpu.VMEM((heads, tok, head), jnp.float32),
                     pltpu.VMEM((heads, tok, head), jnp.float32),
                 ],
                 compiler_params=limits,
-            )(place, starts, cache_len, queries, eighth, arrived, *states)
+            )(place, starts, cache_len, queries, arrived, behind)
 
         return run
 
     attended = lax.switch(
         pick[0],
-        [attend(turn) for turn in turns],
+        [exchange(turn) for turn in turns],
         shards,
-        eighth,
-        arrived,
+        own,
+        raw_behind,
         starts,
         cache_len,
         queries[:, 0],
-        states,
     )
     share = tok // head_count
     moved = lax.all_to_all(

time: 79.6 us -> 67.1 us (0.84)
  the two profiles are of different devices: /device:TPU:1 before, /device:TPU:48 now
where the time goes in v2:
time: 67.1 us; the launch traced here: 66.5 us
  blocking collectives  38.4 us (57%)
  starting transfers between devices  10.7 us (16%)
  Pallas kernels  10.3 us (15%)
  waiting for transfers between devices  3.18 us (5%)
  local copies, waits for them, and re-layouts  3.16 us (5%)
    all_to_all x1, blocking collectives, local(): lax.all_to_all(attended.reshape(head_count, share, width), 'head', split_...  20.6 us
    all_to_all x1, blocking collectives, run(): arrived = lax.all_to_all(packed, 'blk', split_axis=0, concat_axis=0)  17.8 us
    all_to_all x1, starting transfers between devices, local(): shards = lax.all_to_all(spread, 'cp', split_axis=0, concat_axis=0)  8.6 us
    pallas_call x1, Pallas kernels, run(): pl.pallas_call(functools.partial(attention_kernel, shard_rows=shard_rows,...  6.98 us
    ppermute x1, waiting for transfers between devices, local(): lax.ppermute(new_raw, 'cp', [(i, (i + 1) % cp_count) for i in range(cp_co...  3.18 us
    unnamed x6, local copies, waits for them, and re-layouts  2.31 us
    ppermute x1, starting transfers between devices, local(): lax.ppermute(new_raw, 'cp', [(i, (i + 1) % cp_count) for i in range(cp_co...  2.05 us
    pallas_call x1, Pallas kernels, local(): pl.pallas_call(spread_kernel, out_shape=jax.ShapeDtypeStruct((cp_count, s...  1.49 us
  transfers between devices with their start and end apart: 2, of which 1 were waited for; matrix products, arithmetic and copies ran while one was open for 0% of the time, Pallas kernels for 1%

profile of v2, /device:TPU:48, one launch (start us, length us, event | category | flops | bytes accessed | tf_op | source)
XLA Modules:
  0.0 66.5 jit_solution(14027516294874133226)
XLA Ops:
  0.0 1.5 %shard_map.65 = bf16[8,64,256]{2,1,0:T(8,128)(2,1)} custom-call(bf16[128,128]{1,0:T(8,128)(2,1)} %bitcast.19), custom_call_target="tpu_custom_call" | custom-call | tf_op jit(solution)/shard_map/pallas_call | solution.py:310
  1.5 8.6 %all-to-all-start.3 = ((bf16[8,64,256]{2,1,0:T(8,128)(2,1)}), bf16[8,64,256]{2,1,0:T(8,128)(2,1)S(1)}, u32[]{:S(2)}, u32[]{:S(2)}) async-start(bf16[8,64,256]{2,1,0:T(8,128)(2,1)} %shard_map.65), calls=%async_computation.3 | async-start | bytes 524288 | tf_op jit(solution)/shard_map/all_to_all | solution.py:318
  10.1 2.0 %collective-permute-start = (bf16[256,128]{1,0:T(8,128)(2,1)}, bf16[256,128]{1,0:T(8,128)(2,1)S(1)}, u32[]{:S(2)}, u32[]{:S(2)}) collective-permute-start(bf16[256,128]{1,0:T(8,128)(2,1)} %bitcast.10), channel_id=1, source_target_pairs={{0,64},{64,128},{128,192},{192,256},{256,320},{320,384},{384,448},... | collective-permute-start | bytes 196616 | tf_op jit(solution)/shard_map/ppermute | solution.py:319
  12.2 0.0 copy-start
  12.2 0.8 %copy-done = bf16[128,1,2,128]{3,2,1,0:T(2,128)(2,1)S(1)} copy-done((bf16[128,1,2,128]{3,2,1,0:T(2,128)(2,1)S(1)}, bf16[128,1,2,128]{3,2,1,0:T(2,128)(2,1)}, u32[]{:S(2)}) %copy-start) | copy-done | bytes 65560
  13.0 0.0 copy-start.1
  13.0 0.8 %copy-done.1 = s32[8192]{0:T(1024)S(1)} copy-done((s32[8192]{0:T(1024)S(1)}, s32[8192]{0:T(1024)}, u32[]{:S(2)}) %copy-start.1) | copy-done | bytes 32792
  13.8 0.0 copy-start.2
  13.8 0.7 %copy-done.2 = s32[4096]{0:T(1024)S(1)} copy-done((s32[4096]{0:T(1024)S(1)}, s32[4096]{0:T(1024)}, u32[]{:S(2)}) %copy-start.2) | copy-done | bytes 16408
  14.5 0.9 %shard_map.64 = (bf16[128,256]{1,0:T(8,128)(2,1)S(1)}, s32[34]{0:T(128)S(1)}, s32[1]{0:T(128)}) custom-call(bf16[256,128]{1,0:T(8,128)(2,1)S(1)} %bitcast.11, s32[64,128]{1,0:T(8,128)S(1)} %bitcast.12, s32[32,128]{1,0:T(8,128)S(1)} %bitcast.13), custom_call_target="tpu_custom_call" | custom-call | tf_op jit(solution)/shard_map/pallas_call | solution.py:320
  16.0 0.1 pad_add_fusion
  16.1 3.2 %collective-permute-done = bf16[256,128]{1,0:T(8,128)(2,1)S(1)} collective-permute-done((bf16[256,128]{1,0:T(8,128)(2,1)}, bf16[256,128]{1,0:T(8,128)(2,1)S(1)}, u32[]{:S(2)}, u32[]{:S(2)}) %collective-permute-start) | collective-permute-done | bytes 65568 | tf_op jit(solution)/shard_map/ppermute | solution.py:319
  19.3 0.0 all-to-all-done.3
  19.3 25.8 %conditional.1 = (bf16[128,1024]{1,0:T(8,128)(2,1)S(1)}) conditional(s32[]{:T(128)} %bitcast.3, (s32[2]{0:T(128)S(1)}, s32[34]{0:T(128)S(1)}, bf16[8,64,256]{2,1,0:T(8,128)(2,1)S(1)}, bf16[128,256]{1,0:T(8,128)(2,1)S(1)}, bf16[256,128]{1,0:T(8,128)(2,1)S(1)}, /*index=5*/s32[64]{0:T(128)}, bf16[128,1024]{1,0:T(8,128)(2,1)}) %tuple.18, ...), branch_computations={%region_0.0_spmd, %region_1.0_spmd, %region_2.0_spmd} | conditional | bytes 6292544 | solution.py:368
  19.3 0.0 copy-start.3
  19.3 0.9 %branch_0_fun.2 = (bf16[8,256,256]{2,1,0:T(8,128)(2,1)S(1)}, bf16[128,256]{1,0:T(8,128)(2,1)S(1)}) custom-call(s32[2]{0:T(128)S(1)} %get-tuple-element.50.place_ref, s32[34]{0:T(128)S(1)} %get-tuple-element.52.starts_ref, bf16[8,64,256]{2,1,0:T(8,128)(2,1)S(1)} %get-tuple-element.55.shards_ref, bf16[128,256]{1,0:T(8,128)(2,1)S(1)} %get-tuple-element.56.own_ref, ...), custom_call_target="tpu_custom_call" | custom-call | tf_op jit(solution)/shard_map/cond/branch_0_fun/pallas_call | solution.py:336
  20.2 17.8 %all_to_all.22.arrived_ref = bf16[8,256,256]{2,1,0:T(8,128)(2,1)S(1)} all-to-all(bf16[8,256,256]{2,1,0:T(8,128)(2,1)S(1)} %get-tuple-element.58), channel_id=1, replica_groups=mesh['cp'=8,'blk'=8,'head'=8] {'blk'}, dimensions={0} | all-to-all | bytes 2097152 | tf_op jit(solution)/shard_map/cond/branch_0_fun/all_to_all | solution.py:347
  38.1 0.0 copy-done.3
  38.1 7.0 %branch_0_fun.3 = bf16[128,1024]{1,0:T(8,128)(2,1)S(1)} custom-call(s32[2]{0:T(128)S(1)} %get-tuple-element.50.place_ref, s32[34]{0:T(128)S(1)} %get-tuple-element.52.starts_ref, s32[64]{0:T(128)} %get-tuple-element.53.cache_len_ref, bf16[128,1024]{1,0:T(8,128)(2,1)S(1)} %copy-done.3, bf16[8,256,256]{2,1,0:T(8,128)(2,1)S(1)} %all_to_all.22.arrived_ref, ...), custom_call_target="tpu_custom_call" | custom-call | tf_op jit(solution)/shard_map/cond/branch_0_fun/pallas_call | solution.py:350
  45.1 20.6 %all_to_all.25 = bf16[8,16,1024]{2,1,0:T(8,128)(2,1)S(1)} all-to-all(bf16[8,16,1024]{2,1,0:T(8,128)(2,1)S(1)} %bitcast.18), channel_id=1, replica_groups=mesh['cp'=8,'blk'=8,'head'=8] {'head'}, dimensions={0} | all-to-all | bytes 524288 | tf_op jit(solution)/shard_map/all_to_all | solution.py:379
  65.7 0.9 %copy.7 = bf16[16,8,1024]{2,1,0:T(8,128)(2,1)} copy(bf16[16,8,1024]{2,0,1:T(8,128)(2,1)S(1)} %bitcast.17) | data formatting | bytes 524288 | tf_op jit(solution)/shard_map/transpose | solution.py:382
Async XLA Ops:
  1.5 17.8 %all-to-all-start.3 = ((bf16[8,64,256]{2,1,0:T(8,128)(2,1)}), bf16[8,64,256]{2,1,0:T(8,128)(2,1)S(1)}, u32[]{:S(2)}, u32[]{:S(2)}) async-start(bf16[8,64,256]{2,1,0:T(8,128)(2,1)} %shard_map.65), calls=%async_computation.3 | async-start | bytes 524288 | tf_op jit(solution)/shard_map/all_to_all | solution.py:318
  10.1 9.2 %collective-permute-start = (bf16[256,128]{1,0:T(8,128)(2,1)}, bf16[256,128]{1,0:T(8,128)(2,1)S(1)}, u32[]{:S(2)}, u32[]{:S(2)}) collective-permute-start(bf16[256,128]{1,0:T(8,128)(2,1)} %bitcast.10), channel_id=1, source_target_pairs={{0,64},{64,128},{128,192},{192,256},{256,320},{320,384},{384,448},... | collective-permute-start | bytes 196616 | tf_op jit(solution)/shard_map/ppermute | solution.py:319
  12.2 0.8 %copy-start = (bf16[128,1,2,128]{3,2,1,0:T(2,128)(2,1)S(1)}, bf16[128,1,2,128]{3,2,1,0:T(2,128)(2,1)}, u32[]{:S(2)}) copy-start(bf16[128,1,2,128]{3,2,1,0:T(2,128)(2,1)} %param.10) | copy-start | bytes 196612
  13.0 0.8 %copy-start.1 = (s32[8192]{0:T(1024)S(1)}, s32[8192]{0:T(1024)}, u32[]{:S(2)}) copy-start(s32[8192]{0:T(1024)} %param.12) | copy-start | bytes 98308
  13.8 0.7 %copy-start.2 = (s32[4096]{0:T(1024)S(1)}, s32[4096]{0:T(1024)}, u32[]{:S(2)}) copy-start(s32[4096]{0:T(1024)} %param.13) | copy-start | bytes 49156
  19.3 18.8 %copy-start.3 = (bf16[128,1024]{1,0:T(8,128)(2,1)S(1)}, bf16[128,1024]{1,0:T(8,128)(2,1)}, u32[]{:S(2)}) copy-start(bf16[128,1024]{1,0:T(8,128)(2,1)} %get-tuple-element.54.queries_ref) | copy-start | bytes 786436 | tf_op jit(solution)/shard_map/cond

commit v3 on v2

--- a/solution.py
+++ b/solution.py
@@ -10,6 +10,7 @@
 
 negative = -1e30
 documents = 16
+block_at, new_low_at, cache_low_at, cache_high_at, target_low_at = 0, 1, 2, 3, 4
 longest = 1024
 head = 128
 pieces = 4
@@ -17,7 +18,6 @@
 vmem = pl.BlockSpec(memory_space=pltpu.VMEM)
 exponent_scale = math.log2(math.e) * head**-0.5
 limits = pltpu.CompilerParams(vmem_limit_bytes=44 * 1024 * 1024)
-large = pltpu.CompilerParams(vmem_limit_bytes=56 * 1024 * 1024)
 
 
 def split_pairs(raw, wide, rows):
@@ -33,27 +33,73 @@
         spread_ref[target] = shard
 
 
+def table_places(count):
+    new_starts = target_low_at + count
+    cache_starts = new_starts + documents + 1
+    return new_starts, cache_starts, cache_starts + documents + 1
+
+
 def prepare_kernel(
-    new_ref, new_doc_ref, cache_doc_ref, own_ref, starts_ref, pick_ref, wide, *, turns, period
+    place_ref,
+    cache_len_ref,
+    new_ref,
+    new_doc_ref,
+    cache_doc_ref,
+    own_ref,
+    table_ref,
+    pick_ref,
+    wide,
+    *,
+    turns,
+    period,
+    count,
 ):
-    own_ref[...] = split_pairs(new_ref[...], wide, own_ref.shape[0])
+    tok = own_ref.shape[0]
+    new_starts, cache_starts, lengths = table_places(count)
+    own_ref[...] = split_pairs(new_ref[...], wide, tok)
     new_doc = new_doc_ref[...]
     cache_doc = cache_doc_ref[...]
     first_doc = new_doc[:, :1]
     last_doc = new_doc[:, -1:]
     low = jnp.zeros(first_doc.shape, jnp.float32)
     high = jnp.full(first_doc.shape, float(cache_doc.size), jnp.float32)
-    starts_ref[0] = 0
-    starts_ref[documents + 1] = 0
+    new_at = [jnp.int32(0)]
+    cache_at = [jnp.int32(0)]
     for doc in range(1, documents):
         before = jnp.sum((new_doc < doc).astype(jnp.float32))
-        starts_ref[doc] = before.astype(jnp.int32)
+        new_at.append(before.astype(jnp.int32))
         before = jnp.sum((cache_doc < doc).astype(jnp.float32))
-        starts_ref[documents + 1 + doc] = before.astype(jnp.int32)
+        cache_at.append(before.astype(jnp.int32))
         low = jnp.where(first_doc == doc, before, low)
         high = jnp.where(last_doc == doc - 1, before, high)
-    starts_ref[documents] = new_doc.size
-    starts_ref[2 * documents + 1] = cache_doc.size
+    new_at.append(jnp.int32(new_doc.size))
+    cache_at.append(jnp.int32(cache_doc.size))
+    for doc in range(documents + 1):
+        table_ref[new_starts + doc] = new_at[doc]
+        table_ref[cache_starts + doc] = cache_at[doc]
+    for shard in range(cache_len_ref.shape[0]):
+        table_ref[lengths + shard] = cache_len_ref[shard]
+
+    def cache_start(place):
+        found = jnp.int32(0)
+        for doc in range(1, documents):
+            found = jnp.where(place >= new_at[doc], cache_at[doc], found)
+        return found
+
+    block = place_ref[0]
+    first = block * tok
+    group_first = block // count * count * tok
+    new_low = jnp.int32(0)
+    cache_high = cache_at[1]
+    for doc in range(1, documents):
+        new_low = jnp.where(first >= new_at[doc], new_at[doc], new_low)
+        cache_high = jnp.where(first + tok - 1 >= new_at[doc], cache_at[doc + 1], cache_high)
+    table_ref[block_at] = block
+    table_ref[new_low_at] = new_low
+    table_ref[cache_low_at] = cache_start(first)
+    table_ref[cache_high_at] = cache_high
+    for target in range(count):
+        table_ref[target_low_at + target] = cache_start(group_first + target * tok)
     widest = jnp.max(high - low).astype(jnp.int32)
     pick = jnp.int32(0)
     for turn in turns[:-1]:
@@ -62,21 +108,17 @@
 
 
 def pack_kernel(
-    place_ref, starts_ref, shards_ref, own_ref, raw_ref, out_ref, behind_ref, wide, *, rounds
+    table_ref, shards_ref, own_ref, raw_ref, out_ref, behind_ref, wide, *, rounds
 ):
     groups, shard_rows, _ = shards_ref.shape
     count = out_ref.shape[0]
     tok = own_ref.shape[0]
     period = count * shard_rows
-    cp_index = place_ref[0]
-    blk_index = place_ref[1]
+    blk_index = table_ref[block_at] % count
     behind_ref[...] = split_pairs(raw_ref[...], wide, tok)
     row = lax.broadcasted_iota(jnp.int32, (shard_rows, 1), 0)
     for target in range(count):
-        first = (cp_index * count + target) * tok
-        low = jnp.int32(0)
-        for doc in range(1, documents):
-            low = jnp.where(first >= starts_ref[doc], starts_ref[documents + 1 + doc], low)
+        low = table_ref[target_low_at + target]
         reached = low - blk_index * shard_rows
         group = (reached - (shard_rows - 1) + period - 1) // period
         cut = reached - group * period
@@ -101,31 +143,19 @@
             out_ref[target, rounds * shard_rows :] = behind_ref[...]
 
 
-def row_bounds(starts_ref, first, tok):
+def row_bounds(table_ref, count, first, tok):
+    new_starts, cache_starts, _ = table_places(count)
     row_place = first + lax.broadcasted_iota(jnp.int32, (tok, 1), 0)
     row_start = jnp.zeros((tok, 1), jnp.int32)
     row_low = jnp.zeros((tok, 1), jnp.int32)
-    row_high = jnp.full((tok, 1), starts_ref[documents + 2], jnp.int32)
+    row_high = jnp.full((tok, 1), table_ref[cache_starts + 1], jnp.int32)
     for doc in range(1, documents):
-        reached = row_place >= starts_ref[doc]
-        row_start = jnp.where(reached, starts_ref[doc], row_start)
-        row_low = jnp.where(reached, starts_ref[documents + 1 + doc], row_low)
-        row_high = jnp.where(reached, starts_ref[documents + 2 + doc], row_high)
+        start = table_ref[new_starts + doc]
+        reached = row_place >= start
+        row_start = jnp.where(reached, start, row_start)
+        row_low = jnp.where(reached, table_ref[cache_starts + doc], row_low)
+        row_high = jnp.where(reached, table_ref[cache_starts + doc + 1], row_high)
     return row_place, row_start, row_low, row_high
-
-
-def block_bounds(starts_ref, first, tok):
-    new_low = jnp.int32(0)
-    cache_low = jnp.int32(0)
-    cache_high = starts_ref[documents + 2]
-    for doc in range(1, documents):
-        start = starts_ref[doc]
-        new_low = jnp.where(first >= start, start, new_low)
-        cache_low = jnp.where(first >= start, starts_ref[documents + 1 + doc], cache_low)
-        cache_high = jnp.where(
-            first + tok - 1 >= start, starts_ref[documents + 2 + doc], cache_high
-        )
-    return new_low, cache_low, cache_high
 
 
 def score(queries_ref, keys, allowed, scores_ref, at, lane_max):
@@ -167,9 +197,7 @@
 
 
 def attention_kernel(
-    place_ref,
-    starts_ref,
-    cache_len_ref,
+    table_ref,
     queries_ref,
     arrived_ref,
     behind_ref,
@@ -183,23 +211,24 @@
     *,
     shard_rows,
     rounds,
+    shards,
 ):
     tok = queries_ref.shape[0]
     heads = lane_max.shape[0]
     count = arrived_ref.shape[0]
-    shards = cache_len_ref.shape[0]
+    lengths = table_places(count)[2]
     period = count * shard_rows
     span = pieces * shard_rows
     new_offset = rounds * shard_rows
-    block = place_ref[0] * count + place_ref[1]
-    first = block * tok
-    row_place, row_start, row_low, row_high = row_bounds(starts_ref, first, tok)
-    new_low, cache_low, cache_high = block_bounds(starts_ref, first, tok)
+    block = table_ref[block_at]
+    cache_low = table_ref[cache_low_at]
+    cache_high = table_ref[cache_high_at]
+    row_place, row_start, row_low, row_high = row_bounds(table_ref, count, block * tok, tok)
     lane_max[...] = jnp.full(lane_max.shape, negative, jnp.float32)
     lane_sum[...] = jnp.zeros(lane_sum.shape, jnp.float32)
     total[...] = jnp.zeros(total.shape, jnp.float32)
     farthest = block - count
-    first_block = new_low // tok
+    first_block = table_ref[new_low_at] // tok
     new_tiles = jnp.minimum((block - first_block) // 2 + 1, count // 2)
     reaches = first_block <= farthest
 
@@ -262,7 +291,7 @@
                 for at in (0, shard_rows - 1):
                     where = base + jnp.bitwise_and(edge + at - base, period - 1)
                     where = where // shard_rows
-                    length = cache_len_ref[jnp.minimum(where, shards - 1)]
+                    length = table_ref[lengths + jnp.minimum(where, shards - 1)]
                     filled = jnp.where(shard == where, length, filled)
             usable = jnp.bitwise_and(place, shard_rows - 1) < filled
             allowed = (place >= row_low) & (place < row_high) & usable
@@ -302,7 +331,8 @@
     cp_count = lax.axis_size("cp")
     head_count = lax.axis_size("head")
     assert tok * blk_count >= longest
-    place = jnp.stack([lax.axis_index("cp"), lax.axis_index("blk")]).astype(jnp.int32)
+    shard_count = cache_len.shape[0]
+    place = lax.axis_index(("cp", "blk")).astype(jnp.int32)[None]
     period = blk_count * shard_rows
     turns = [2, 3, cp_count]
     new_raw = new_kv.reshape(2 * tok, head)
@@ -313,25 +343,25 @@
         in_specs=[vmem],
         out_specs=vmem,
         scratch_shapes=[pltpu.VMEM((2 * shard_rows, head), jnp.float32)],
-        compiler_params=large,
+        compiler_params=limits,
     )(cache_raw)
     shards = lax.all_to_all(spread, "cp", split_axis=0, concat_axis=0)
     raw_behind = lax.ppermute(new_raw, "cp", [(i, (i + 1) % cp_count) for i in range(cp_count)])
-    own, starts, pick = pl.pallas_call(
-        functools.partial(prepare_kernel, turns=turns, period=period),
+    own, table, pick = pl.pallas_call(
+        functools.partial(prepare_kernel, turns=turns, period=period, count=blk_count),
         out_shape=[
             jax.ShapeDtypeStruct((tok, 2 * head), jnp.bfloat16),
-            jax.ShapeDtypeStruct((2 * documents + 2,), jnp.int32),
+            jax.ShapeDtypeStruct((table_places(blk_count)[2] + shard_count,), jnp.int32),
             jax.ShapeDtypeStruct((1,), jnp.int32),
         ],
-        in_specs=[vmem] * 3,
+        in_specs=[smem] * 2 + [vmem] * 3,
         out_specs=[vmem, smem, smem],
         scratch_shapes=[pltpu.VMEM((2 * tok, head), jnp.float32)],
         compiler_params=limits,
-    )(new_raw, new_doc.reshape(-1, tok), cache_doc.reshape(-1, 128))
+    )(place, cache_len, new_raw, new_doc.reshape(-1, tok), cache_doc.reshape(-1, 128))
 
     def exchange(rounds):
-        def run(shards, own, raw_behind, starts, cache_len, queries):
+        def run(shards, own, raw_behind, table, queries):
             rows = rounds * shard_rows + tok
             packed, behind = pl.pallas_call(
                 functools.partial(pack_kernel, rounds=rounds),
@@ -339,18 +369,20 @@
                     jax.ShapeDtypeStruct((blk_count, rows, 2 * head), jnp.bfloat16),
                     jax.ShapeDtypeStruct((tok, 2 * head), jnp.bfloat16),
                 ],
-                in_specs=[smem, smem, vmem, vmem, vmem],
+                in_specs=[smem, vmem, vmem, vmem],
                 out_specs=[vmem, vmem],
                 scratch_shapes=[pltpu.VMEM((2 * tok, head), jnp.float32)],
                 compiler_params=limits,
-            )(place, starts, shards, own, raw_behind)
+            )(table, shards, own, raw_behind)
             arrived = lax.all_to_all(packed, "blk", split_axis=0, concat_axis=0)
             span = pieces * shard_rows
             tiles = rounds * blk_count // pieces
             return pl.pallas_call(
-                functools.partial(attention_kernel, shard_rows=shard_rows, rounds=rounds),
+                functools.partial(
+                    attention_kernel, shard_rows=shard_rows, rounds=rounds, shards=shard_count
+                ),
                 out_shape=jax.ShapeDtypeStruct((tok, width), jnp.bfloat16),
-                in_specs=[smem, smem, smem, vmem, vmem, vmem],
+                in_specs=[smem, vmem, vmem, vmem],
                 out_specs=vmem,
                 scratch_shapes=[
                     pltpu.VMEM((blk_count // 2, heads, tok, 2 * tok), jnp.float32),
@@ -361,7 +393,7 @@
                     pltpu.VMEM((heads, tok, head), jnp.float32),
                 ],
                 compiler_params=limits,
-            )(place, starts, cache_len, queries, arrived, behind)
+            )(table, queries, arrived, behind)
 
         return run
 
@@ -371,8 +403,7 @@
         shards,
         own,
         raw_behind,
-        starts,
-        cache_len,
+        table,
         queries[:, 0],
     )
     share = tok // head_count

time: 67.1 us -> 67.8 us (1.010)
  the two profiles are of different devices: /device:TPU:48 before, /device:TPU:16 now
where the time goes in v3:
time: 67.8 us; the launch traced here: 67.2 us
  blocking collectives  40.9 us (60%)
  starting transfers between devices  11.1 us (16%)
  Pallas kernels  8.15 us (12%)
  local copies, waits for them, and re-layouts  4.58 us (7%)
  waiting for transfers between devices  1.72 us (3%)
  between operations  0.73 us (1%)
    all_to_all x1, blocking collectives, local(): lax.all_to_all(attended.reshape(head_count, share, width), 'head', split_...  20.5 us
    all_to_all x1, blocking collectives, run(): arrived = lax.all_to_all(packed, 'blk', split_axis=0, concat_axis=0)  20.4 us
    all_to_all x1, starting transfers between devices, local(): shards = lax.all_to_all(spread, 'cp', split_axis=0, concat_axis=0)  9.03 us
    pallas_call x1, Pallas kernels, run(): pl.pallas_call(functools.partial(attention_kernel, shard_rows=shard_rows,...  5.02 us
    unnamed x10, local copies, waits for them, and re-layouts  3.72 us
    ppermute x1, starting transfers between devices, local(): lax.ppermute(new_raw, 'cp', [(i, (i + 1) % cp_count) for i in range(cp_co...  2.05 us
    pallas_call x1, Pallas kernels, local(): pl.pallas_call(functools.partial(prepare_kernel, turns=turns, period=peri...  1.58 us
    all_to_all x1, waiting for transfers between devices, local(): shards = lax.all_to_all(spread, 'cp', split_axis=0, concat_axis=0)  1.47 us
  transfers between devices with their start and end apart: 2, of which 2 were waited for; matrix products, arithmetic and copies ran while one was open for 0% of the time, Pallas kernels for 2%

profile of v3, /device:TPU:16, one launch (start us, length us, event | category | flops | bytes accessed | tf_op | source)
XLA Modules:
  0.0 67.2 jit_solution(14929142450829764289)
XLA Ops:
  0.0 0.0 copy-start.1
  0.0 0.8 %copy-done.1 = bf16[64,1,2,128]{3,2,1,0:T(2,128)(2,1)S(1)} copy-done((bf16[64,1,2,128]{3,2,1,0:T(2,128)(2,1)S(1)}, bf16[64,1,2,128]{3,2,1,0:T(2,128)(2,1)}, u32[]{:S(2)}) %copy-start.1) | copy-done | bytes 32792
  0.8 0.7 %shard_map.65 = bf16[8,64,256]{2,1,0:T(8,128)(2,1)} custom-call(bf16[128,128]{1,0:T(8,128)(2,1)S(1)} %bitcast.11), custom_call_target="tpu_custom_call" | custom-call | tf_op jit(solution)/shard_map/pallas_call | solution.py:340
  1.5 9.0 %all-to-all-start.3 = ((bf16[8,64,256]{2,1,0:T(8,128)(2,1)}), bf16[8,64,256]{2,1,0:T(8,128)(2,1)S(1)}, u32[]{:S(2)}, u32[]{:S(2)}) async-start(bf16[8,64,256]{2,1,0:T(8,128)(2,1)} %shard_map.65), calls=%async_computation.3 | async-start | bytes 524288 | tf_op jit(solution)/shard_map/all_to_all | solution.py:348
  10.5 2.0 %collective-permute-start = (bf16[256,128]{1,0:T(8,128)(2,1)}, bf16[256,128]{1,0:T(8,128)(2,1)S(1)}, u32[]{:S(2)}, u32[]{:S(2)}) collective-permute-start(bf16[256,128]{1,0:T(8,128)(2,1)} %bitcast.9), channel_id=1, source_target_pairs={{0,64},{64,128},{128,192},{192,256},{256,320},{320,384},{384,448},... | collective-permute-start | bytes 196616 | tf_op jit(solution)/shard_map/ppermute | solution.py:349
  12.6 0.0 copy-start
  12.6 0.8 %copy-done = bf16[128,1,2,128]{3,2,1,0:T(2,128)(2,1)S(1)} copy-done((bf16[128,1,2,128]{3,2,1,0:T(2,128)(2,1)S(1)}, bf16[128,1,2,128]{3,2,1,0:T(2,128)(2,1)}, u32[]{:S(2)}) %copy-start) | copy-done | bytes 65560
  13.4 0.0 copy-start.2
  13.4 0.8 %copy-done.2 = s32[8192]{0:T(1024)S(1)} copy-done((s32[8192]{0:T(1024)S(1)}, s32[8192]{0:T(1024)}, u32[]{:S(2)}) %copy-start.2) | copy-done | bytes 32792
  14.2 0.0 copy-start.3
  14.2 0.7 %copy-done.3 = s32[4096]{0:T(1024)S(1)} copy-done((s32[4096]{0:T(1024)S(1)}, s32[4096]{0:T(1024)}, u32[]{:S(2)}) %copy-start.3) | copy-done | bytes 16408
  14.9 0.0 copy-start.4
  14.9 0.7 copy-done.4
  15.6 1.6 %shard_map.64 = (bf16[128,256]{1,0:T(8,128)(2,1)S(1)}, s32[110]{0:T(128)S(1)}, s32[1]{0:T(128)}) custom-call(s32[1]{0:T(128)} %bitcast.place_ref, s32[64]{0:T(128)S(1)} %copy-done.4, bf16[256,128]{1,0:T(8,128)(2,1)S(1)} %bitcast.10, s32[64,128]{1,0:T(8,128)S(1)} %bitcast.12, s32[32,128]{1,0:T(8,128)S(1)} %bitcast.13), custom_call_target="tpu_custom_call" | custom-call | tf_op jit(solution)/shard_map/pallas_call | solution.py:350
  17.8 0.2 collective-permute-done
  18.1 1.5 %all-to-all-done.3 = bf16[8,64,256]{2,1,0:T(8,128)(2,1)S(1)} async-done(((bf16[8,64,256]{2,1,0:T(8,128)(2,1)}), bf16[8,64,256]{2,1,0:T(8,128)(2,1)S(1)}, u32[]{:S(2)}, u32[]{:S(2)}) %all-to-all-start.3) | async-done | bytes 262176 | tf_op jit(solution)/shard_map/all_to_all | solution.py:348
  19.6 26.3 %conditional.1 = (bf16[128,1024]{1,0:T(8,128)(2,1)S(1)}) conditional(s32[]{:T(128)} %bitcast.4, (s32[110]{0:T(128)S(1)}, bf16[8,64,256]{2,1,0:T(8,128)(2,1)S(1)}, bf16[128,256]{1,0:T(8,128)(2,1)S(1)}, bf16[256,128]{1,0:T(8,128)(2,1)S(1)}, bf16[128,1024]{1,0:T(8,128)(2,1)}) %tuple.18, (s32[110]{0:T(128)S(1)}, ...), branch_computations={%region_0.0_spmd, %region_1.0_spmd, %region_2.0_spmd} | conditional | bytes 6291492 | solution.py:400
  19.6 0.0 copy-start.5
  19.6 0.8 %branch_0_fun.2 = (bf16[8,256,256]{2,1,0:T(8,128)(2,1)S(1)}, bf16[128,256]{1,0:T(8,128)(2,1)S(1)}) custom-call(s32[110]{0:T(128)S(1)} %get-tuple-element.38.table_ref, bf16[8,64,256]{2,1,0:T(8,128)(2,1)S(1)} %get-tuple-element.41.shards_ref, bf16[128,256]{1,0:T(8,128)(2,1)S(1)} %get-tuple-element.42.own_ref, bf16[256,128]{1,0:T(8,128)(2,1)S(1)} %get-tuple-element.43.raw_ref), custom_call_target="tpu_custom_call" | custom-call | tf_op jit(solution)/shard_map/cond/branch_0_fun/pallas_call | solution.py:366
  20.4 20.4 %all_to_all.22.arrived_ref = bf16[8,256,256]{2,1,0:T(8,128)(2,1)S(1)} all-to-all(bf16[8,256,256]{2,1,0:T(8,128)(2,1)S(1)} %get-tuple-element.44), channel_id=1, replica_groups=mesh['cp'=8,'blk'=8,'head'=8] {'blk'}, dimensions={0} | all-to-all | bytes 2097152 | tf_op jit(solution)/shard_map/cond/branch_0_fun/all_to_all | solution.py:377
  40.8 0.0 copy-done.5
  40.8 5.0 %branch_0_fun.3 = bf16[128,1024]{1,0:T(8,128)(2,1)S(1)} custom-call(s32[110]{0:T(128)S(1)} %get-tuple-element.38.table_ref, bf16[128,1024]{1,0:T(8,128)(2,1)S(1)} %copy-done.5, bf16[8,256,256]{2,1,0:T(8,128)(2,1)S(1)} %all_to_all.22.arrived_ref, bf16[128,256]{1,0:T(8,128)(2,1)S(1)} %get-tuple-element.45.behind_ref), custom_call_target="tpu_custom_call" | custom-call | tf_op jit(solution)/shard_map/cond/branch_0_fun/pallas_call | solution.py:380
  45.9 20.5 %all_to_all.25 = bf16[8,16,1024]{2,1,0:T(8,128)(2,1)S(1)} all-to-all(bf16[8,16,1024]{2,1,0:T(8,128)(2,1)S(1)} %bitcast.18), channel_id=1, replica_groups=mesh['cp'=8,'blk'=8,'head'=8] {'head'}, dimensions={0} | all-to-all | bytes 524288 | tf_op jit(solution)/shard_map/all_to_all | solution.py:410
  66.4 0.9 %copy.7 = bf16[16,8,1024]{2,1,0:T(8,128)(2,1)} copy(bf16[16,8,1024]{2,0,1:T(8,128)(2,1)S(1)} %bitcast.17) | data formatting | bytes 524288 | tf_op jit(solution)/shard_map/transpose | solution.py:413
Async XLA Ops:
  0.0 0.8 %copy-start.1 = (bf16[64,1,2,128]{3,2,1,0:T(2,128)(2,1)S(1)}, bf16[64,1,2,128]{3,2,1,0:T(2,128)(2,1)}, u32[]{:S(2)}) copy-start(bf16[64,1,2,128]{3,2,1,0:T(2,128)(2,1)} %param.11) | copy-start | bytes 98308
  1.5 18.1 %all-to-all-start.3 = ((bf16[8,64,256]{2,1,0:T(8,128)(2,1)}), bf16[8,64,256]{2,1,0:T(8,128)(2,1)S(1)}, u32[]{:S(2)}, u32[]{:S(2)}) async-start(bf16[8,64,256]{2,1,0:T(8,128)(2,1)} %shard_map.65), calls=%async_computation.3 | async-start | bytes 524288 | tf_op jit(solution)/shard_map/all_to_all | solution.py:348
  10.5 7.6 %collective-permute-start = (bf16[256,128]{1,0:T(8,128)(2,1)}, bf16[256,128]{1,0:T(8,128)(2,1)S(1)}, u32[]{:S(2)}, u32[]{:S(2)}) collective-permute-start(bf16[256,128]{1,0:T(8,128)(2,1)} %bitcast.9), channel_id=1, source_target_pairs={{0,64},{64,128},{128,192},{192,256},{256,320},{320,384},{384,448},... | collective-permute-start | bytes 196616 | tf_op jit(solution)/shard_map/ppermute | solution.py:349
  12.6 0.8 %copy-start = (bf16[128,1,2,128]{3,2,1,0:T(2,128)(2,1)S(1)}, bf16[128,1,2,128]{3,2,1,0:T(2,128)(2,1)}, u32[]{:S(2)}) copy-start(bf16[128,1,2,128]{3,2,1,0:T(2,128)(2,1)} %param.10) | copy-start | bytes 196612
  13.4 0.8 %copy-start.2 = (s32[8192]{0:T(1024)S(1)}, s32[8192]{0:T(1024)}, u32[]{:S(2)}) copy-start(s32[8192]{0:T(1024)} %param.12) | copy-start | bytes 98308
  14.2 0.7 %copy-start.3 = (s32[4096]{0:T(1024)S(1)}, s32[4096]{0:T(1024)}, u32[]{:S(2)}) copy-start(s32[4096]{0:T(1024)} %param.13) | copy-start | bytes 49156
  14.9 0.7 copy-start.4
  19.6 21.3 %copy-start.5 = (bf16[128,1024]{1,0:T(8,128)(2,1)S(1)}, bf16[128,1024]{1,0:T(8,128)(2,1)}, u32[]{:S(2)}) copy-start(bf16[128,1024]{1,0:T(8,128)(2,1)} %get-tuple-element.40.queries_ref) | copy-start | bytes 786436 | tf_op jit(solution)/shard_map/cond

commit v4 on v3

--- a/solution.py
+++ b/solution.py
@@ -158,42 +158,43 @@
     return row_place, row_start, row_low, row_high
 
 
-def score(queries_ref, keys, allowed, scores_ref, at, lane_max):
-    for h in range(lane_max.shape[0]):
-        scores = lax.dot_general(
-            queries_ref[:, h * head : (h + 1) * head],
-            keys,
-            (((1,), (1,)), ((), ())),
-            preferred_element_type=jnp.float32,
-        )
-        scores = jnp.where(allowed, scores, negative)
-        scores_ref[at, h] = scores
-        best = scores[:, :head]
-        for part in range(1, scores.shape[1] // head):
-            best = jnp.maximum(best, scores[:, part * head : (part + 1) * head])
-        lane_max[h] = jnp.maximum(lane_max[h], best)
-
-
-def weigh(values, scores_ref, at, lane_max, lane_sum, total):
-    for h in range(lane_max.shape[0]):
-        scores = scores_ref[at, h]
-        best = lane_max[h]
-        added = lane_sum[h]
+def score(rows_ref, keys, allowed, scores_ref, at, lane_max):
+    tok = allowed.shape[0]
+    products = lax.dot_general(
+        rows_ref[...], keys, (((1,), (1,)), ((), ())), preferred_element_type=jnp.float32
+    )
+    for first in range(0, rows_ref.shape[0], tok):
+        rows = slice(first, first + tok)
+        scores = jnp.where(allowed, products[rows], negative)
+        scores_ref[at, rows] = scores
+        best = lane_max[rows]
+        for lane in range(0, scores.shape[1], head):
+            best = jnp.maximum(best, scores[:, lane : lane + head])
+        lane_max[rows] = best
+
+
+def weigh(values, scores_ref, at, lane_max, lane_sum, total, tok):
+    rounded = []
+    for first in range(0, total.shape[0], tok):
+        rows = slice(first, first + tok)
+        scores = scores_ref[at, rows]
+        best = lane_max[rows]
+        added = lane_sum[rows]
         parts = []
-        for part in range(scores.shape[1] // head):
-            piece = scores[:, part * head : (part + 1) * head]
-            weight = jnp.exp2((piece - best) * exponent_scale)
+        for lane in range(0, scores.shape[1], head):
+            weight = jnp.exp2((scores[:, lane : lane + head] - best) * exponent_scale)
             added = added + weight
             parts.append(weight.astype(jnp.bfloat16))
-        lane_sum[h] = added
-        rounded = parts[0] if len(parts) == 1 else jnp.concatenate(parts, axis=1)
-        total[h] += jnp.dot(rounded, values, preferred_element_type=jnp.float32)
+        lane_sum[rows] = added
+        rounded.append(parts[0] if len(parts) == 1 else jnp.concatenate(parts, axis=1))
+    total[...] += jnp.dot(
+        jnp.concatenate(rounded, axis=0), values, preferred_element_type=jnp.float32
+    )
 
 
 def settle(lane_max):
-    for h in range(lane_max.shape[0]):
-        best = jnp.max(lane_max[h], axis=1, keepdims=True)
-        lane_max[h] = jnp.broadcast_to(best, lane_max.shape[1:])
+    best = jnp.max(lane_max[...], axis=1, keepdims=True)
+    lane_max[...] = jnp.broadcast_to(best, lane_max.shape)
 
 
 def attention_kernel(
@@ -202,6 +203,7 @@
     arrived_ref,
     behind_ref,
     out_ref,
+    query_rows,
     new_scores,
     far_scores,
     cache_scores,
@@ -214,7 +216,7 @@
     shards,
 ):
     tok = queries_ref.shape[0]
-    heads = lane_max.shape[0]
+    heads = query_rows.shape[0] // tok
     count = arrived_ref.shape[0]
     lengths = table_places(count)[2]
     period = count * shard_rows
@@ -224,6 +226,8 @@
     cache_low = table_ref[cache_low_at]
     cache_high = table_ref[cache_high_at]
     row_place, row_start, row_low, row_high = row_bounds(table_ref, count, block * tok, tok)
+    for h in range(heads):
+        query_rows[h * tok : (h + 1) * tok] = queries_ref[:, h * head : (h + 1) * head]
     lane_max[...] = jnp.full(lane_max.shape, negative, jnp.float32)
     lane_sum[...] = jnp.zeros(lane_sum.shape, jnp.float32)
     total[...] = jnp.zeros(total.shape, jnp.float32)
@@ -249,12 +253,12 @@
     @pl.loop(0, new_tiles)
     def _(number):
         allowed = new_allowed((block - 2 * number - 1) * tok, 2 * tok)
-        score(queries_ref, new_part(number, 0), allowed, new_scores, number, lane_max)
+        score(query_rows, new_part(number, 0), allowed, new_scores, number, lane_max)
 
     @pl.when(reaches)
     def _():
         allowed = new_allowed(farthest * tok, tok)
-        score(queries_ref, behind_ref[:, :head], allowed, far_scores, 0, lane_max)
+        score(query_rows, behind_ref[:, :head], allowed, far_scores, 0, lane_max)
 
     def cache_tile(number):
         turn = number // (count // pieces)
@@ -296,17 +300,17 @@
             usable = jnp.bitwise_and(place, shard_rows - 1) < filled
             allowed = (place >= row_low) & (place < row_high) & usable
             keys = cache_part(turn, source, 0)
-            score(queries_ref, keys, allowed, cache_scores, number, lane_max)
+            score(query_rows, keys, allowed, cache_scores, number, lane_max)
 
     settle(lane_max)
 
     @pl.loop(0, new_tiles)
     def _(number):
-        weigh(new_part(number, head), new_scores, number, lane_max, lane_sum, total)
+        weigh(new_part(number, head), new_scores, number, lane_max, lane_sum, total, tok)
 
     @pl.when(reaches)
     def _():
-        weigh(behind_ref[:, head:], far_scores, 0, lane_max, lane_sum, total)
+        weigh(behind_ref[:, head:], far_scores, 0, lane_max, lane_sum, total, tok)
 
     @pl.loop(0, tiles)
     def _(number):
@@ -315,11 +319,12 @@
         @pl.when(needed)
         def _():
             values = cache_part(turn, source, head)
-            weigh(values, cache_scores, number, lane_max, lane_sum, total)
+            weigh(values, cache_scores, number, lane_max, lane_sum, total, tok)
 
     for h in range(heads):
-        row_total = jnp.sum(lane_sum[h], axis=1, keepdims=True)
-        out_ref[:, h * head : (h + 1) * head] = (total[h] / row_total).astype(jnp.bfloat16)
+        rows = slice(h * tok, (h + 1) * tok)
+        row_total = jnp.sum(lane_sum[rows], axis=1, keepdims=True)
+        out_ref[:, h * head : (h + 1) * head] = (total[rows] / row_total).astype(jnp.bfloat16)
 
 
 def local(queries, new_kv, cached_key_value, new_doc, cache_doc, cache_len):
@@ -385,12 +390,13 @@
                 in_specs=[smem, vmem, vmem, vmem],
                 out_specs=vmem,
                 scratch_shapes=[
-                    pltpu.VMEM((blk_count // 2, heads, tok, 2 * tok), jnp.float32),
-                    pltpu.VMEM((1, heads, tok, tok), jnp.float32),
-                    pltpu.VMEM((tiles, heads, tok, span), jnp.float32),
-                    pltpu.VMEM((heads, tok, head), jnp.float32),
-                    pltpu.VMEM((heads, tok, head), jnp.float32),
-                    pltpu.VMEM((heads, tok, head), jnp.float32),
+                    pltpu.VMEM((heads * tok, head), jnp.bfloat16),
+                    pltpu.VMEM((blk_count // 2, heads * tok, 2 * tok), jnp.float32),
+                    pltpu.VMEM((1, heads * tok, tok), jnp.float32),
+                    pltpu.VMEM((tiles, heads * tok, span), jnp.float32),
+                    pltpu.VMEM((heads * tok, head), jnp.float32),
+                    pltpu.VMEM((heads * tok, head), jnp.float32),
+                    pltpu.VMEM((heads * tok, head), jnp.float32),
                 ],
                 compiler_params=limits,
             )(table, queries, arrived, behind)

time: 67.8 us -> 67.8 us (level)
  the two profiles are of different devices: /device:TPU:16 before, /device:TPU:25 now
where the time goes in v4:
time: 67.8 us; the launch traced here: 67.2 us
  blocking collectives  41.4 us (61%)
  starting transfers between devices  12.3 us (18%)
  Pallas kernels  8.14 us (12%)
  local copies, waits for them, and re-layouts  4.58 us (7%)
  between operations  0.75 us (1%)
    all_to_all x1, blocking collectives, local(): lax.all_to_all(attended.reshape(head_count, share, width), 'head', split_...  22.1 us
    all_to_all x1, blocking collectives, run(): arrived = lax.all_to_all(packed, 'blk', split_axis=0, concat_axis=0)  19.3 us
    all_to_all x1, starting transfers between devices, local(): shards = lax.all_to_all(spread, 'cp', split_axis=0, concat_axis=0)  6.85 us
    ppermute x1, starting transfers between devices, local(): lax.ppermute(new_raw, 'cp', [(i, (i + 1) % cp_count) for i in range(cp_co...  5.44 us
    pallas_call x1, Pallas kernels, run(): pl.pallas_call(functools.partial(attention_kernel, shard_rows=shard_rows,...  5.01 us
    unnamed x10, local copies, waits for them, and re-layouts  3.72 us
    pallas_call x1, Pallas kernels, local(): pl.pallas_call(functools.partial(prepare_kernel, turns=turns, period=peri...  1.58 us
  transfers between devices with their start and end apart: 2, of which 0 were waited for; matrix products, arithmetic and copies ran while one was open for 0% of the time, Pallas kernels for 2%

profile of v4, /device:TPU:25, one launch (start us, length us, event | category | flops | bytes accessed | tf_op | source)
XLA Modules:
  0.0 67.2 jit_solution(12078252862195550804)
XLA Ops:
  0.0 0.0 copy-start.1
  0.0 0.8 %copy-done.1 = bf16[64,1,2,128]{3,2,1,0:T(2,128)(2,1)S(1)} copy-done((bf16[64,1,2,128]{3,2,1,0:T(2,128)(2,1)S(1)}, bf16[64,1,2,128]{3,2,1,0:T(2,128)(2,1)}, u32[]{:S(2)}) %copy-start.1) | copy-done | bytes 32792
  0.8 0.7 %shard_map.65 = bf16[8,64,256]{2,1,0:T(8,128)(2,1)} custom-call(bf16[128,128]{1,0:T(8,128)(2,1)S(1)} %bitcast.11), custom_call_target="tpu_custom_call" | custom-call | tf_op jit(solution)/shard_map/pallas_call | solution.py:345
  1.5 6.8 %all-to-all-start.3 = ((bf16[8,64,256]{2,1,0:T(8,128)(2,1)}), bf16[8,64,256]{2,1,0:T(8,128)(2,1)S(1)}, u32[]{:S(2)}, u32[]{:S(2)}) async-start(bf16[8,64,256]{2,1,0:T(8,128)(2,1)} %shard_map.65), calls=%async_computation.3 | async-start | bytes 524288 | tf_op jit(solution)/shard_map/all_to_all | solution.py:353
  8.3 5.4 %collective-permute-start = (bf16[256,128]{1,0:T(8,128)(2,1)}, bf16[256,128]{1,0:T(8,128)(2,1)S(1)}, u32[]{:S(2)}, u32[]{:S(2)}) collective-permute-start(bf16[256,128]{1,0:T(8,128)(2,1)} %bitcast.9), channel_id=1, source_target_pairs={{0,64},{64,128},{128,192},{192,256},{256,320},{320,384},{384,448},... | collective-permute-start | bytes 196616 | tf_op jit(solution)/shard_map/ppermute | solution.py:354
  13.8 0.0 copy-start
  13.8 0.8 %copy-done = bf16[128,1,2,128]{3,2,1,0:T(2,128)(2,1)S(1)} copy-done((bf16[128,1,2,128]{3,2,1,0:T(2,128)(2,1)S(1)}, bf16[128,1,2,128]{3,2,1,0:T(2,128)(2,1)}, u32[]{:S(2)}) %copy-start) | copy-done | bytes 65560
  14.6 0.0 copy-start.2
  14.6 0.8 %copy-done.2 = s32[8192]{0:T(1024)S(1)} copy-done((s32[8192]{0:T(1024)S(1)}, s32[8192]{0:T(1024)}, u32[]{:S(2)}) %copy-start.2) | copy-done | bytes 32792
  15.4 0.0 copy-start.3
  15.4 0.7 %copy-done.3 = s32[4096]{0:T(1024)S(1)} copy-done((s32[4096]{0:T(1024)S(1)}, s32[4096]{0:T(1024)}, u32[]{:S(2)}) %copy-start.3) | copy-done | bytes 16408
  16.1 0.0 copy-start.4
  16.1 0.7 copy-done.4
  16.8 1.6 %shard_map.64 = (bf16[128,256]{1,0:T(8,128)(2,1)S(1)}, s32[110]{0:T(128)S(1)}, s32[1]{0:T(128)}) custom-call(s32[1]{0:T(128)} %bitcast.place_ref, s32[64]{0:T(128)S(1)} %copy-done.4, bf16[256,128]{1,0:T(8,128)(2,1)S(1)} %bitcast.10, s32[64,128]{1,0:T(8,128)S(1)} %bitcast.12, s32[32,128]{1,0:T(8,128)S(1)} %bitcast.13), custom_call_target="tpu_custom_call" | custom-call | tf_op jit(solution)/shard_map/pallas_call | solution.py:355
  19.0 0.0 collective-permute-done
  19.1 0.0 all-to-all-done.3
  19.1 25.2 %conditional.1 = (bf16[128,1024]{1,0:T(8,128)(2,1)S(1)}) conditional(s32[]{:T(128)} %bitcast.4, (s32[110]{0:T(128)S(1)}, bf16[8,64,256]{2,1,0:T(8,128)(2,1)S(1)}, bf16[128,256]{1,0:T(8,128)(2,1)S(1)}, bf16[256,128]{1,0:T(8,128)(2,1)S(1)}, bf16[128,1024]{1,0:T(8,128)(2,1)}) %tuple.18, (s32[110]{0:T(128)S(1)}, ...), branch_computations={%region_0.0_spmd, %region_1.0_spmd, %region_2.0_spmd} | conditional | bytes 6291492 | solution.py:406
  19.1 0.0 copy-start.5
  19.1 0.8 %branch_0_fun.2 = (bf16[8,256,256]{2,1,0:T(8,128)(2,1)S(1)}, bf16[128,256]{1,0:T(8,128)(2,1)S(1)}) custom-call(s32[110]{0:T(128)S(1)} %get-tuple-element.38.table_ref, bf16[8,64,256]{2,1,0:T(8,128)(2,1)S(1)} %get-tuple-element.41.shards_ref, bf16[128,256]{1,0:T(8,128)(2,1)S(1)} %get-tuple-element.42.own_ref, bf16[256,128]{1,0:T(8,128)(2,1)S(1)} %get-tuple-element.43.raw_ref), custom_call_target="tpu_custom_call" | custom-call | tf_op jit(solution)/shard_map/cond/branch_0_fun/pallas_call | solution.py:371
  19.9 19.3 %all_to_all.22.arrived_ref = bf16[8,256,256]{2,1,0:T(8,128)(2,1)S(1)} all-to-all(bf16[8,256,256]{2,1,0:T(8,128)(2,1)S(1)} %get-tuple-element.44), channel_id=1, replica_groups=mesh['cp'=8,'blk'=8,'head'=8] {'blk'}, dimensions={0} | all-to-all | bytes 2097152 | tf_op jit(solution)/shard_map/cond/branch_0_fun/all_to_all | solution.py:382
  39.2 0.0 copy-done.5
  39.2 5.0 %branch_0_fun.3 = bf16[128,1024]{1,0:T(8,128)(2,1)S(1)} custom-call(s32[110]{0:T(128)S(1)} %get-tuple-element.38.table_ref, bf16[128,1024]{1,0:T(8,128)(2,1)S(1)} %copy-done.5, bf16[8,256,256]{2,1,0:T(8,128)(2,1)S(1)} %all_to_all.22.arrived_ref, bf16[128,256]{1,0:T(8,128)(2,1)S(1)} %get-tuple-element.45.behind_ref), custom_call_target="tpu_custom_call" | custom-call | tf_op jit(solution)/shard_map/cond/branch_0_fun/pallas_call | solution.py:385
  44.3 22.1 %all_to_all.25 = bf16[8,16,1024]{2,1,0:T(8,128)(2,1)S(1)} all-to-all(bf16[8,16,1024]{2,1,0:T(8,128)(2,1)S(1)} %bitcast.18), channel_id=1, replica_groups=mesh['cp'=8,'blk'=8,'head'=8] {'head'}, dimensions={0} | all-to-all | bytes 524288 | tf_op jit(solution)/shard_map/all_to_all | solution.py:416
  66.4 0.9 %copy.7 = bf16[16,8,1024]{2,1,0:T(8,128)(2,1)} copy(bf16[16,8,1024]{2,0,1:T(8,128)(2,1)S(1)} %bitcast.17) | data formatting | bytes 524288 | tf_op jit(solution)/shard_map/transpose | solution.py:419
Async XLA Ops:
  0.0 0.8 %copy-start.1 = (bf16[64,1,2,128]{3,2,1,0:T(2,128)(2,1)S(1)}, bf16[64,1,2,128]{3,2,1,0:T(2,128)(2,1)}, u32[]{:S(2)}) copy-start(bf16[64,1,2,128]{3,2,1,0:T(2,128)(2,1)} %param.11) | copy-start | bytes 98308
  1.5 17.6 %all-to-all-start.3 = ((bf16[8,64,256]{2,1,0:T(8,128)(2,1)}), bf16[8,64,256]{2,1,0:T(8,128)(2,1)S(1)}, u32[]{:S(2)}, u32[]{:S(2)}) async-start(bf16[8,64,256]{2,1,0:T(8,128)(2,1)} %shard_map.65), calls=%async_computation.3 | async-start | bytes 524288 | tf_op jit(solution)/shard_map/all_to_all | solution.py:353
  8.3 10.7 %collective-permute-start = (bf16[256,128]{1,0:T(8,128)(2,1)}, bf16[256,128]{1,0:T(8,128)(2,1)S(1)}, u32[]{:S(2)}, u32[]{:S(2)}) collective-permute-start(bf16[256,128]{1,0:T(8,128)(2,1)} %bitcast.9), channel_id=1, source_target_pairs={{0,64},{64,128},{128,192},{192,256},{256,320},{320,384},{384,448},... | collective-permute-start | bytes 196616 | tf_op jit(solution)/shard_map/ppermute | solution.py:354
  13.8 0.8 %copy-start = (bf16[128,1,2,128]{3,2,1,0:T(2,128)(2,1)S(1)}, bf16[128,1,2,128]{3,2,1,0:T(2,128)(2,1)}, u32[]{:S(2)}) copy-start(bf16[128,1,2,128]{3,2,1,0:T(2,128)(2,1)} %param.10) | copy-start | bytes 196612
  14.6 0.8 %copy-start.2 = (s32[8192]{0:T(1024)S(1)}, s32[8192]{0:T(1024)}, u32[]{:S(2)}) copy-start(s32[8192]{0:T(1024)} %param.12) | copy-start | bytes 98308
  15.4 0.7 %copy-start.3 = (s32[4096]{0:T(1024)S(1)}, s32[4096]{0:T(1024)}, u32[]{:S(2)}) copy-start(s32[4096]{0:T(1024)} %param.13) | copy-start | bytes 49156
  16.1 0.7 copy-start.4
  19.1 20.2 %copy-start.5 = (bf16[128,1024]{1,0:T(8,128)(2,1)S(1)}, bf16[128,1024]{1,0:T(8,128)(2,1)}, u32[]{:S(2)}) copy-start(bf16[128,1024]{1,0:T(8,128)(2,1)} %get-tuple-element.40.queries_ref) | copy-start | bytes 786436 | tf_op jit(solution)/shard_map/cond

commit v5 on v3

--- a/solution.py
+++ b/solution.py
@@ -159,14 +159,13 @@
 
 
 def score(queries_ref, keys, allowed, scores_ref, at, lane_max):
+    turned = keys.T
+    shift = jnp.where(allowed, 0.0, negative)
     for h in range(lane_max.shape[0]):
-        scores = lax.dot_general(
-            queries_ref[:, h * head : (h + 1) * head],
-            keys,
-            (((1,), (1,)), ((), ())),
-            preferred_element_type=jnp.float32,
+        scores = jnp.dot(
+            queries_ref[:, h * head : (h + 1) * head], turned, preferred_element_type=jnp.float32
         )
-        scores = jnp.where(allowed, scores, negative)
+        scores = scores + shift
         scores_ref[at, h] = scores
         best = scores[:, :head]
         for part in range(1, scores.shape[1] // head):

time: 67.8 us -> 67.4 us (level)
  Pallas kernels: 8.15 us -> 6.95 us
  blocking collectives: 40.9 us -> 41.8 us
    pallas_call x1, Pallas kernels: 5.02 us -> 3.82 us  [run(): pl.pallas_call(functools.partial(attention_kernel, shard_rows=shard_rows,...]
    all_to_all x1, blocking collectives: 20.5 us -> 21.3 us  [local(): lax.all_to_all(attended.reshape(head_count, share, width), 'head', split_...]
where the time goes in v5:
time: 67.4 us; the launch traced here: 66.9 us
  blocking collectives  41.8 us (62%)
  starting transfers between devices  11.1 us (16%)
  Pallas kernels  6.95 us (10%)
  local copies, waits for them, and re-layouts  4.58 us (7%)
  waiting for transfers between devices  1.72 us (3%)
  between operations  0.73 us (1%)
    all_to_all x1, blocking collectives, local(): lax.all_to_all(attended.reshape(head_count, share, width), 'head', split_...  21.3 us
    all_to_all x1, blocking collectives, run(): arrived = lax.all_to_all(packed, 'blk', split_axis=0, concat_axis=0)  20.4 us
    all_to_all x1, starting transfers between devices, local(): shards = lax.all_to_all(spread, 'cp', split_axis=0, concat_axis=0)  9.03 us
    pallas_call x1, Pallas kernels, run(): pl.pallas_call(functools.partial(attention_kernel, shard_rows=shard_rows,...  3.82 us
    unnamed x10, local copies, waits for them, and re-layouts  3.72 us
    ppermute x1, starting transfers between devices, local(): lax.ppermute(new_raw, 'cp', [(i, (i + 1) % cp_count) for i in range(cp_co...  2.05 us
    pallas_call x1, Pallas kernels, local(): pl.pallas_call(functools.partial(prepare_kernel, turns=turns, period=peri...  1.58 us
    all_to_all x1, waiting for transfers between devices, local(): shards = lax.all_to_all(spread, 'cp', split_axis=0, concat_axis=0)  1.47 us
  transfers between devices with their start and end apart: 2, of which 2 were waited for; matrix products, arithmetic and copies ran while one was open for 0% of the time, Pallas kernels for 2%

profile of v5, /device:TPU:16, one launch (start us, length us, event | category | flops | bytes accessed | tf_op | source)
XLA Modules:
  0.0 66.9 jit_solution(3283046557535217428)
XLA Ops:
  0.0 0.0 copy-start.1
  0.0 0.8 %copy-done.1 = bf16[64,1,2,128]{3,2,1,0:T(2,128)(2,1)S(1)} copy-done((bf16[64,1,2,128]{3,2,1,0:T(2,128)(2,1)S(1)}, bf16[64,1,2,128]{3,2,1,0:T(2,128)(2,1)}, u32[]{:S(2)}) %copy-start.1) | copy-done | bytes 32792
  0.8 0.7 %shard_map.65 = bf16[8,64,256]{2,1,0:T(8,128)(2,1)} custom-call(bf16[128,128]{1,0:T(8,128)(2,1)S(1)} %bitcast.11), custom_call_target="tpu_custom_call" | custom-call | tf_op jit(solution)/shard_map/pallas_call | solution.py:339
  1.5 9.0 %all-to-all-start.3 = ((bf16[8,64,256]{2,1,0:T(8,128)(2,1)}), bf16[8,64,256]{2,1,0:T(8,128)(2,1)S(1)}, u32[]{:S(2)}, u32[]{:S(2)}) async-start(bf16[8,64,256]{2,1,0:T(8,128)(2,1)} %shard_map.65), calls=%async_computation.3 | async-start | bytes 524288 | tf_op jit(solution)/shard_map/all_to_all | solution.py:347
  10.5 2.0 %collective-permute-start = (bf16[256,128]{1,0:T(8,128)(2,1)}, bf16[256,128]{1,0:T(8,128)(2,1)S(1)}, u32[]{:S(2)}, u32[]{:S(2)}) collective-permute-start(bf16[256,128]{1,0:T(8,128)(2,1)} %bitcast.9), channel_id=1, source_target_pairs={{0,64},{64,128},{128,192},{192,256},{256,320},{320,384},{384,448},... | collective-permute-start | bytes 196616 | tf_op jit(solution)/shard_map/ppermute | solution.py:348
  12.6 0.0 copy-start
  12.6 0.8 %copy-done = bf16[128,1,2,128]{3,2,1,0:T(2,128)(2,1)S(1)} copy-done((bf16[128,1,2,128]{3,2,1,0:T(2,128)(2,1)S(1)}, bf16[128,1,2,128]{3,2,1,0:T(2,128)(2,1)}, u32[]{:S(2)}) %copy-start) | copy-done | bytes 65560
  13.4 0.0 copy-start.2
  13.4 0.8 %copy-done.2 = s32[8192]{0:T(1024)S(1)} copy-done((s32[8192]{0:T(1024)S(1)}, s32[8192]{0:T(1024)}, u32[]{:S(2)}) %copy-start.2) | copy-done | bytes 32792
  14.2 0.0 copy-start.3
  14.2 0.7 %copy-done.3 = s32[4096]{0:T(1024)S(1)} copy-done((s32[4096]{0:T(1024)S(1)}, s32[4096]{0:T(1024)}, u32[]{:S(2)}) %copy-start.3) | copy-done | bytes 16408
  14.9 0.0 copy-start.4
  14.9 0.7 copy-done.4
  15.6 1.6 %shard_map.64 = (bf16[128,256]{1,0:T(8,128)(2,1)S(1)}, s32[110]{0:T(128)S(1)}, s32[1]{0:T(128)}) custom-call(s32[1]{0:T(128)} %bitcast.place_ref, s32[64]{0:T(128)S(1)} %copy-done.4, bf16[256,128]{1,0:T(8,128)(2,1)S(1)} %bitcast.10, s32[64,128]{1,0:T(8,128)S(1)} %bitcast.12, s32[32,128]{1,0:T(8,128)S(1)} %bitcast.13), custom_call_target="tpu_custom_call" | custom-call | tf_op jit(solution)/shard_map/pallas_call | solution.py:349
  17.8 0.2 collective-permute-done
  18.1 1.5 %all-to-all-done.3 = bf16[8,64,256]{2,1,0:T(8,128)(2,1)S(1)} async-done(((bf16[8,64,256]{2,1,0:T(8,128)(2,1)}), bf16[8,64,256]{2,1,0:T(8,128)(2,1)S(1)}, u32[]{:S(2)}, u32[]{:S(2)}) %all-to-all-start.3) | async-done | bytes 262176 | tf_op jit(solution)/shard_map/all_to_all | solution.py:347
  19.6 25.1 %conditional.1 = (bf16[128,1024]{1,0:T(8,128)(2,1)S(1)}) conditional(s32[]{:T(128)} %bitcast.4, (s32[110]{0:T(128)S(1)}, bf16[8,64,256]{2,1,0:T(8,128)(2,1)S(1)}, bf16[128,256]{1,0:T(8,128)(2,1)S(1)}, bf16[256,128]{1,0:T(8,128)(2,1)S(1)}, bf16[128,1024]{1,0:T(8,128)(2,1)}) %tuple.18, (s32[110]{0:T(128)S(1)}, ...), branch_computations={%region_0.0_spmd, %region_1.0_spmd, %region_2.0_spmd} | conditional | bytes 6291492 | solution.py:399
  19.6 0.0 copy-start.5
  19.6 0.8 %branch_0_fun.2 = (bf16[8,256,256]{2,1,0:T(8,128)(2,1)S(1)}, bf16[128,256]{1,0:T(8,128)(2,1)S(1)}) custom-call(s32[110]{0:T(128)S(1)} %get-tuple-element.38.table_ref, bf16[8,64,256]{2,1,0:T(8,128)(2,1)S(1)} %get-tuple-element.41.shards_ref, bf16[128,256]{1,0:T(8,128)(2,1)S(1)} %get-tuple-element.42.own_ref, bf16[256,128]{1,0:T(8,128)(2,1)S(1)} %get-tuple-element.43.raw_ref), custom_call_target="tpu_custom_call" | custom-call | tf_op jit(solution)/shard_map/cond/branch_0_fun/pallas_call | solution.py:365
  20.4 20.4 %all_to_all.22.arrived_ref = bf16[8,256,256]{2,1,0:T(8,128)(2,1)S(1)} all-to-all(bf16[8,256,256]{2,1,0:T(8,128)(2,1)S(1)} %get-tuple-element.44), channel_id=1, replica_groups=mesh['cp'=8,'blk'=8,'head'=8] {'blk'}, dimensions={0} | all-to-all | bytes 2097152 | tf_op jit(solution)/shard_map/cond/branch_0_fun/all_to_all | solution.py:376
  40.8 0.0 copy-done.5
  40.8 3.8 %branch_0_fun.3 = bf16[128,1024]{1,0:T(8,128)(2,1)S(1)} custom-call(s32[110]{0:T(128)S(1)} %get-tuple-element.38.table_ref, bf16[128,1024]{1,0:T(8,128)(2,1)S(1)} %copy-done.5, bf16[8,256,256]{2,1,0:T(8,128)(2,1)S(1)} %all_to_all.22.arrived_ref, bf16[128,256]{1,0:T(8,128)(2,1)S(1)} %get-tuple-element.45.behind_ref), custom_call_target="tpu_custom_call" | custom-call | tf_op jit(solution)/shard_map/cond/branch_0_fun/pallas_call | solution.py:379
  44.7 21.3 %all_to_all.25 = bf16[8,16,1024]{2,1,0:T(8,128)(2,1)S(1)} all-to-all(bf16[8,16,1024]{2,1,0:T(8,128)(2,1)S(1)} %bitcast.18), channel_id=1, replica_groups=mesh['cp'=8,'blk'=8,'head'=8] {'head'}, dimensions={0} | all-to-all | bytes 524288 | tf_op jit(solution)/shard_map/all_to_all | solution.py:409
  66.0 0.9 %copy.7 = bf16[16,8,1024]{2,1,0:T(8,128)(2,1)} copy(bf16[16,8,1024]{2,0,1:T(8,128)(2,1)S(1)} %bitcast.17) | data formatting | bytes 524288 | tf_op jit(solution)/shard_map/transpose | solution.py:412
Async XLA Ops:
  0.0 0.8 %copy-start.1 = (bf16[64,1,2,128]{3,2,1,0:T(2,128)(2,1)S(1)}, bf16[64,1,2,128]{3,2,1,0:T(2,128)(2,1)}, u32[]{:S(2)}) copy-start(bf16[64,1,2,128]{3,2,1,0:T(2,128)(2,1)} %param.11) | copy-start | bytes 98308
  1.5 18.1 %all-to-all-start.3 = ((bf16[8,64,256]{2,1,0:T(8,128)(2,1)}), bf16[8,64,256]{2,1,0:T(8,128)(2,1)S(1)}, u32[]{:S(2)}, u32[]{:S(2)}) async-start(bf16[8,64,256]{2,1,0:T(8,128)(2,1)} %shard_map.65), calls=%async_computation.3 | async-start | bytes 524288 | tf_op jit(solution)/shard_map/all_to_all | solution.py:347
  10.5 7.6 %collective-permute-start = (bf16[256,128]{1,0:T(8,128)(2,1)}, bf16[256,128]{1,0:T(8,128)(2,1)S(1)}, u32[]{:S(2)}, u32[]{:S(2)}) collective-permute-start(bf16[256,128]{1,0:T(8,128)(2,1)} %bitcast.9), channel_id=1, source_target_pairs={{0,64},{64,128},{128,192},{192,256},{256,320},{320,384},{384,448},... | collective-permute-start | bytes 196616 | tf_op jit(solution)/shard_map/ppermute | solution.py:348
  12.6 0.8 %copy-start = (bf16[128,1,2,128]{3,2,1,0:T(2,128)(2,1)S(1)}, bf16[128,1,2,128]{3,2,1,0:T(2,128)(2,1)}, u32[]{:S(2)}) copy-start(bf16[128,1,2,128]{3,2,1,0:T(2,128)(2,1)} %param.10) | copy-start | bytes 196612
  13.4 0.8 %copy-start.2 = (s32[8192]{0:T(1024)S(1)}, s32[8192]{0:T(1024)}, u32[]{:S(2)}) copy-start(s32[8192]{0:T(1024)} %param.12) | copy-start | bytes 98308
  14.2 0.7 %copy-start.3 = (s32[4096]{0:T(1024)S(1)}, s32[4096]{0:T(1024)}, u32[]{:S(2)}) copy-start(s32[4096]{0:T(1024)} %param.13) | copy-start | bytes 49156
  14.9 0.7 copy-start.4
  19.6 21.3 %copy-start.5 = (bf16[128,1024]{1,0:T(8,128)(2,1)S(1)}, bf16[128,1024]{1,0:T(8,128)(2,1)}, u32[]{:S(2)}) copy-start(bf16[128,1024]{1,0:T(8,128)(2,1)} %get-tuple-element.40.queries_ref) | copy-start | bytes 786436 | tf_op jit(solution)/shard_map/cond

commit v6 on v5

--- a/solution.py
+++ b/solution.py
@@ -45,7 +45,9 @@
     new_ref,
     new_doc_ref,
     cache_doc_ref,
+    queries_ref,
     own_ref,
+    turned_ref,
     table_ref,
     pick_ref,
     wide,
@@ -57,6 +59,8 @@
     tok = own_ref.shape[0]
     new_starts, cache_starts, lengths = table_places(count)
     own_ref[...] = split_pairs(new_ref[...], wide, tok)
+    for first in range(0, turned_ref.shape[1], head):
+        turned_ref[:, first : first + head] = queries_ref[:, first : first + head].T
     new_doc = new_doc_ref[...]
     cache_doc = cache_doc_ref[...]
     first_doc = new_doc[:, :1]
@@ -145,10 +149,10 @@
 
 def row_bounds(table_ref, count, first, tok):
     new_starts, cache_starts, _ = table_places(count)
-    row_place = first + lax.broadcasted_iota(jnp.int32, (tok, 1), 0)
-    row_start = jnp.zeros((tok, 1), jnp.int32)
-    row_low = jnp.zeros((tok, 1), jnp.int32)
-    row_high = jnp.full((tok, 1), table_ref[cache_starts + 1], jnp.int32)
+    row_place = first + lax.broadcasted_iota(jnp.int32, (1, tok), 1)
+    row_start = jnp.zeros((1, tok), jnp.int32)
+    row_low = jnp.zeros((1, tok), jnp.int32)
+    row_high = jnp.full((1, tok), table_ref[cache_starts + 1], jnp.int32)
     for doc in range(1, documents):
         start = table_ref[new_starts + doc]
         reached = row_place >= start
@@ -158,62 +162,40 @@
     return row_place, row_start, row_low, row_high
 
 
-def score(queries_ref, keys, allowed, scores_ref, at, lane_max):
-    turned = keys.T
+def attend_tile(turned_ref, keys, values, allowed, best_ref, sum_ref, total):
+    turned_values = values.T
     shift = jnp.where(allowed, 0.0, negative)
-    for h in range(lane_max.shape[0]):
-        scores = jnp.dot(
-            queries_ref[:, h * head : (h + 1) * head], turned, preferred_element_type=jnp.float32
+    wide = 2 * allowed.shape[1]
+    shift = jnp.concatenate([shift, shift], axis=1)
+    for first in range(0, turned_ref.shape[1], wide):
+        rows = slice(first, first + wide)
+        scores = jnp.dot(keys, turned_ref[:, rows], preferred_element_type=jnp.float32) + shift
+        before = best_ref[:, rows]
+        best = jnp.maximum(before, jnp.max(scores, axis=0, keepdims=True))
+        weights = jnp.exp2((scores - best) * exponent_scale)
+        scale = jnp.exp2((before - best) * exponent_scale)
+        best_ref[:, rows] = best
+        sum_ref[:, rows] = sum_ref[:, rows] * scale + jnp.sum(weights, axis=0, keepdims=True)
+        total[:, rows] = total[:, rows] * scale + jnp.dot(
+            turned_values, weights.astype(jnp.bfloat16), preferred_element_type=jnp.float32
         )
-        scores = scores + shift
-        scores_ref[at, h] = scores
-        best = scores[:, :head]
-        for part in range(1, scores.shape[1] // head):
-            best = jnp.maximum(best, scores[:, part * head : (part + 1) * head])
-        lane_max[h] = jnp.maximum(lane_max[h], best)
-
-
-def weigh(values, scores_ref, at, lane_max, lane_sum, total):
-    for h in range(lane_max.shape[0]):
-        scores = scores_ref[at, h]
-        best = lane_max[h]
-        added = lane_sum[h]
-        parts = []
-        for part in range(scores.shape[1] // head):
-            piece = scores[:, part * head : (part + 1) * head]
-            weight = jnp.exp2((piece - best) * exponent_scale)
-            added = added + weight
-            parts.append(weight.astype(jnp.bfloat16))
-        lane_sum[h] = added
-        rounded = parts[0] if len(parts) == 1 else jnp.concatenate(parts, axis=1)
-        total[h] += jnp.dot(rounded, values, preferred_element_type=jnp.float32)
-
-
-def settle(lane_max):
-    for h in range(lane_max.shape[0]):
-        best = jnp.max(lane_max[h], axis=1, keepdims=True)
-        lane_max[h] = jnp.broadcast_to(best, lane_max.shape[1:])
 
 
 def attention_kernel(
     table_ref,
-    queries_ref,
+    turned_ref,
     arrived_ref,
     behind_ref,
     out_ref,
-    new_scores,
-    far_scores,
-    cache_scores,
-    lane_max,
-    lane_sum,
+    best_ref,
+    sum_ref,
     total,
     *,
     shard_rows,
     rounds,
     shards,
 ):
-    tok = queries_ref.shape[0]
-    heads = lane_max.shape[0]
+    tok, width = out_ref.shape
     count = arrived_ref.shape[0]
     lengths = table_places(count)[2]
     period = count * shard_rows
@@ -223,102 +205,71 @@
     cache_low = table_ref[cache_low_at]
     cache_high = table_ref[cache_high_at]
     row_place, row_start, row_low, row_high = row_bounds(table_ref, count, block * tok, tok)
-    lane_max[...] = jnp.full(lane_max.shape, negative, jnp.float32)
-    lane_sum[...] = jnp.zeros(lane_sum.shape, jnp.float32)
+    best_ref[...] = jnp.full(best_ref.shape, negative, jnp.float32)
+    sum_ref[...] = jnp.zeros(sum_ref.shape, jnp.float32)
     total[...] = jnp.zeros(total.shape, jnp.float32)
     farthest = block - count
     first_block = table_ref[new_low_at] // tok
     new_tiles = jnp.minimum((block - first_block) // 2 + 1, count // 2)
-    reaches = first_block <= farthest
-
-    def new_part(number, first_lane):
-        lanes = slice(first_lane, first_lane + head)
-        return jnp.concatenate(
+
+    def attend(keys, values, allowed):
+        attend_tile(turned_ref, keys, values, allowed, best_ref, sum_ref, total)
+
+    def new_allowed(place, keys):
+        key_place = place + lax.broadcasted_iota(jnp.int32, (keys, tok), 0)
+        return (key_place >= row_start) & (key_place <= row_place)
+
+    @pl.loop(0, new_tiles)
+    def _(number):
+        rows = jnp.concatenate(
             [
-                arrived_ref[lax.rem(block - 2 * number - back + count, count), new_offset:, lanes]
+                arrived_ref[lax.rem(block - 2 * number - back + count, count), new_offset:]
                 for back in (1, 0)
             ],
             axis=0,
         )
-
-    def new_allowed(place, lanes):
-        key_place = place + lax.broadcasted_iota(jnp.int32, (1, lanes), 1)
-        return (key_place >= row_start) & (key_place <= row_place)
-
-    @pl.loop(0, new_tiles)
+        allowed = new_allowed((block - 2 * number - 1) * tok, 2 * tok)
+        attend(rows[:, :head], rows[:, head:], allowed)
+
+    @pl.when(first_block <= farthest)
+    def _():
+        attend(behind_ref[:, :head], behind_ref[:, head:], new_allowed(farthest * tok, tok))
+
+    @pl.loop(0, rounds * count // pieces)
     def _(number):
-        allowed = new_allowed((block - 2 * number - 1) * tok, 2 * tok)
-        score(queries_ref, new_part(number, 0), allowed, new_scores, number, lane_max)
-
-    @pl.when(reaches)
-    def _():
-        allowed = new_allowed(farthest * tok, tok)
-        score(queries_ref, behind_ref[:, :head], allowed, far_scores, 0, lane_max)
-
-    def cache_tile(number):
         turn = number // (count // pieces)
         source = number % (count // pieces) * pieces
         base = cache_low + turn * period
         begin = base + jnp.bitwise_and(source * shard_rows - base, period - 1)
         holds = jnp.bitwise_and(base - source * shard_rows, period - 1) < span
-        return turn, source, base, (begin < cache_high) | (holds & (base < cache_high))
-
-    def cache_part(turn, source, first_lane):
-        offset = pl.multiple_of(turn * shard_rows, shard_rows)
-        return jnp.concatenate(
-            [
-                arrived_ref[source + part, pl.ds(offset, shard_rows), first_lane : first_lane + head]
-                for part in range(pieces)
-            ],
-            axis=0,
-        )
-
-    tiles = rounds * count // pieces
-
-    @pl.loop(0, tiles)
-    def _(number):
-        turn, source, base, needed = cache_tile(number)
-
-        @pl.when(needed)
+
+        @pl.when((begin < cache_high) | (holds & (base < cache_high)))
         def _():
-            lane = lax.broadcasted_iota(jnp.int32, (1, span), 1)
-            place = base + jnp.bitwise_and(source * shard_rows + lane - base, period - 1)
-            shard = place // shard_rows
-            filled = jnp.zeros((1, span), jnp.int32)
+            offset = pl.multiple_of(turn * shard_rows, shard_rows)
+            rows = jnp.concatenate(
+                [arrived_ref[source + part, pl.ds(offset, shard_rows)] for part in range(pieces)],
+                axis=0,
+            )
+            key = lax.broadcasted_iota(jnp.int32, (shard_rows, tok), 0)
+            allowed = []
             for part in range(pieces):
-                edge = (source + part) * shard_rows
-                for at in (0, shard_rows - 1):
-                    where = base + jnp.bitwise_and(edge + at - base, period - 1)
-                    where = where // shard_rows
-                    length = table_ref[lengths + jnp.minimum(where, shards - 1)]
-                    filled = jnp.where(shard == where, length, filled)
-            usable = jnp.bitwise_and(place, shard_rows - 1) < filled
-            allowed = (place >= row_low) & (place < row_high) & usable
-            keys = cache_part(turn, source, 0)
-            score(queries_ref, keys, allowed, cache_scores, number, lane_max)
-
-    settle(lane_max)
-
-    @pl.loop(0, new_tiles)
-    def _(number):
-        weigh(new_part(number, head), new_scores, number, lane_max, lane_sum, total)
-
-    @pl.when(reaches)
-    def _():
-        weigh(behind_ref[:, head:], far_scores, 0, lane_max, lane_sum, total)
-
-    @pl.loop(0, tiles)
-    def _(number):
-        turn, source, base, needed = cache_tile(number)
-
-        @pl.when(needed)
-        def _():
-            values = cache_part(turn, source, head)
-            weigh(values, cache_scores, number, lane_max, lane_sum, total)
-
-    for h in range(heads):
-        row_total = jnp.sum(lane_sum[h], axis=1, keepdims=True)
-        out_ref[:, h * head : (h + 1) * head] = (total[h] / row_total).astype(jnp.bfloat16)
+                edge = (source + part) * shard_rows - base
+                place = base + jnp.bitwise_and(edge + key, period - 1)
+                head_shard = (base + jnp.bitwise_and(edge, period - 1)) // shard_rows
+                tail_shard = (
+                    base + jnp.bitwise_and(edge + shard_rows - 1, period - 1)
+                ) // shard_rows
+                head_length = table_ref[lengths + jnp.minimum(head_shard, shards - 1)]
+                tail_length = table_ref[lengths + jnp.minimum(tail_shard, shards - 1)]
+                in_head = place < (head_shard + 1) * shard_rows
+                in_head = in_head & (place >= head_shard * shard_rows)
+                filled = jnp.where(in_head, head_length, tail_length)
+                allowed.append((place >= row_low) & (place < row_high) & (key < filled))
+            attend(rows[:, :head], rows[:, head:], jnp.concatenate(allowed, axis=0))
+
+    for first in range(0, width, head):
+        rows = slice(first, first + head)
+        out_ref[:, rows] = (total[:, rows] / sum_ref[:, rows]).T.astype(jnp.bfloat16)
 
 
 def local(queries, new_kv, cached_key_value, new_doc, cache_doc, cache_len):
@@ -346,21 +297,29 @@
     )(cache_raw)
     shards = lax.all_to_all(spread, "cp", split_axis=0, concat_axis=0)
     raw_behind = lax.ppermute(new_raw, "cp", [(i, (i + 1) % cp_count) for i in range(cp_count)])
-    own, table, pick = pl.pallas_call(
+    own, turned, table, pick = pl.pallas_call(
         functools.partial(prepare_kernel, turns=turns, period=period, count=blk_count),
         out_shape=[
             jax.ShapeDtypeStruct((tok, 2 * head), jnp.bfloat16),
+            jax.ShapeDtypeStruct((head, heads * tok), jnp.bfloat16),
             jax.ShapeDtypeStruct((table_places(blk_count)[2] + shard_count,), jnp.int32),
             jax.ShapeDtypeStruct((1,), jnp.int32),
         ],
-        in_specs=[smem] * 2 + [vmem] * 3,
-        out_specs=[vmem, smem, smem],
+        in_specs=[smem] * 2 + [vmem] * 4,
+        out_specs=[vmem, vmem, smem, smem],
         scratch_shapes=[pltpu.VMEM((2 * tok, head), jnp.float32)],
         compiler_params=limits,
-    )(place, cache_len, new_raw, new_doc.reshape(-1, tok), cache_doc.reshape(-1, 128))
+    )(
+        place,
+        cache_len,
+        new_raw,
+        new_doc.reshape(-1, tok),
+        cache_doc.reshape(-1, 128),
+        queries[:, 0],
+    )
 
     def exchange(rounds):
-        def run(shards, own, raw_behind, table, queries):
+        def run(shards, own, raw_behind, table, turned):
             rows = rounds * shard_rows + tok
             packed, behind = pl.pallas_call(
                 functools.partial(pack_kernel, rounds=rounds),
@@ -374,8 +333,6 @@
                 compiler_params=limits,
             )(table, shards, own, raw_behind)
             arrived = lax.all_to_all(packed, "blk", split_axis=0, concat_axis=0)
-            span = pieces * shard_rows
-            tiles = rounds * blk_count // pieces
             return pl.pallas_call(
                 functools.partial(
                     attention_kernel, shard_rows=shard_rows, rounds=rounds, shards=shard_count
@@ -384,15 +341,12 @@
                 in_specs=[smem, vmem, vmem, vmem],
                 out_specs=vmem,
                 scratch_shapes=[
-                    pltpu.VMEM((blk_count // 2, heads, tok, 2 * tok), jnp.float32),
-                    pltpu.VMEM((1, heads, tok, tok), jnp.float32),
-                    pltpu.VMEM((tiles, heads, tok, span), jnp.float32),
-                    pltpu.VMEM((heads, tok, head), jnp.float32),
-                    pltpu.VMEM((heads, tok, head), jnp.float32),
-                    pltpu.VMEM((heads, tok, head), jnp.float32),
+                    pltpu.VMEM((1, heads * tok), jnp.float32),
+                    pltpu.VMEM((1, heads * tok), jnp.float32),
+                    pltpu.VMEM((head, heads * tok), jnp.float32),
                 ],
                 compiler_params=limits,
-            )(table, queries, arrived, behind)
+            )(table, turned, arrived, behind)
 
         return run
 
@@ -403,7 +357,7 @@
         own,
         raw_behind,
         table,
-        queries[:, 0],
+        turned,
     )
     share = tok // head_count
     moved = lax.all_to_all(

time: 67.4 us -> 72.1 us (1.070)
  the two profiles are of different devices: /device:TPU:16 before, /device:TPU:27 now
where the time goes in v6:
time: 72.1 us; the launch traced here: 71.5 us
  blocking collectives  41.6 us (58%)
  starting transfers between devices  12.3 us (17%)
  Pallas kernels  11.4 us (16%)
  local copies, waits for them, and re-layouts  5.52 us (8%)
    all_to_all x1, blocking collectives, local(): lax.all_to_all(attended.reshape(head_count, share, width), 'head', split_...  22 us
    all_to_all x1, blocking collectives, run(): arrived = lax.all_to_all(packed, 'blk', split_axis=0, concat_axis=0)  19.6 us
    pallas_call x1, Pallas kernels, run(): pl.pallas_call(functools.partial(attention_kernel, shard_rows=shard_rows,...  8.23 us
    all_to_all x1, starting transfers between devices, local(): shards = lax.all_to_all(spread, 'cp', split_axis=0, concat_axis=0)  6.85 us
    ppermute x1, starting transfers between devices, local(): lax.ppermute(new_raw, 'cp', [(i, (i + 1) % cp_count) for i in range(cp_co...  5.44 us
    unnamed x12, local copies, waits for them, and re-layouts  4.67 us
    pallas_call x1, Pallas kernels, local(): pl.pallas_call(functools.partial(prepare_kernel, turns=turns, period=peri...  1.58 us
  transfers between devices with their start and end apart: 2, of which 0 were waited for; matrix products, arithmetic and copies ran while one was open for 0% of the time, Pallas kernels for 2%

profile of v6, /device:TPU:27, one launch (start us, length us, event | category | flops | bytes accessed | tf_op | source)
XLA Modules:
  0.0 71.5 jit_solution(7118791341998693795)
XLA Ops:
  0.0 0.0 copy-start.2
  0.0 0.8 %copy-done.2 = bf16[64,1,2,128]{3,2,1,0:T(2,128)(2,1)S(1)} copy-done((bf16[64,1,2,128]{3,2,1,0:T(2,128)(2,1)S(1)}, bf16[64,1,2,128]{3,2,1,0:T(2,128)(2,1)}, u32[]{:S(2)}) %copy-start.2) | copy-done | bytes 32792
  0.8 0.7 %shard_map.65 = bf16[8,64,256]{2,1,0:T(8,128)(2,1)} custom-call(bf16[128,128]{1,0:T(8,128)(2,1)S(1)} %bitcast.12), custom_call_target="tpu_custom_call" | custom-call | tf_op jit(solution)/shard_map/pallas_call | solution.py:290
  1.5 6.8 %all-to-all-start.3 = ((bf16[8,64,256]{2,1,0:T(8,128)(2,1)}), bf16[8,64,256]{2,1,0:T(8,128)(2,1)S(1)}, u32[]{:S(2)}, u32[]{:S(2)}) async-start(bf16[8,64,256]{2,1,0:T(8,128)(2,1)} %shard_map.65), calls=%async_computation.3 | async-start | bytes 524288 | tf_op jit(solution)/shard_map/all_to_all | solution.py:298
  8.3 5.4 %collective-permute-start = (bf16[256,128]{1,0:T(8,128)(2,1)}, bf16[256,128]{1,0:T(8,128)(2,1)S(1)}, u32[]{:S(2)}, u32[]{:S(2)}) collective-permute-start(bf16[256,128]{1,0:T(8,128)(2,1)} %bitcast.10), channel_id=1, source_target_pairs={{0,64},{64,128},{128,192},{192,256},{256,320},{320,384},{384,448},... | collective-permute-start | bytes 196616 | tf_op jit(solution)/shard_map/ppermute | solution.py:299
  13.8 0.0 copy-start
  13.8 0.9 %copy-done = bf16[128,1,1024]{2,0,1:T(8,128)(2,1)S(1)} copy-done((bf16[128,1,1024]{2,0,1:T(8,128)(2,1)S(1)}, bf16[128,1,1024]{2,0,1:T(8,128)(2,1)}, u32[]{:S(2)}) %copy-start) | copy-done | bytes 262168
  14.7 0.0 copy-start.1
  14.7 0.8 %copy-done.1 = bf16[128,1,2,128]{3,2,1,0:T(2,128)(2,1)S(1)} copy-done((bf16[128,1,2,128]{3,2,1,0:T(2,128)(2,1)S(1)}, bf16[128,1,2,128]{3,2,1,0:T(2,128)(2,1)}, u32[]{:S(2)}) %copy-start.1) | copy-done | bytes 65560
  15.6 0.0 copy-start.3
  15.6 0.8 %copy-done.3 = s32[8192]{0:T(1024)S(1)} copy-done((s32[8192]{0:T(1024)S(1)}, s32[8192]{0:T(1024)}, u32[]{:S(2)}) %copy-start.3) | copy-done | bytes 32792
  16.3 0.0 copy-start.4
  16.3 0.7 %copy-done.4 = s32[4096]{0:T(1024)S(1)} copy-done((s32[4096]{0:T(1024)S(1)}, s32[4096]{0:T(1024)}, u32[]{:S(2)}) %copy-start.4) | copy-done | bytes 16408
  17.1 0.0 copy-start.5
  17.1 0.7 copy-done.5
  17.7 1.6 %shard_map.64 = (bf16[128,256]{1,0:T(8,128)(2,1)S(1)}, bf16[128,1024]{1,0:T(8,128)(2,1)S(1)}, s32[110]{0:T(128)S(1)}, s32[1]{0:T(128)}) custom-call(s32[1]{0:T(128)} %bitcast.place_ref, s32[64]{0:T(128)S(1)} %copy-done.5, bf16[256,128]{1,0:T(8,128)(2,1)S(1)} %bitcast.11, s32[64,128]{1,0:T(8,128)S(1)} %bitcast.13, s32[32,128]{1,0:T(8,128)S(1)} %bitcast.14, ...), custom_call_target="tpu_custom_call" | custom-call | tf_op jit(solution)/shard_map/pallas_call | solution.py:300
  19.9 0.0 collective-permute-done
  19.9 0.0 all-to-all-done.3
  20.0 28.6 %conditional.1 = (bf16[128,1024]{1,0:T(8,128)(2,1)S(1)}) conditional(s32[]{:T(128)} %bitcast.5, (s32[110]{0:T(128)S(1)}, bf16[8,64,256]{2,1,0:T(8,128)(2,1)S(1)}, bf16[128,256]{1,0:T(8,128)(2,1)S(1)}, bf16[256,128]{1,0:T(8,128)(2,1)S(1)}, bf16[128,1024]{1,0:T(8,128)(2,1)S(1)}) %tuple.14, (s32[110]{0:T(128)S(1)}, ...), branch_computations={%region_0.0_spmd, %region_1.0_spmd, %region_2.0_spmd} | conditional | bytes 5242888 | solution.py:353
  20.0 0.8 %branch_0_fun.2 = (bf16[8,256,256]{2,1,0:T(8,128)(2,1)S(1)}, bf16[128,256]{1,0:T(8,128)(2,1)S(1)}) custom-call(s32[110]{0:T(128)S(1)} %get-tuple-element.38.table_ref, bf16[8,64,256]{2,1,0:T(8,128)(2,1)S(1)} %get-tuple-element.41.shards_ref, bf16[128,256]{1,0:T(8,128)(2,1)S(1)} %get-tuple-element.42.own_ref, bf16[256,128]{1,0:T(8,128)(2,1)S(1)} %get-tuple-element.43.raw_ref), custom_call_target="tpu_custom_call" | custom-call | tf_op jit(solution)/shard_map/cond/branch_0_fun/pallas_call | solution.py:324
  20.8 19.6 %all_to_all.22.arrived_ref = bf16[8,256,256]{2,1,0:T(8,128)(2,1)S(1)} all-to-all(bf16[8,256,256]{2,1,0:T(8,128)(2,1)S(1)} %get-tuple-element.44), channel_id=1, replica_groups=mesh['cp'=8,'blk'=8,'head'=8] {'blk'}, dimensions={0} | all-to-all | bytes 2097152 | tf_op jit(solution)/shard_map/cond/branch_0_fun/all_to_all | solution.py:335
  40.4 8.2 %branch_0_fun.3 = bf16[128,1024]{1,0:T(8,128)(2,1)S(1)} custom-call(s32[110]{0:T(128)S(1)} %get-tuple-element.38.table_ref, bf16[128,1024]{1,0:T(8,128)(2,1)S(1)} %get-tuple-element.40.turned_ref, bf16[8,256,256]{2,1,0:T(8,128)(2,1)S(1)} %all_to_all.22.arrived_ref, bf16[128,256]{1,0:T(8,128)(2,1)S(1)} %get-tuple-element.45.behind_ref), custom_call_target="tpu_custom_call" | custom-call | tf_op jit(solution)/shard_map/cond/branch_0_fun/pallas_call | solution.py:336
  48.6 22.0 %all_to_all.25 = bf16[8,16,1024]{2,1,0:T(8,128)(2,1)S(1)} all-to-all(bf16[8,16,1024]{2,1,0:T(8,128)(2,1)S(1)} %bitcast.16), channel_id=1, replica_groups=mesh['cp'=8,'blk'=8,'head'=8] {'head'}, dimensions={0} | all-to-all | bytes 524288 | tf_op jit(solution)/shard_map/all_to_all | solution.py:363
  70.6 0.9 %copy.7 = bf16[16,8,1024]{2,1,0:T(8,128)(2,1)} copy(bf16[16,8,1024]{2,0,1:T(8,128)(2,1)S(1)} %bitcast.15) | data formatting | bytes 524288 | tf_op jit(solution)/shard_map/transpose | solution.py:366
Async XLA Ops:
  0.0 0.8 %copy-start.2 = (bf16[64,1,2,128]{3,2,1,0:T(2,128)(2,1)S(1)}, bf16[64,1,2,128]{3,2,1,0:T(2,128)(2,1)}, u32[]{:S(2)}) copy-start(bf16[64,1,2,128]{3,2,1,0:T(2,128)(2,1)} %param.11) | copy-start | bytes 98308
  1.5 18.5 %all-to-all-start.3 = ((bf16[8,64,256]{2,1,0:T(8,128)(2,1)}), bf16[8,64,256]{2,1,0:T(8,128)(2,1)S(1)}, u32[]{:S(2)}, u32[]{:S(2)}) async-start(bf16[8,64,256]{2,1,0:T(8,128)(2,1)} %shard_map.65), calls=%async_computation.3 | async-start | bytes 524288 | tf_op jit(solution)/shard_map/all_to_all | solution.py:298
  8.3 11.6 %collective-permute-start = (bf16[256,128]{1,0:T(8,128)(2,1)}, bf16[256,128]{1,0:T(8,128)(2,1)S(1)}, u32[]{:S(2)}, u32[]{:S(2)}) collective-permute-start(bf16[256,128]{1,0:T(8,128)(2,1)} %bitcast.10), channel_id=1, source_target_pairs={{0,64},{64,128},{128,192},{192,256},{256,320},{320,384},{384,448},... | collective-permute-start | bytes 196616 | tf_op jit(solution)/shard_map/ppermute | solution.py:299
  13.8 1.0 %copy-start = (bf16[128,1,1024]{2,0,1:T(8,128)(2,1)S(1)}, bf16[128,1,1024]{2,0,1:T(8,128)(2,1)}, u32[]{:S(2)}) copy-start(bf16[128,1,1024]{2,0,1:T(8,128)(2,1)} %param.9) | copy-start | bytes 786436
  14.7 0.8 %copy-start.1 = (bf16[128,1,2,128]{3,2,1,0:T(2,128)(2,1)S(1)}, bf16[128,1,2,128]{3,2,1,0:T(2,128)(2,1)}, u32[]{:S(2)}) copy-start(bf16[128,1,2,128]{3,2,1,0:T(2,128)(2,1)} %param.10) | copy-start | bytes 196612
  15.6 0.8 %copy-start.3 = (s32[8192]{0:T(1024)S(1)}, s32[8192]{0:T(1024)}, u32[]{:S(2)}) copy-start(s32[8192]{0:T(1024)} %param.12) | copy-start | bytes 98308
  16.3 0.7 %copy-start.4 = (s32[4096]{0:T(1024)S(1)}, s32[4096]{0:T(1024)}, u32[]{:S(2)}) copy-start(s32[4096]{0:T(1024)} %param.13) | copy-start | bytes 49156
  17.1 0.7 copy-start.5

commit v7 on v5

--- a/solution.py
+++ b/solution.py
@@ -13,7 +13,8 @@
 block_at, new_low_at, cache_low_at, cache_high_at, target_low_at = 0, 1, 2, 3, 4
 longest = 1024
 head = 128
-pieces = 4
+pieces = 8
+blocks = 4
 smem = pl.BlockSpec(memory_space=pltpu.SMEM)
 vmem = pl.BlockSpec(memory_space=pltpu.VMEM)
 exponent_scale = math.log2(math.e) * head**-0.5
@@ -228,15 +229,17 @@
     total[...] = jnp.zeros(total.shape, jnp.float32)
     farthest = block - count
     first_block = table_ref[new_low_at] // tok
-    new_tiles = jnp.minimum((block - first_block) // 2 + 1, count // 2)
+    new_tiles = jnp.minimum((block - first_block) // blocks + 1, count // blocks)
     reaches = first_block <= farthest
 
     def new_part(number, first_lane):
         lanes = slice(first_lane, first_lane + head)
         return jnp.concatenate(
             [
-                arrived_ref[lax.rem(block - 2 * number - back + count, count), new_offset:, lanes]
-                for back in (1, 0)
+                arrived_ref[
+                    lax.rem(block - blocks * number - back + count, count), new_offset:, lanes
+                ]
+                for back in range(blocks - 1, -1, -1)
             ],
             axis=0,
         )
@@ -247,7 +250,7 @@
 
     @pl.loop(0, new_tiles)
     def _(number):
-        allowed = new_allowed((block - 2 * number - 1) * tok, 2 * tok)
+        allowed = new_allowed((block - blocks * number - blocks + 1) * tok, blocks * tok)
         score(queries_ref, new_part(number, 0), allowed, new_scores, number, lane_max)
 
     @pl.when(reaches)
@@ -384,7 +387,7 @@
                 in_specs=[smem, vmem, vmem, vmem],
                 out_specs=vmem,
                 scratch_shapes=[
-                    pltpu.VMEM((blk_count // 2, heads, tok, 2 * tok), jnp.float32),
+                    pltpu.VMEM((blk_count // blocks, heads, tok, blocks * tok), jnp.float32),
                     pltpu.VMEM((1, heads, tok, tok), jnp.float32),
                     pltpu.VMEM((tiles, heads, tok, span), jnp.float32),
                     pltpu.VMEM((heads, tok, head), jnp.float32),

time: 67.4 us -> 66.8 us (level)
  Pallas kernels: 6.95 us -> 7.86 us
  blocking collectives: 41.8 us -> 40.9 us
    pallas_call x1, Pallas kernels: 3.82 us -> 4.73 us  [run(): pl.pallas_call(functools.partial(attention_kernel, shard_rows=shard_rows,...]
    all_to_all x1, blocking collectives: 21.3 us -> 20.5 us  [local(): lax.all_to_all(attended.reshape(head_count, share, width), 'head', split_...]
where the time goes in v7:
time: 66.8 us; the launch traced here: 66.9 us
  blocking collectives  40.9 us (61%)
  starting transfers between devices  11.1 us (17%)
  Pallas kernels  7.86 us (12%)
  local copies, waits for them, and re-layouts  4.58 us (7%)
  waiting for transfers between devices  1.72 us (3%)
  between operations  0.73 us (1%)
    all_to_all x1, blocking collectives, local(): lax.all_to_all(attended.reshape(head_count, share, width), 'head', split_...  20.5 us
    all_to_all x1, blocking collectives, run(): arrived = lax.all_to_all(packed, 'blk', split_axis=0, concat_axis=0)  20.4 us
    all_to_all x1, starting transfers between devices, local(): shards = lax.all_to_all(spread, 'cp', split_axis=0, concat_axis=0)  9.03 us
    pallas_call x1, Pallas kernels, run(): pl.pallas_call(functools.partial(attention_kernel, shard_rows=shard_rows,...  4.73 us
    unnamed x10, local copies, waits for them, and re-layouts  3.72 us
    ppermute x1, starting transfers between devices, local(): lax.ppermute(new_raw, 'cp', [(i, (i + 1) % cp_count) for i in range(cp_co...  2.05 us
    pallas_call x1, Pallas kernels, local(): pl.pallas_call(functools.partial(prepare_kernel, turns=turns, period=peri...  1.58 us
    all_to_all x1, waiting for transfers between devices, local(): shards = lax.all_to_all(spread, 'cp', split_axis=0, concat_axis=0)  1.47 us
  transfers between devices with their start and end apart: 2, of which 2 were waited for; matrix products, arithmetic and copies ran while one was open for 0% of the time, Pallas kernels for 2%

profile of v7, /device:TPU:16, one launch (start us, length us, event | category | flops | bytes accessed | tf_op | source)
XLA Modules:
  0.0 66.9 jit_solution(424065191212208960)
XLA Ops:
  0.0 0.0 copy-start.1
  0.0 0.8 %copy-done.1 = bf16[64,1,2,128]{3,2,1,0:T(2,128)(2,1)S(1)} copy-done((bf16[64,1,2,128]{3,2,1,0:T(2,128)(2,1)S(1)}, bf16[64,1,2,128]{3,2,1,0:T(2,128)(2,1)}, u32[]{:S(2)}) %copy-start.1) | copy-done | bytes 32792
  0.8 0.7 %shard_map.65 = bf16[8,64,256]{2,1,0:T(8,128)(2,1)} custom-call(bf16[128,128]{1,0:T(8,128)(2,1)S(1)} %bitcast.11), custom_call_target="tpu_custom_call" | custom-call | tf_op jit(solution)/shard_map/pallas_call | solution.py:342
  1.5 9.0 %all-to-all-start.3 = ((bf16[8,64,256]{2,1,0:T(8,128)(2,1)}), bf16[8,64,256]{2,1,0:T(8,128)(2,1)S(1)}, u32[]{:S(2)}, u32[]{:S(2)}) async-start(bf16[8,64,256]{2,1,0:T(8,128)(2,1)} %shard_map.65), calls=%async_computation.3 | async-start | bytes 524288 | tf_op jit(solution)/shard_map/all_to_all | solution.py:350
  10.5 2.0 %collective-permute-start = (bf16[256,128]{1,0:T(8,128)(2,1)}, bf16[256,128]{1,0:T(8,128)(2,1)S(1)}, u32[]{:S(2)}, u32[]{:S(2)}) collective-permute-start(bf16[256,128]{1,0:T(8,128)(2,1)} %bitcast.9), channel_id=1, source_target_pairs={{0,64},{64,128},{128,192},{192,256},{256,320},{320,384},{384,448},... | collective-permute-start | bytes 196616 | tf_op jit(solution)/shard_map/ppermute | solution.py:351
  12.6 0.0 copy-start
  12.6 0.8 %copy-done = bf16[128,1,2,128]{3,2,1,0:T(2,128)(2,1)S(1)} copy-done((bf16[128,1,2,128]{3,2,1,0:T(2,128)(2,1)S(1)}, bf16[128,1,2,128]{3,2,1,0:T(2,128)(2,1)}, u32[]{:S(2)}) %copy-start) | copy-done | bytes 65560
  13.4 0.0 copy-start.2
  13.4 0.8 %copy-done.2 = s32[8192]{0:T(1024)S(1)} copy-done((s32[8192]{0:T(1024)S(1)}, s32[8192]{0:T(1024)}, u32[]{:S(2)}) %copy-start.2) | copy-done | bytes 32792
  14.2 0.0 copy-start.3
  14.2 0.7 %copy-done.3 = s32[4096]{0:T(1024)S(1)} copy-done((s32[4096]{0:T(1024)S(1)}, s32[4096]{0:T(1024)}, u32[]{:S(2)}) %copy-start.3) | copy-done | bytes 16408
  14.9 0.0 copy-start.4
  14.9 0.7 copy-done.4
  15.6 1.6 %shard_map.64 = (bf16[128,256]{1,0:T(8,128)(2,1)S(1)}, s32[110]{0:T(128)S(1)}, s32[1]{0:T(128)}) custom-call(s32[1]{0:T(128)} %bitcast.place_ref, s32[64]{0:T(128)S(1)} %copy-done.4, bf16[256,128]{1,0:T(8,128)(2,1)S(1)} %bitcast.10, s32[64,128]{1,0:T(8,128)S(1)} %bitcast.12, s32[32,128]{1,0:T(8,128)S(1)} %bitcast.13), custom_call_target="tpu_custom_call" | custom-call | tf_op jit(solution)/shard_map/pallas_call | solution.py:352
  17.8 0.2 collective-permute-done
  18.1 1.5 %all-to-all-done.3 = bf16[8,64,256]{2,1,0:T(8,128)(2,1)S(1)} async-done(((bf16[8,64,256]{2,1,0:T(8,128)(2,1)}), bf16[8,64,256]{2,1,0:T(8,128)(2,1)S(1)}, u32[]{:S(2)}, u32[]{:S(2)}) %all-to-all-start.3) | async-done | bytes 262176 | tf_op jit(solution)/shard_map/all_to_all | solution.py:350
  19.6 26.0 %conditional.1 = (bf16[128,1024]{1,0:T(8,128)(2,1)S(1)}) conditional(s32[]{:T(128)} %bitcast.4, (s32[110]{0:T(128)S(1)}, bf16[8,64,256]{2,1,0:T(8,128)(2,1)S(1)}, bf16[128,256]{1,0:T(8,128)(2,1)S(1)}, bf16[256,128]{1,0:T(8,128)(2,1)S(1)}, bf16[128,1024]{1,0:T(8,128)(2,1)}) %tuple.18, (s32[110]{0:T(128)S(1)}, ...), branch_computations={%region_0.0_spmd, %region_1.0_spmd, %region_2.0_spmd} | conditional | bytes 6291492 | solution.py:402
  19.6 0.0 copy-start.5
  19.6 0.8 %branch_0_fun.2 = (bf16[8,256,256]{2,1,0:T(8,128)(2,1)S(1)}, bf16[128,256]{1,0:T(8,128)(2,1)S(1)}) custom-call(s32[110]{0:T(128)S(1)} %get-tuple-element.38.table_ref, bf16[8,64,256]{2,1,0:T(8,128)(2,1)S(1)} %get-tuple-element.41.shards_ref, bf16[128,256]{1,0:T(8,128)(2,1)S(1)} %get-tuple-element.42.own_ref, bf16[256,128]{1,0:T(8,128)(2,1)S(1)} %get-tuple-element.43.raw_ref), custom_call_target="tpu_custom_call" | custom-call | tf_op jit(solution)/shard_map/cond/branch_0_fun/pallas_call | solution.py:368
  20.4 20.4 %all_to_all.22.arrived_ref = bf16[8,256,256]{2,1,0:T(8,128)(2,1)S(1)} all-to-all(bf16[8,256,256]{2,1,0:T(8,128)(2,1)S(1)} %get-tuple-element.44), channel_id=1, replica_groups=mesh['cp'=8,'blk'=8,'head'=8] {'blk'}, dimensions={0} | all-to-all | bytes 2097152 | tf_op jit(solution)/shard_map/cond/branch_0_fun/all_to_all | solution.py:379
  40.8 0.0 copy-done.5
  40.8 4.7 %branch_0_fun.3 = bf16[128,1024]{1,0:T(8,128)(2,1)S(1)} custom-call(s32[110]{0:T(128)S(1)} %get-tuple-element.38.table_ref, bf16[128,1024]{1,0:T(8,128)(2,1)S(1)} %copy-done.5, bf16[8,256,256]{2,1,0:T(8,128)(2,1)S(1)} %all_to_all.22.arrived_ref, bf16[128,256]{1,0:T(8,128)(2,1)S(1)} %get-tuple-element.45.behind_ref), custom_call_target="tpu_custom_call" | custom-call | tf_op jit(solution)/shard_map/cond/branch_0_fun/pallas_call | solution.py:382
  45.6 20.5 %all_to_all.25 = bf16[8,16,1024]{2,1,0:T(8,128)(2,1)S(1)} all-to-all(bf16[8,16,1024]{2,1,0:T(8,128)(2,1)S(1)} %bitcast.18), channel_id=1, replica_groups=mesh['cp'=8,'blk'=8,'head'=8] {'head'}, dimensions={0} | all-to-all | bytes 524288 | tf_op jit(solution)/shard_map/all_to_all | solution.py:412
  66.1 0.9 %copy.7 = bf16[16,8,1024]{2,1,0:T(8,128)(2,1)} copy(bf16[16,8,1024]{2,0,1:T(8,128)(2,1)S(1)} %bitcast.17) | data formatting | bytes 524288 | tf_op jit(solution)/shard_map/transpose | solution.py:415
Async XLA Ops:
  0.0 0.8 %copy-start.1 = (bf16[64,1,2,128]{3,2,1,0:T(2,128)(2,1)S(1)}, bf16[64,1,2,128]{3,2,1,0:T(2,128)(2,1)}, u32[]{:S(2)}) copy-start(bf16[64,1,2,128]{3,2,1,0:T(2,128)(2,1)} %param.11) | copy-start | bytes 98308
  1.5 18.1 %all-to-all-start.3 = ((bf16[8,64,256]{2,1,0:T(8,128)(2,1)}), bf16[8,64,256]{2,1,0:T(8,128)(2,1)S(1)}, u32[]{:S(2)}, u32[]{:S(2)}) async-start(bf16[8,64,256]{2,1,0:T(8,128)(2,1)} %shard_map.65), calls=%async_computation.3 | async-start | bytes 524288 | tf_op jit(solution)/shard_map/all_to_all | solution.py:350
  10.5 7.6 %collective-permute-start = (bf16[256,128]{1,0:T(8,128)(2,1)}, bf16[256,128]{1,0:T(8,128)(2,1)S(1)}, u32[]{:S(2)}, u32[]{:S(2)}) collective-permute-start(bf16[256,128]{1,0:T(8,128)(2,1)} %bitcast.9), channel_id=1, source_target_pairs={{0,64},{64,128},{128,192},{192,256},{256,320},{320,384},{384,448},... | collective-permute-start | bytes 196616 | tf_op jit(solution)/shard_map/ppermute | solution.py:351
  12.6 0.8 %copy-start = (bf16[128,1,2,128]{3,2,1,0:T(2,128)(2,1)S(1)}, bf16[128,1,2,128]{3,2,1,0:T(2,128)(2,1)}, u32[]{:S(2)}) copy-start(bf16[128,1,2,128]{3,2,1,0:T(2,128)(2,1)} %param.10) | copy-start | bytes 196612
  13.4 0.8 %copy-start.2 = (s32[8192]{0:T(1024)S(1)}, s32[8192]{0:T(1024)}, u32[]{:S(2)}) copy-start(s32[8192]{0:T(1024)} %param.12) | copy-start | bytes 98308
  14.2 0.7 %copy-start.3 = (s32[4096]{0:T(1024)S(1)}, s32[4096]{0:T(1024)}, u32[]{:S(2)}) copy-start(s32[4096]{0:T(1024)} %param.13) | copy-start | bytes 49156
  14.9 0.7 copy-start.4
  19.6 21.3 %copy-start.5 = (bf16[128,1024]{1,0:T(8,128)(2,1)S(1)}, bf16[128,1024]{1,0:T(8,128)(2,1)}, u32[]{:S(2)}) copy-start(bf16[128,1024]{1,0:T(8,128)(2,1)} %get-tuple-element.40.queries_ref) | copy-start | bytes 786436 | tf_op jit(solution)/shard_map/cond

commit v8 on v4

--- a/solution.py
+++ b/solution.py
@@ -13,7 +13,8 @@
 block_at, new_low_at, cache_low_at, cache_high_at, target_low_at = 0, 1, 2, 3, 4
 longest = 1024
 head = 128
-pieces = 4
+pieces = 8
+blocks = 4
 smem = pl.BlockSpec(memory_space=pltpu.SMEM)
 vmem = pl.BlockSpec(memory_space=pltpu.VMEM)
 exponent_scale = math.log2(math.e) * head**-0.5
@@ -233,15 +234,17 @@
     total[...] = jnp.zeros(total.shape, jnp.float32)
     farthest = block - count
     first_block = table_ref[new_low_at] // tok
-    new_tiles = jnp.minimum((block - first_block) // 2 + 1, count // 2)
+    new_tiles = jnp.minimum((block - first_block) // blocks + 1, count // blocks)
     reaches = first_block <= farthest
 
     def new_part(number, first_lane):
         lanes = slice(first_lane, first_lane + head)
         return jnp.concatenate(
             [
-                arrived_ref[lax.rem(block - 2 * number - back + count, count), new_offset:, lanes]
-                for back in (1, 0)
+                arrived_ref[
+                    lax.rem(block - blocks * number - back + count, count), new_offset:, lanes
+                ]
+                for back in range(blocks - 1, -1, -1)
             ],
             axis=0,
         )
@@ -252,7 +255,7 @@
 
     @pl.loop(0, new_tiles)
     def _(number):
-        allowed = new_allowed((block - 2 * number - 1) * tok, 2 * tok)
+        allowed = new_allowed((block - blocks * number - blocks + 1) * tok, blocks * tok)
         score(query_rows, new_part(number, 0), allowed, new_scores, number, lane_max)
 
     @pl.when(reaches)
@@ -391,7 +394,7 @@
                 out_specs=vmem,
                 scratch_shapes=[
                     pltpu.VMEM((heads * tok, head), jnp.bfloat16),
-                    pltpu.VMEM((blk_count // 2, heads * tok, 2 * tok), jnp.float32),
+                    pltpu.VMEM((blk_count // blocks, heads * tok, blocks * tok), jnp.float32),
                     pltpu.VMEM((1, heads * tok, tok), jnp.float32),
                     pltpu.VMEM((tiles, heads * tok, span), jnp.float32),
                     pltpu.VMEM((heads * tok, head), jnp.float32),

time: 67.8 us -> 67.6 us (level)
  the two profiles are of different devices: /device:TPU:25 before, /device:TPU:24 now
where the time goes in v8:
time: 67.6 us
  blocking collectives  43.4 us (64%)
  starting transfers between devices  8.58 us (13%)
  Pallas kernels  7.32 us (11%)
  local copies, waits for them, and re-layouts  4.58 us (7%)
  waiting for transfers between devices  2.94 us (4%)
  between operations  0.74 us (1%)
    all_to_all x1, blocking collectives, local(): lax.all_to_all(attended.reshape(head_count, share, width), 'head', split_...  22.4 us
    all_to_all x1, blocking collectives, run(): arrived = lax.all_to_all(packed, 'blk', split_axis=0, concat_axis=0)  21 us
    all_to_all x1, starting transfers between devices, local(): shards = lax.all_to_all(spread, 'cp', split_axis=0, concat_axis=0)  6.53 us
    pallas_call x1, Pallas kernels, run(): pl.pallas_call(functools.partial(attention_kernel, shard_rows=shard_rows,...  4.2 us
    unnamed x10, local copies, waits for them, and re-layouts  3.72 us
    all_to_all x1, waiting for transfers between devices, local(): shards = lax.all_to_all(spread, 'cp', split_axis=0, concat_axis=0)  2.94 us
    ppermute x1, starting transfers between devices, local(): lax.ppermute(new_raw, 'cp', [(i, (i + 1) % cp_count) for i in range(cp_co...  2.05 us
    pallas_call x1, Pallas kernels, local(): pl.pallas_call(functools.partial(prepare_kernel, turns=turns, period=peri...  1.58 us
  transfers between devices with their start and end apart: 2, of which 1 were waited for; matrix products, arithmetic and copies ran while one was open for 0% of the time, Pallas kernels for 2%

profile of v8, /device:TPU:24, one launch (start us, length us, event | category | flops | bytes accessed | tf_op | source)
XLA Modules:
  0.0 67.6 jit_solution(15410616773291098471)
XLA Ops:
  0.0 0.0 copy-start.1
  0.0 0.8 %copy-done.1 = bf16[64,1,2,128]{3,2,1,0:T(2,128)(2,1)S(1)} copy-done((bf16[64,1,2,128]{3,2,1,0:T(2,128)(2,1)S(1)}, bf16[64,1,2,128]{3,2,1,0:T(2,128)(2,1)}, u32[]{:S(2)}) %copy-start.1) | copy-done | bytes 32792
  0.8 0.7 %shard_map.65 = bf16[8,64,256]{2,1,0:T(8,128)(2,1)} custom-call(bf16[128,128]{1,0:T(8,128)(2,1)S(1)} %bitcast.11), custom_call_target="tpu_custom_call" | custom-call | tf_op jit(solution)/shard_map/pallas_call | solution.py:348
  1.5 6.5 %all-to-all-start.3 = ((bf16[8,64,256]{2,1,0:T(8,128)(2,1)}), bf16[8,64,256]{2,1,0:T(8,128)(2,1)S(1)}, u32[]{:S(2)}, u32[]{:S(2)}) async-start(bf16[8,64,256]{2,1,0:T(8,128)(2,1)} %shard_map.65), calls=%async_computation.3 | async-start | bytes 524288 | tf_op jit(solution)/shard_map/all_to_all | solution.py:356
  8.0 2.0 %collective-permute-start = (bf16[256,128]{1,0:T(8,128)(2,1)}, bf16[256,128]{1,0:T(8,128)(2,1)S(1)}, u32[]{:S(2)}, u32[]{:S(2)}) collective-permute-start(bf16[256,128]{1,0:T(8,128)(2,1)} %bitcast.9), channel_id=1, source_target_pairs={{0,64},{64,128},{128,192},{192,256},{256,320},{320,384},{384,448},... | collective-permute-start | bytes 196616 | tf_op jit(solution)/shard_map/ppermute | solution.py:357
  10.1 0.0 copy-start
  10.1 0.8 %copy-done = bf16[128,1,2,128]{3,2,1,0:T(2,128)(2,1)S(1)} copy-done((bf16[128,1,2,128]{3,2,1,0:T(2,128)(2,1)S(1)}, bf16[128,1,2,128]{3,2,1,0:T(2,128)(2,1)}, u32[]{:S(2)}) %copy-start) | copy-done | bytes 65560
  10.9 0.0 copy-start.2
  10.9 0.8 %copy-done.2 = s32[8192]{0:T(1024)S(1)} copy-done((s32[8192]{0:T(1024)S(1)}, s32[8192]{0:T(1024)}, u32[]{:S(2)}) %copy-start.2) | copy-done | bytes 32792
  11.7 0.0 copy-start.3
  11.7 0.7 %copy-done.3 = s32[4096]{0:T(1024)S(1)} copy-done((s32[4096]{0:T(1024)S(1)}, s32[4096]{0:T(1024)}, u32[]{:S(2)}) %copy-start.3) | copy-done | bytes 16408
  12.4 0.0 copy-start.4
  12.4 0.7 copy-done.4
  13.1 1.6 %shard_map.64 = (bf16[128,256]{1,0:T(8,128)(2,1)S(1)}, s32[110]{0:T(128)S(1)}, s32[1]{0:T(128)}) custom-call(s32[1]{0:T(128)} %bitcast.place_ref, s32[64]{0:T(128)S(1)} %copy-done.4, bf16[256,128]{1,0:T(8,128)(2,1)S(1)} %bitcast.10, s32[64,128]{1,0:T(8,128)S(1)} %bitcast.12, s32[32,128]{1,0:T(8,128)S(1)} %bitcast.13), custom_call_target="tpu_custom_call" | custom-call | tf_op jit(solution)/shard_map/pallas_call | solution.py:358
  15.3 0.0 collective-permute-done
  15.3 2.9 %all-to-all-done.3 = bf16[8,64,256]{2,1,0:T(8,128)(2,1)S(1)} async-done(((bf16[8,64,256]{2,1,0:T(8,128)(2,1)}), bf16[8,64,256]{2,1,0:T(8,128)(2,1)S(1)}, u32[]{:S(2)}, u32[]{:S(2)}) %all-to-all-start.3) | async-done | bytes 262176 | tf_op jit(solution)/shard_map/all_to_all | solution.py:356
  18.3 26.0 %conditional.1 = (bf16[128,1024]{1,0:T(8,128)(2,1)S(1)}) conditional(s32[]{:T(128)} %bitcast.4, (s32[110]{0:T(128)S(1)}, bf16[8,64,256]{2,1,0:T(8,128)(2,1)S(1)}, bf16[128,256]{1,0:T(8,128)(2,1)S(1)}, bf16[256,128]{1,0:T(8,128)(2,1)S(1)}, bf16[128,1024]{1,0:T(8,128)(2,1)}) %tuple.18, (s32[110]{0:T(128)S(1)}, ...), branch_computations={%region_0.0_spmd, %region_1.0_spmd, %region_2.0_spmd} | conditional | bytes 6291492 | solution.py:409
  18.3 0.0 copy-start.5
  18.3 0.8 %branch_0_fun.2 = (bf16[8,256,256]{2,1,0:T(8,128)(2,1)S(1)}, bf16[128,256]{1,0:T(8,128)(2,1)S(1)}) custom-call(s32[110]{0:T(128)S(1)} %get-tuple-element.38.table_ref, bf16[8,64,256]{2,1,0:T(8,128)(2,1)S(1)} %get-tuple-element.41.shards_ref, bf16[128,256]{1,0:T(8,128)(2,1)S(1)} %get-tuple-element.42.own_ref, bf16[256,128]{1,0:T(8,128)(2,1)S(1)} %get-tuple-element.43.raw_ref), custom_call_target="tpu_custom_call" | custom-call | tf_op jit(solution)/shard_map/cond/branch_0_fun/pallas_call | solution.py:374
  19.1 21.0 %all_to_all.22.arrived_ref = bf16[8,256,256]{2,1,0:T(8,128)(2,1)S(1)} all-to-all(bf16[8,256,256]{2,1,0:T(8,128)(2,1)S(1)} %get-tuple-element.44), channel_id=1, replica_groups=mesh['cp'=8,'blk'=8,'head'=8] {'blk'}, dimensions={0} | all-to-all | bytes 2097152 | tf_op jit(solution)/shard_map/cond/branch_0_fun/all_to_all | solution.py:385
  40.1 0.0 copy-done.5
  40.1 4.2 %branch_0_fun.3 = bf16[128,1024]{1,0:T(8,128)(2,1)S(1)} custom-call(s32[110]{0:T(128)S(1)} %get-tuple-element.38.table_ref, bf16[128,1024]{1,0:T(8,128)(2,1)S(1)} %copy-done.5, bf16[8,256,256]{2,1,0:T(8,128)(2,1)S(1)} %all_to_all.22.arrived_ref, bf16[128,256]{1,0:T(8,128)(2,1)S(1)} %get-tuple-element.45.behind_ref), custom_call_target="tpu_custom_call" | custom-call | tf_op jit(solution)/shard_map/cond/branch_0_fun/pallas_call | solution.py:388
  44.3 22.4 %all_to_all.25 = bf16[8,16,1024]{2,1,0:T(8,128)(2,1)S(1)} all-to-all(bf16[8,16,1024]{2,1,0:T(8,128)(2,1)S(1)} %bitcast.18), channel_id=1, replica_groups=mesh['cp'=8,'blk'=8,'head'=8] {'head'}, dimensions={0} | all-to-all | bytes 524288 | tf_op jit(solution)/shard_map/all_to_all | solution.py:419
  66.7 0.9 %copy.7 = bf16[16,8,1024]{2,1,0:T(8,128)(2,1)} copy(bf16[16,8,1024]{2,0,1:T(8,128)(2,1)S(1)} %bitcast.17) | data formatting | bytes 524288 | tf_op jit(solution)/shard_map/transpose | solution.py:422
Async XLA Ops:
  0.0 0.8 %copy-start.1 = (bf16[64,1,2,128]{3,2,1,0:T(2,128)(2,1)S(1)}, bf16[64,1,2,128]{3,2,1,0:T(2,128)(2,1)}, u32[]{:S(2)}) copy-start(bf16[64,1,2,128]{3,2,1,0:T(2,128)(2,1)} %param.11) | copy-start | bytes 98308
  1.5 16.8 %all-to-all-start.3 = ((bf16[8,64,256]{2,1,0:T(8,128)(2,1)}), bf16[8,64,256]{2,1,0:T(8,128)(2,1)S(1)}, u32[]{:S(2)}, u32[]{:S(2)}) async-start(bf16[8,64,256]{2,1,0:T(8,128)(2,1)} %shard_map.65), calls=%async_computation.3 | async-start | bytes 524288 | tf_op jit(solution)/shard_map/all_to_all | solution.py:356
  8.0 7.3 %collective-permute-start = (bf16[256,128]{1,0:T(8,128)(2,1)}, bf16[256,128]{1,0:T(8,128)(2,1)S(1)}, u32[]{:S(2)}, u32[]{:S(2)}) collective-permute-start(bf16[256,128]{1,0:T(8,128)(2,1)} %bitcast.9), channel_id=1, source_target_pairs={{0,64},{64,128},{128,192},{192,256},{256,320},{320,384},{384,448},... | collective-permute-start | bytes 196616 | tf_op jit(solution)/shard_map/ppermute | solution.py:357
  10.1 0.8 %copy-start = (bf16[128,1,2,128]{3,2,1,0:T(2,128)(2,1)S(1)}, bf16[128,1,2,128]{3,2,1,0:T(2,128)(2,1)}, u32[]{:S(2)}) copy-start(bf16[128,1,2,128]{3,2,1,0:T(2,128)(2,1)} %param.10) | copy-start | bytes 196612
  10.9 0.8 %copy-start.2 = (s32[8192]{0:T(1024)S(1)}, s32[8192]{0:T(1024)}, u32[]{:S(2)}) copy-start(s32[8192]{0:T(1024)} %param.12) | copy-start | bytes 98308
  11.7 0.7 %copy-start.3 = (s32[4096]{0:T(1024)S(1)}, s32[4096]{0:T(1024)}, u32[]{:S(2)}) copy-start(s32[4096]{0:T(1024)} %param.13) | copy-start | bytes 49156
  12.4 0.7 copy-start.4
  18.3 21.8 %copy-start.5 = (bf16[128,1024]{1,0:T(8,128)(2,1)S(1)}, bf16[128,1024]{1,0:T(8,128)(2,1)}, u32[]{:S(2)}) copy-start(bf16[128,1024]{1,0:T(8,128)(2,1)} %get-tuple-element.40.queries_ref) | copy-start | bytes 786436 | tf_op jit(solution)/shard_map/cond
